TPU v7x, 32 devices: a whole 2x2x4 slice. The times are simulated.
32 devices in a mesh: mode: 8 (over z, y), tile: 4 (over x, core).
Axes of the slice: x: 2, y: 2, z: 4, core: 2. Of those that a mesh axis runs over, the one named last changes fastest.
Arguments:
- magnetic: float32 [32, 6, 32, 512], P('mode', None, None, 'tile'), may hold values from -6 to 6
- velocity_stack: float32 [8, 9, 32, 512], P('mode', None, None, 'tile'), may hold values from -6 to 6
- wavenumber: int32 [32], P('mode'), may hold values from -16 to 15, as said below
- velocity_owner: int32 [1], replicated, may hold values from 0 to 7
Outputs:
- evolved: float32 [32, 6, 32, 512], P('mode', None, None, 'tile')
Inputs may be any that keep to these rules, and one draw needn't show every extreme that they name: Slot k holds wavenumber ((k + s) mod 32) - 16 for one whole number s of the draw.
All inputs are finite; a program needn't handle non-finite values.
Results may differ from a plain program's by a relative error of at most 0.0003.
Values sent between devices are 32-bit elements; how exact they have to be, the bound alone decides.
No kernel may reach another device: no remote copies, remote signals or barrier semaphores. Data moves between devices by JAX's collectives and lax.ppermute only.
A program may use at most 64 MiB of HBM per device.

v0:
```python
import jax
import jax.numpy as jnp
from jax import lax
from jax.sharding import PartitionSpec as P

STEPS = 2


diffusivity = 0.5
time_step = 0.2
inner_radius = 32.0


def with_halo(cells, sides, width, closed):
    for axis, dim in sides:
        count = lax.axis_size(axis)
        ends = count if closed else count - 1
        head = lax.slice_in_dim(cells, 0, width, axis=dim)
        tail = lax.slice_in_dim(cells, cells.shape[dim] - width, cells.shape[dim], axis=dim)
        cells = jnp.concatenate(
            [
                lax.ppermute(tail, axis, [(i, (i + 1) % count) for i in range(ends)]),
                cells,
                lax.ppermute(head, axis, [((i + 1) % count, i) for i in range(ends)]),
            ],
            axis=dim,
        )
    return cells


def from_root(x, axis, root):
    mine = lax.axis_index(axis) == root
    return lax.psum(jnp.where(mine, x, jnp.zeros_like(x)), axis)


def complex_product(left_pair, right_pair):
    return (
        left_pair[0] * right_pair[0] - left_pair[1] * right_pair[1],
        left_pair[0] * right_pair[1] + left_pair[1] * right_pair[0],
    )


def subtract_pair(left_pair, right_pair):
    return (left_pair[0] - right_pair[0], left_pair[1] - right_pair[1])


def components(values):
    return [
        (values[..., 2 * component, :, :], values[..., 2 * component + 1, :, :])
        for component in range(3)
    ]


def cross_product(left_vec, right_vec):
    radial_out = subtract_pair(
        complex_product(left_vec[1], right_vec[2]), complex_product(left_vec[2], right_vec[1])
    )
    azimuth_out = subtract_pair(
        complex_product(left_vec[2], right_vec[0]), complex_product(left_vec[0], right_vec[2])
    )
    axial_out = subtract_pair(
        complex_product(left_vec[0], right_vec[1]), complex_product(left_vec[1], right_vec[0])
    )
    return [radial_out, azimuth_out, axial_out]


def electromotive(velocity, lower_mode, centre, upper_mode):
    nothing = jnp.zeros_like(velocity[0])
    steady = [(velocity[0], nothing), (velocity[1], nothing), (velocity[2], nothing)]
    swirling = [(velocity[3], velocity[4]), (velocity[5], velocity[6]), (velocity[7], velocity[8])]
    mirror = [(pair[0], -pair[1]) for pair in swirling]
    first = cross_product(steady, components(centre))
    second = cross_product(swirling, components(lower_mode))
    third = cross_product(mirror, components(upper_mode))
    pieces = []
    for component in range(3):
        for part_index in range(2):
            pieces.append(
                first[component][part_index]
                + second[component][part_index]
                + third[component][part_index]
            )
    return jnp.stack(pieces, axis=-3)


def interior(values):
    return values[..., 1:-1]


def pad_axial(values):
    return jnp.pad(values, [(0, 0)] * (values.ndim - 2) + [(1, 1), (0, 0)])


def along_axial(values):
    padded = pad_axial(values)
    return 0.5 * (padded[..., 2:, :] - padded[..., :-2, :])


def along_radial(values):
    return 0.5 * (values[..., 2:] - values[..., :-2])


def laplace(values, radius):
    centre = interior(values)
    padded = pad_axial(centre)
    return (
        values[..., 2:]
        + values[..., :-2]
        + padded[..., 2:, :]
        + padded[..., :-2, :]
        - 4.0 * centre
        + along_radial(values) / radius
    )


def radial_flux(values, radius):
    return 0.5 * ((radius + 1.0) * values[..., 2:] - (radius - 1.0) * values[..., :-2]) / radius


def rates(wide_field, wide_emf, waves, radius):
    field_r, field_p, field_z = components(wide_field)
    emf_r, emf_p, emf_z = components(wide_emf)
    wave_over = waves / radius
    decay_rate = (waves * waves + 1.0) / (radius * radius)
    coupling = 2.0 * waves / (radius * radius)
    axial_decay = waves * waves / (radius * radius)
    r_real = (
        -wave_over * interior(emf_z[1])
        - along_axial(interior(emf_p[0]))
        + diffusivity
        * (
            laplace(field_r[0], radius)
            - decay_rate * interior(field_r[0])
            + coupling * interior(field_p[1])
        )
    )
    r_imag = (
        wave_over * interior(emf_z[0])
        - along_axial(interior(emf_p[1]))
        + diffusivity
        * (
            laplace(field_r[1], radius)
            - decay_rate * interior(field_r[1])
            - coupling * interior(field_p[0])
        )
    )
    p_real = (
        along_axial(interior(emf_r[0]))
        - along_radial(emf_z[0])
        + diffusivity
        * (
            laplace(field_p[0], radius)
            - decay_rate * interior(field_p[0])
            - coupling * interior(field_r[1])
        )
    )
    p_imag = (
        along_axial(interior(emf_r[1]))
        - along_radial(emf_z[1])
        + diffusivity
        * (
            laplace(field_p[1], radius)
            - decay_rate * interior(field_p[1])
            + coupling * interior(field_r[0])
        )
    )
    z_real = (
        radial_flux(emf_p[0], radius)
        + wave_over * interior(emf_r[1])
        + diffusivity * (laplace(field_z[0], radius) - axial_decay * interior(field_z[0]))
    )
    z_imag = (
        radial_flux(emf_p[1], radius)
        - wave_over * interior(emf_r[0])
        + diffusivity * (laplace(field_z[1], radius) - axial_decay * interior(field_z[1]))
    )
    return jnp.stack([r_real, r_imag, p_real, p_imag, z_real, z_imag], axis=-3)


def mode_rim(state):
    return with_halo(state, (("mode", 0),), 1, True)


def body(magnetic, velocity_stack, wavenumber, velocity_owner):
    columns = magnetic.shape[3]
    velocity = from_root(velocity_stack[0], "mode", velocity_owner[0])
    start = lax.axis_index("tile") * columns
    radius = inner_radius + (start + jnp.arange(columns, dtype=jnp.int32)).astype(jnp.float32) + 0.5
    waves = wavenumber.astype(jnp.float32)[:, None, None]
    state = magnetic

    def evaluate(current):
        shifted = mode_rim(current)
        emf = electromotive(velocity, shifted[:-2], shifted[1:-1], shifted[2:])
        stacked = with_halo(jnp.concatenate([emf, current], axis=1), (("tile", 3),), 1, False)
        return rates(stacked[:, 6:], stacked[:, :6], waves, radius)

    for step_index in range(STEPS):
        first = evaluate(state)
        trial = state + time_step * first
        second = evaluate(trial)
        state = state + 0.5 * time_step * (first + second)
    return state


def solution(mesh):
    placed = (P("mode", None, None, "tile"), P("mode", None, None, "tile"), P("mode"), P())
    return jax.shard_map(
        body, mesh=mesh, in_specs=placed, out_specs=P("mode", None, None, "tile"), check_vma=False
    )
```

profile of v0, /device:TPU:0, one launch (start us, length us, event | category | flops | bytes accessed | tf_op | source)
XLA Modules:
  0.0 162.7 jit_solution(8661590595684947659)
XLA Ops:
  7.2 0.7 select_bitcast_fusion
  8.0 1.0 fusion.304
  8.9 3.0 %collective-permute-start = (f32[1,6,32,128]{3,2,1,0:T(8,128)S(1)}, f32[1,6,32,128]{3,2,1,0:T(8,128)S(1)}, u32[]{:S(2)}, u32[]{:S(2)}) collective-permute-start(f32[1,6,32,128]{3,2,1,0:T(8,128)S(1)} %get-tuple-element.111), channel_id=1, source_target_pairs={{0,4},{4,8},{8,12},{12,16},{16,20},{20,24},{24,28},{28,0},{1,5},{5... | collective-permute-start | bytes 294920 | tf_op jit(solution)/shard_map/ppermute | solution.py:22
  11.9 3.1 %collective-permute-start.1 = (f32[1,6,32,128]{3,2,1,0:T(8,128)S(1)}, f32[1,6,32,128]{3,2,1,0:T(8,128)S(1)}, u32[]{:S(2)}, u32[]{:S(2)}) collective-permute-start(f32[1,6,32,128]{3,2,1,0:T(8,128)S(1)} %get-tuple-element.112), channel_id=1, source_target_pairs={{4,0},{8,4},{12,8},{16,12},{20,16},{24,20},{28,24},{0,28},{5,1},{9... | collective-permute-start | bytes 294920 | tf_op jit(solution)/shard_map/ppermute | solution.py:24
  15.0 0.7 convert_element_type.60
  15.7 0.7 convert_multiply_fusion
  16.5 1.4 collective-permute-done
  17.9 1.1 constant_dynamic-update-slice_fusion
  19.0 64.3 %all-reduce.42.cloned.1.call-done = f32[9,32,128]{2,1,0:T(8,128)} async-done(((f32[9,32,128]{2,1,0:T(8,128)}), f32[9,32,128]{2,1,0:T(8,128)}) %all-reduce.42.cloned.1.call-update) | async-done | bytes 147472 | tf_op jit(solution)/shard_map/psum | solution.py:33
  83.3 0.9 slice_bitcast_fusion.49
  84.8 0.3 fusion.300
  85.1 0.4 copy.229
  85.5 0.4 copy.230
  85.8 1.3 collective-permute-start.3
  87.1 3.0 %collective-permute-start.2 = (f32[4,12,32,1]{2,0,3,1:T(4,128)S(1)}, f32[4,12,32,1]{2,0,3,1:T(4,128)S(1)}, u32[]{:S(2)}, u32[]{:S(2)}) collective-permute-start(f32[4,12,32,1]{2,0,3,1:T(4,128)S(1)} %copy.229), channel_id=1, source_target_pairs={{0,1},{1,2},{2,3},{4,5},{5,6},{6,7},{8,9},{9,10},{10,11},{12,13},{... | collective-permute-start | bytes 18440 | tf_op jit(solution)/shard_map/ppermute | solution.py:22
  90.2 0.8 collective-permute-done.2
  91.0 0.4 copy.177
  91.4 0.4 copy.178
  91.7 0.7 pad_maximum_fusion
  93.4 0.1 constant_dynamic-update-slice_fusion.16
  93.6 0.1 constant_dynamic-update-slice_fusion.14
  93.8 0.1 constant_dynamic-update-slice_fusion.13
  94.3 2.4 %collective-permute-start.5 = (f32[1,6,32,128]{3,2,1,0:T(8,128)S(1)}, f32[1,6,32,128]{3,2,1,0:T(8,128)S(1)}, u32[]{:S(2)}, u32[]{:S(2)}) collective-permute-start(f32[1,6,32,128]{3,2,1,0:T(8,128)S(1)} %get-tuple-element.107), channel_id=1, source_target_pairs={{4,0},{8,4},{12,8},{16,12},{20,16},{24,20},{28,24},{0,28},{5,1},{9... | collective-permute-start | bytes 294920 | tf_op jit(solution)/shard_map/ppermute | solution.py:24
  96.7 3.1 %collective-permute-done.5 = f32[1,6,32,128]{3,2,1,0:T(8,128)S(1)} collective-permute-done((f32[1,6,32,128]{3,2,1,0:T(8,128)S(1)}, f32[1,6,32,128]{3,2,1,0:T(8,128)S(1)}, u32[]{:S(2)}, u32[]{:S(2)}) %collective-permute-start.5) | collective-permute-done | bytes 98336 | tf_op jit(solution)/shard_map/ppermute | solution.py:24
  99.8 5.2 %collective-permute-done.4 = f32[1,6,32,128]{3,2,1,0:T(8,128)S(1)} collective-permute-done((f32[1,6,32,128]{3,2,1,0:T(8,128)S(1)}, f32[1,6,32,128]{3,2,1,0:T(8,128)S(1)}, u32[]{:S(2)}, u32[]{:S(2)}) %collective-permute-start.4) | collective-permute-done | bytes 98336 | tf_op jit(solution)/shard_map/ppermute | solution.py:22
  105.6 0.3 fusion.299
  105.9 0.4 copy.242
  106.3 1.9 %collective-permute-start.6 = (f32[4,12,32,1]{2,0,3,1:T(4,128)S(1)}, f32[4,12,32,1]{2,0,3,1:T(4,128)S(1)}, u32[]{:S(2)}, u32[]{:S(2)}) collective-permute-start(f32[4,12,32,1]{2,0,3,1:T(4,128)S(1)} %copy.242), channel_id=1, source_target_pairs={{0,1},{1,2},{2,3},{4,5},{5,6},{6,7},{8,9},{9,10},{10,11},{12,13},{... | collective-permute-start | bytes 18440 | tf_op jit(solution)/shard_map/ppermute | solution.py:22
  108.2 0.3 copy.243
  108.6 1.3 collective-permute-start.7
  109.9 0.4 copy.198
  110.2 3.4 %collective-permute-done.7 = f32[4,12,32,1]{2,0,3,1:T(4,128)S(1)} collective-permute-done((f32[4,12,32,1]{2,0,3,1:T(4,128)S(1)}, f32[4,12,32,1]{2,0,3,1:T(4,128)S(1)}, u32[]{:S(2)}, u32[]{:S(2)}) %collective-permute-start.7) | collective-permute-done | bytes 6176 | tf_op jit(solution)/shard_map/ppermute | solution.py:24
  113.6 0.4 copy.200
  114.0 0.7 pad_maximum_fusion.1
  115.6 0.1 constant_dynamic-update-slice_fusion.29
  115.9 0.1 constant_dynamic-update-slice_fusion.27
  116.1 0.1 constant_dynamic-update-slice_fusion.26
  116.6 2.0 %collective-permute-start.8 = (f32[1,6,32,128]{3,2,1,0:T(8,128)S(1)}, f32[1,6,32,128]{3,2,1,0:T(8,128)S(1)}, u32[]{:S(2)}, u32[]{:S(2)}) collective-permute-start(f32[1,6,32,128]{3,2,1,0:T(8,128)S(1)} %get-tuple-element.106), channel_id=1, source_target_pairs={{0,4},{4,8},{8,12},{12,16},{16,20},{20,24},{24,28},{28,0},{1,5},{5... | collective-permute-start | bytes 294920 | tf_op jit(solution)/shard_map/ppermute | solution.py:22
  118.7 2.6 %collective-permute-done.9 = f32[1,6,32,128]{3,2,1,0:T(8,128)S(1)} collective-permute-done((f32[1,6,32,128]{3,2,1,0:T(8,128)S(1)}, f32[1,6,32,128]{3,2,1,0:T(8,128)S(1)}, u32[]{:S(2)}, u32[]{:S(2)}) %collective-permute-start.9) | collective-permute-done | bytes 98336 | tf_op jit(solution)/shard_map/ppermute | solution.py:24
  121.3 2.8 %collective-permute-done.8 = f32[1,6,32,128]{3,2,1,0:T(8,128)S(1)} collective-permute-done((f32[1,6,32,128]{3,2,1,0:T(8,128)S(1)}, f32[1,6,32,128]{3,2,1,0:T(8,128)S(1)}, u32[]{:S(2)}, u32[]{:S(2)}) %collective-permute-start.8) | collective-permute-done | bytes 98336 | tf_op jit(solution)/shard_map/ppermute | solution.py:22
  124.6 0.3 fusion.298
  124.9 0.4 copy.244
  125.3 3.3 %collective-permute-start.10 = (f32[4,12,32,1]{2,0,3,1:T(4,128)S(1)}, f32[4,12,32,1]{2,0,3,1:T(4,128)S(1)}, u32[]{:S(2)}, u32[]{:S(2)}) collective-permute-start(f32[4,12,32,1]{2,0,3,1:T(4,128)S(1)} %copy.244), channel_id=1, source_target_pairs={{0,1},{1,2},{2,3},{4,5},{5,6},{6,7},{8,9},{9,10},{10,11},{12,13},{... | collective-permute-start | bytes 18440 | tf_op jit(solution)/shard_map/ppermute | solution.py:22
  128.6 0.3 copy.245
  129.0 1.3 collective-permute-start.11
  130.3 0.4 copy.209
  130.6 2.1 %collective-permute-done.11 = f32[4,12,32,1]{2,0,3,1:T(4,128)S(1)} collective-permute-done((f32[4,12,32,1]{2,0,3,1:T(4,128)S(1)}, f32[4,12,32,1]{2,0,3,1:T(4,128)S(1)}, u32[]{:S(2)}, u32[]{:S(2)}) %collective-permute-start.11) | collective-permute-done | bytes 6176 | tf_op jit(solution)/shard_map/ppermute | solution.py:24
  132.7 0.4 copy.211
  133.1 0.7 pad_maximum_fusion.2
  134.7 0.1 constant_dynamic-update-slice_fusion.42
  135.7 2.0 %collective-permute-start.12 = (f32[1,6,32,128]{3,2,1,0:T(8,128)S(1)}, f32[1,6,32,128]{3,2,1,0:T(8,128)S(1)}, u32[]{:S(2)}, u32[]{:S(2)}) collective-permute-start(f32[1,6,32,128]{3,2,1,0:T(8,128)S(1)} %get-tuple-element.104), channel_id=1, source_target_pairs={{0,4},{4,8},{8,12},{12,16},{16,20},{20,24},{24,28},{28,0},{1,5},{5... | collective-permute-start | bytes 294920 | tf_op jit(solution)/shard_map/ppermute | solution.py:22
  137.7 2.6 %collective-permute-done.13 = f32[1,6,32,128]{3,2,1,0:T(8,128)S(1)} collective-permute-done((f32[1,6,32,128]{3,2,1,0:T(8,128)S(1)}, f32[1,6,32,128]{3,2,1,0:T(8,128)S(1)}, u32[]{:S(2)}, u32[]{:S(2)}) %collective-permute-start.13) | collective-permute-done | bytes 98336 | tf_op jit(solution)/shard_map/ppermute | solution.py:24
  140.3 2.9 %collective-permute-done.12 = f32[1,6,32,128]{3,2,1,0:T(8,128)S(1)} collective-permute-done((f32[1,6,32,128]{3,2,1,0:T(8,128)S(1)}, f32[1,6,32,128]{3,2,1,0:T(8,128)S(1)}, u32[]{:S(2)}, u32[]{:S(2)}) %collective-permute-start.12) | collective-permute-done | bytes 98336 | tf_op jit(solution)/shard_map/ppermute | solution.py:22
  143.9 0.3 fusion.297
  144.2 0.4 copy.246
  144.6 3.3 %collective-permute-start.14 = (f32[4,12,32,1]{2,1,3,0:T(8,128)S(1)}, f32[4,12,32,1]{2,1,3,0:T(8,128)S(1)}, u32[]{:S(2)}, u32[]{:S(2)}) collective-permute-start(f32[4,12,32,1]{2,1,3,0:T(8,128)S(1)} %copy.246), channel_id=1, source_target_pairs={{0,1},{1,2},{2,3},{4,5},{5,6},{6,7},{8,9},{9,10},{10,11},{12,13},{... | collective-permute-start | bytes 18440 | tf_op jit(solution)/shard_map/ppermute | solution.py:22
  147.9 0.4 copy.247
  148.4 1.3 collective-permute-start.15
  149.7 0.4 copy.220
  150.1 2.1 %collective-permute-done.15 = f32[4,12,32,1]{2,1,3,0:T(8,128)S(1)} collective-permute-done((f32[4,12,32,1]{2,1,3,0:T(8,128)S(1)}, f32[4,12,32,1]{2,1,3,0:T(8,128)S(1)}, u32[]{:S(2)}, u32[]{:S(2)}) %collective-permute-start.15) | collective-permute-done | bytes 6176 | tf_op jit(solution)/shard_map/ppermute | solution.py:24
  152.2 0.4 copy.222
  152.5 0.7 pad_maximum_fusion.3
  154.2 0.1 constant_dynamic-update-slice_fusion.55
  155.0 0.8 multiply_add_fusion
  (116 shorter events, 8.8 us)
Async XLA Ops:
  6.5 77.6 %copy-start = (f32[4,6,32,128]{3,2,1,0:T(8,128)S(1)}, f32[4,6,32,128]{3,2,1,0:T(8,128)}, u32[]{:S(2)}) copy-start(f32[4,6,32,128]{3,2,1,0:T(8,128)} %param.4) | copy-start | bytes 1179652
  6.5 76.8 %all-reduce.42.cloned.1.call-start = ((), (), s32[]{:S(2)}) async-start(), calls=%async_computation | async-start | bytes 294912 | tf_op jit(solution)/shard_map/psum | solution.py:33
  8.9 9.0 %collective-permute-start = (f32[1,6,32,128]{3,2,1,0:T(8,128)S(1)}, f32[1,6,32,128]{3,2,1,0:T(8,128)S(1)}, u32[]{:S(2)}, u32[]{:S(2)}) collective-permute-start(f32[1,6,32,128]{3,2,1,0:T(8,128)S(1)} %get-tuple-element.111), channel_id=1, source_target_pairs={{0,4},{4,8},{8,12},{12,16},{16,20},{20,24},{24,28},{28,0},{1,5},{5... | collective-permute-start | bytes 294920 | tf_op jit(solution)/shard_map/ppermute | solution.py:22
  11.9 7.1 %collective-permute-start.1 = (f32[1,6,32,128]{3,2,1,0:T(8,128)S(1)}, f32[1,6,32,128]{3,2,1,0:T(8,128)S(1)}, u32[]{:S(2)}, u32[]{:S(2)}) collective-permute-start(f32[1,6,32,128]{3,2,1,0:T(8,128)S(1)} %get-tuple-element.112), channel_id=1, source_target_pairs={{4,0},{8,4},{12,8},{16,12},{20,16},{24,20},{28,24},{0,28},{5,1},{9... | collective-permute-start | bytes 294920 | tf_op jit(solution)/shard_map/ppermute | solution.py:24
  85.8 5.5 %collective-permute-start.3 = (f32[4,12,32,1]{2,0,3,1:T(4,128)S(1)}, f32[4,12,32,1]{2,0,3,1:T(4,128)S(1)}, u32[]{:S(2)}, u32[]{:S(2)}) collective-permute-start(f32[4,12,32,1]{2,0,3,1:T(4,128)S(1)} %copy.230), channel_id=1, source_target_pairs={{1,0},{2,1},{3,2},{5,4},{6,5},{7,6},{9,8},{10,9},{11,10},{13,12},{... | collective-permute-start | bytes 18440 | tf_op jit(solution)/shard_map/ppermute | solution.py:24
  87.1 3.9 %collective-permute-start.2 = (f32[4,12,32,1]{2,0,3,1:T(4,128)S(1)}, f32[4,12,32,1]{2,0,3,1:T(4,128)S(1)}, u32[]{:S(2)}, u32[]{:S(2)}) collective-permute-start(f32[4,12,32,1]{2,0,3,1:T(4,128)S(1)} %copy.229), channel_id=1, source_target_pairs={{0,1},{1,2},{2,3},{4,5},{5,6},{6,7},{8,9},{9,10},{10,11},{12,13},{... | collective-permute-start | bytes 18440 | tf_op jit(solution)/shard_map/ppermute | solution.py:22
  94.3 5.5 %collective-permute-start.5 = (f32[1,6,32,128]{3,2,1,0:T(8,128)S(1)}, f32[1,6,32,128]{3,2,1,0:T(8,128)S(1)}, u32[]{:S(2)}, u32[]{:S(2)}) collective-permute-start(f32[1,6,32,128]{3,2,1,0:T(8,128)S(1)} %get-tuple-element.107), channel_id=1, source_target_pairs={{4,0},{8,4},{12,8},{16,12},{20,16},{24,20},{28,24},{0,28},{5,1},{9... | collective-permute-start | bytes 294920 | tf_op jit(solution)/shard_map/ppermute | solution.py:24
  96.7 8.3 %collective-permute-start.4 = (f32[1,6,32,128]{3,2,1,0:T(8,128)S(1)}, f32[1,6,32,128]{3,2,1,0:T(8,128)S(1)}, u32[]{:S(2)}, u32[]{:S(2)}) collective-permute-start(f32[1,6,32,128]{3,2,1,0:T(8,128)S(1)} %get-tuple-element.108), channel_id=1, source_target_pairs={{0,4},{4,8},{8,12},{12,16},{16,20},{20,24},{24,28},{28,0},{1,5},{5... | collective-permute-start | bytes 294920 | tf_op jit(solution)/shard_map/ppermute | solution.py:22
  106.3 3.6 %collective-permute-start.6 = (f32[4,12,32,1]{2,0,3,1:T(4,128)S(1)}, f32[4,12,32,1]{2,0,3,1:T(4,128)S(1)}, u32[]{:S(2)}, u32[]{:S(2)}) collective-permute-start(f32[4,12,32,1]{2,0,3,1:T(4,128)S(1)} %copy.242), channel_id=1, source_target_pairs={{0,1},{1,2},{2,3},{4,5},{5,6},{6,7},{8,9},{9,10},{10,11},{12,13},{... | collective-permute-start | bytes 18440 | tf_op jit(solution)/shard_map/ppermute | solution.py:22
  108.6 5.1 %collective-permute-start.7 = (f32[4,12,32,1]{2,0,3,1:T(4,128)S(1)}, f32[4,12,32,1]{2,0,3,1:T(4,128)S(1)}, u32[]{:S(2)}, u32[]{:S(2)}) collective-permute-start(f32[4,12,32,1]{2,0,3,1:T(4,128)S(1)} %copy.243), channel_id=1, source_target_pairs={{1,0},{2,1},{3,2},{5,4},{6,5},{7,6},{9,8},{10,9},{11,10},{13,12},{... | collective-permute-start | bytes 18440 | tf_op jit(solution)/shard_map/ppermute | solution.py:24
  116.6 4.7 %collective-permute-start.9 = (f32[1,6,32,128]{3,2,1,0:T(8,128)S(1)}, f32[1,6,32,128]{3,2,1,0:T(8,128)S(1)}, u32[]{:S(2)}, u32[]{:S(2)}) collective-permute-start(f32[1,6,32,128]{3,2,1,0:T(8,128)S(1)} %get-tuple-element.105), channel_id=1, source_target_pairs={{4,0},{8,4},{12,8},{16,12},{20,16},{24,20},{28,24},{0,28},{5,1},{9... | collective-permute-start | bytes 294920 | tf_op jit(solution)/shard_map/ppermute | solution.py:24
  116.6 7.4 %collective-permute-start.8 = (f32[1,6,32,128]{3,2,1,0:T(8,128)S(1)}, f32[1,6,32,128]{3,2,1,0:T(8,128)S(1)}, u32[]{:S(2)}, u32[]{:S(2)}) collective-permute-start(f32[1,6,32,128]{3,2,1,0:T(8,128)S(1)} %get-tuple-element.106), channel_id=1, source_target_pairs={{0,4},{4,8},{8,12},{12,16},{16,20},{20,24},{24,28},{28,0},{1,5},{5... | collective-permute-start | bytes 294920 | tf_op jit(solution)/shard_map/ppermute | solution.py:22
  125.3 5.0 %collective-permute-start.10 = (f32[4,12,32,1]{2,0,3,1:T(4,128)S(1)}, f32[4,12,32,1]{2,0,3,1:T(4,128)S(1)}, u32[]{:S(2)}, u32[]{:S(2)}) collective-permute-start(f32[4,12,32,1]{2,0,3,1:T(4,128)S(1)} %copy.244), channel_id=1, source_target_pairs={{0,1},{1,2},{2,3},{4,5},{5,6},{6,7},{8,9},{9,10},{10,11},{12,13},{... | collective-permute-start | bytes 18440 | tf_op jit(solution)/shard_map/ppermute | solution.py:22
  129.0 3.8 %collective-permute-start.11 = (f32[4,12,32,1]{2,0,3,1:T(4,128)S(1)}, f32[4,12,32,1]{2,0,3,1:T(4,128)S(1)}, u32[]{:S(2)}, u32[]{:S(2)}) collective-permute-start(f32[4,12,32,1]{2,0,3,1:T(4,128)S(1)} %copy.245), channel_id=1, source_target_pairs={{1,0},{2,1},{3,2},{5,4},{6,5},{7,6},{9,8},{10,9},{11,10},{13,12},{... | collective-permute-start | bytes 18440 | tf_op jit(solution)/shard_map/ppermute | solution.py:24
  135.5 4.8 %copy-start.1 = (f32[4,6,32,128]{3,2,1,0:T(8,128)}, f32[4,6,32,128]{3,2,1,0:T(8,128)S(1)}, u32[]{:S(2)}) copy-start(f32[4,6,32,128]{3,2,1,0:T(8,128)S(1)} %constant_dynamic-update-slice_fusion.37) | copy-start | bytes 1179652
  135.6 4.7 %collective-permute-start.13 = (f32[1,6,32,128]{3,2,1,0:T(8,128)S(1)}, f32[1,6,32,128]{3,2,1,0:T(8,128)S(1)}, u32[]{:S(2)}, u32[]{:S(2)}) collective-permute-start(f32[1,6,32,128]{3,2,1,0:T(8,128)S(1)} %get-tuple-element.103), channel_id=1, source_target_pairs={{4,0},{8,4},{12,8},{16,12},{20,16},{24,20},{28,24},{0,28},{5,1},{9... | collective-permute-start | bytes 294920 | tf_op jit(solution)/shard_map/ppermute | solution.py:24
  135.7 7.5 %collective-permute-start.12 = (f32[1,6,32,128]{3,2,1,0:T(8,128)S(1)}, f32[1,6,32,128]{3,2,1,0:T(8,128)S(1)}, u32[]{:S(2)}, u32[]{:S(2)}) collective-permute-start(f32[1,6,32,128]{3,2,1,0:T(8,128)S(1)} %get-tuple-element.104), channel_id=1, source_target_pairs={{0,4},{4,8},{8,12},{12,16},{16,20},{20,24},{24,28},{28,0},{1,5},{5... | collective-permute-start | bytes 294920 | tf_op jit(solution)/shard_map/ppermute | solution.py:22
  144.6 5.1 %collective-permute-start.14 = (f32[4,12,32,1]{2,1,3,0:T(8,128)S(1)}, f32[4,12,32,1]{2,1,3,0:T(8,128)S(1)}, u32[]{:S(2)}, u32[]{:S(2)}) collective-permute-start(f32[4,12,32,1]{2,1,3,0:T(8,128)S(1)} %copy.246), channel_id=1, source_target_pairs={{0,1},{1,2},{2,3},{4,5},{5,6},{6,7},{8,9},{9,10},{10,11},{12,13},{... | collective-permute-start | bytes 18440 | tf_op jit(solution)/shard_map/ppermute | solution.py:22
  148.4 3.8 %collective-permute-start.15 = (f32[4,12,32,1]{2,1,3,0:T(8,128)S(1)}, f32[4,12,32,1]{2,1,3,0:T(8,128)S(1)}, u32[]{:S(2)}, u32[]{:S(2)}) collective-permute-start(f32[4,12,32,1]{2,1,3,0:T(8,128)S(1)} %copy.247), channel_id=1, source_target_pairs={{1,0},{2,1},{3,2},{5,4},{6,5},{7,6},{9,8},{10,9},{11,10},{13,12},{... | collective-permute-start | bytes 18440 | tf_op jit(solution)/shard_map/ppermute | solution.py:24
  154.0 1.0 copy-start.2
Sparse Core Ops, SparseCore 0:
  10.7 72.5 all-reduce.41
where the time goes:
time: 165 us; the launch traced here: 163 us
  waiting for transfers between devices  93.2 us (56%)
  starting transfers between devices  29.5 us (18%)
  between operations  14.7 us (9%)
  local copies, waits for them, and re-layouts  13.2 us (8%)
  other arithmetic  12.1 us (7%)
    psum x1, waiting for transfers between devices, from_root(): return lax.psum(jnp.where(mine, x, jnp.zeros_like(x)), axis)  64.3 us
    ppermute x8, starting transfers between devices, with_halo(): lax.ppermute(tail, axis, [(i, (i + 1) % count) for i in range(ends)])  18.7 us
    ppermute x8, waiting for transfers between devices, with_halo(): lax.ppermute(head, axis, [((i + 1) % count, i) for i in range(ends)])  15.8 us
    ppermute x8, waiting for transfers between devices, with_halo(): lax.ppermute(tail, axis, [(i, (i + 1) % count) for i in range(ends)])  13.1 us
    ppermute x8, starting transfers between devices, with_halo(): lax.ppermute(head, axis, [((i + 1) % count, i) for i in range(ends)])  10.8 us
    unnamed x44, other arithmetic  4.81 us
    slice x40, local copies, waits for them, and re-layouts, interior(): return values[..., 1:-1]  3.4 us
  transfers between devices with their start and end apart: 17, of which 12 were waited for; matrix products, arithmetic and copies ran while one was open for 4% of the time, Pallas kernels for 0%

commit v1 on v0

v1 whole, which is shorter than its diff:
```python
import functools

import jax
import jax.numpy as jnp
from jax import lax
from jax.experimental import pallas as pl
from jax.experimental.pallas import tpu as pltpu
from jax.sharding import PartitionSpec as P

inner_radius = 32.0
f32 = jnp.float32
GROUP = 4
EDGE = 8
SLOTS = 3 * GROUP


def lane_index(rows=8):
    return lax.broadcasted_iota(jnp.int32, (rows, 128), 1)


def turn(x, shift, axis=1):
    if isinstance(shift, int):
        shift %= x.shape[axis]
        if shift == 0:
            return x
    return pltpu.roll(x, shift, axis)


def pack_kernel(field_ref, flow_ref, edges_ref):
    lane = lane_index()
    for comp in range(6):
        total = jnp.zeros((8, 128), f32)
        for zt in range(4):
            for mode in range(GROUP):
                at = 32 * zt + 8 * mode
                piece = turn(field_ref[mode, comp, 8 * zt : 8 * zt + 8, :], at + 4)
                total = jnp.where((lane >= at) & (lane < at + 8), piece, total)
        edges_ref[comp] = total
    for block in range(3):
        total = jnp.zeros((8, 128), f32)
        for part in range(4):
            row = 4 * block + part
            if row < 9:
                for zt in range(4):
                    at = 32 * part + 8 * zt
                    piece = turn(flow_ref[0, row, 8 * zt : 8 * zt + 8, :], at + 4)
                    total = jnp.where((lane >= at) & (lane < at + 8), piece, total)
        edges_ref[6 + block] = total


def join_kernel(pick_ref, edges_ref, left_ref, right_ref, left2_ref, right2_ref, flow_ref, flow2_ref, strips_ref, message_ref):
    low = lane_index() % 8 < 4
    for comp in range(6):
        strips_ref[0, comp] = jnp.where(low, left_ref[comp], edges_ref[comp])
        strips_ref[1, comp] = jnp.where(low, edges_ref[comp], right_ref[comp])
    keep = pick_ref[0] == 0

    @pl.when(keep)
    def _():
        for row in range(9):
            message_ref[32 * row : 32 * row + 32, :] = flow_ref[0, row]
        for block in range(3):
            message_ref[288 + 8 * block : 296 + 8 * block, :] = jnp.where(low, left_ref[6 + block], right_ref[6 + block])

    @pl.when(jnp.logical_not(keep))
    def _():
        for row in range(9):
            message_ref[32 * row : 32 * row + 32, :] = flow2_ref[0, row]
        for block in range(3):
            message_ref[288 + 8 * block : 296 + 8 * block, :] = jnp.where(low, left2_ref[block], right2_ref[block])


def emf_of(flow, lower, centre, upper):
    total = [lower[i] + upper[i] for i in range(6)]
    gap = [lower[i] - upper[i] for i in range(6)]
    steady = flow[0:3]
    swirl_re = (flow[3], flow[5], flow[7])
    swirl_im = (flow[4], flow[6], flow[8])
    out = []
    for comp in range(3):
        i, j = (comp + 1) % 3, (comp + 2) % 3
        real = (
            (steady[i] * centre[2 * j] - steady[j] * centre[2 * i])
            + (swirl_re[i] * total[2 * j] - swirl_re[j] * total[2 * i])
            - (swirl_im[i] * gap[2 * j + 1] - swirl_im[j] * gap[2 * i + 1])
        )
        imag = (
            (steady[i] * centre[2 * j + 1] - steady[j] * centre[2 * i + 1])
            + (swirl_re[i] * total[2 * j + 1] - swirl_re[j] * total[2 * i + 1])
            + (swirl_im[i] * gap[2 * j] - swirl_im[j] * gap[2 * i])
        )
        out += [real, imag]
    return out


def coefficients(radius):
    inner, outer = radius - 1.0, radius + 1.0
    return dict(
        up=1.0 + 0.5 / inner, down=1.0 - 0.5 / outer, flux_up=radius / inner, flux_down=radius / outer,
        inv=1.0 / radius, inv2=1.0 / (radius * radius),
    )


def stencil(field, emf, coef, waves):
    decay = -4.0 - (waves * waves + 1.0) * coef["inv2"]
    axial_decay = -4.0 - (waves * waves) * coef["inv2"]
    coupling = (2.0 * waves) * coef["inv2"]
    wave_over = (2.0 * waves) * coef["inv"]
    up, down = coef["up"], coef["down"]
    right = [field[i] * up for i in range(6)]
    left = [field[i] * down for i in range(6)]
    above = list(field)
    below = list(field)
    place = [field[i] * (decay if i < 4 else axial_decay) for i in range(6)]
    for part in range(2):
        right[2 + part] = right[2 + part] - emf[4 + part]
        left[2 + part] = left[2 + part] + emf[4 + part]
        right[4 + part] = right[4 + part] + emf[2 + part] * coef["flux_up"]
        left[4 + part] = left[4 + part] - emf[2 + part] * coef["flux_down"]
        above[part] = field[part] - emf[2 + part]
        below[part] = field[part] + emf[2 + part]
        above[2 + part] = field[2 + part] + emf[part]
        below[2 + part] = field[2 + part] - emf[part]
    place[0] = place[0] + coupling * field[3] - wave_over * emf[5]
    place[1] = place[1] - coupling * field[2] + wave_over * emf[4]
    place[2] = place[2] - coupling * field[1]
    place[3] = place[3] + coupling * field[0]
    place[4] = place[4] + wave_over * emf[1]
    place[5] = place[5] - wave_over * emf[0]
    return right, left, above, below, place


def steps_kernel(
    modes, tiles, info_ref, flow_ref, flow2_ref, strips_own, strips_low, strips_high, own_hbm, low_hbm, high_hbm, out_ref,
    state, trial, half, strip, strip_trial, strip_half, inject, flow, flow_strip, sems,
):
    loads = [
        pltpu.make_async_copy(src, state.at[pl.ds(GROUP * i, GROUP)], sems.at[i])
        for i, src in enumerate((low_hbm, own_hbm, high_hbm))
    ]
    for load in loads:
        load.start()
    base, tile, take = info_ref[0], info_ref[1], info_ref[2]
    lane8, lane = lane_index(), lane_index(32)
    row = lax.broadcasted_iota(jnp.int32, (32, 128), 0)
    column8 = lane8 % 8

    for source, wanted in ((flow_ref, 0), (flow2_ref, 1)):

        @pl.when(take == wanted)
        def _(source=source):
            for r in range(9):
                flow[r] = source[32 * r : 32 * r + 32, :]
            own = jnp.where(column8 < 4, 124 + column8, column8 - 4)
            for r in range(9):
                halo = source[288 + 8 * (r // 4) : 296 + 8 * (r // 4), :]
                for zt in range(4):
                    rows = slice(8 * zt, 8 * zt + 8)
                    inside = jnp.take_along_axis(source[32 * r + 8 * zt : 32 * r + 8 * zt + 8, :], own, axis=1)
                    outside = jnp.take_along_axis(halo, 32 * (r % 4) + 8 * zt + column8, axis=1)
                    flow_strip[0, r, rows] = jnp.where(column8 < 4, outside, inside)
                    flow_strip[1, r, rows] = jnp.where(column8 < 4, inside, outside)

    for side in range(2):
        for comp in range(6):
            low, own, high = strips_low[side, comp], strips_own[side, comp], strips_high[side, comp]
            for zt in range(4):
                value = jnp.where(lane8 < 32, turn(low, -32 * zt), turn(own, 32 - 32 * zt))
                value = jnp.where(lane8 < 64, value, turn(high, 64 - 32 * zt))
                strip[side, comp, 8 * zt : 8 * zt + 8] = jnp.where(lane8 < 96, value, 0.0)

    def wave_at(slot):
        return lax.rem(base + slot, modes) - modes // 2

    first_column = tile * 128
    radius = inner_radius + 0.5 + (first_column + lane8[:1]).astype(f32)
    main_coef = coefficients(radius)
    strip_waves = wave_at(lane8[:1] // 8).astype(f32)
    strip_coef, strip_inside = [], []
    for side in range(2):
        column = first_column + column8[:1] + (124 if side else -4)
        strip_coef.append(coefficients(inner_radius + 0.5 + column.astype(f32)))
        strip_inside.append((column >= 0) & (column < tiles * 128))

    def from_above(x):
        return turn(jnp.where(row == 0, 0.0, x), -1, 0)

    def from_below(x):
        return turn(jnp.where(row == 31, 0.0, x), 1, 0)

    def strips_eval(source, store):
        rights = []
        for side in range(2):
            centre = [source[side, i] for i in range(6)]
            lower = [turn(x, EDGE) for x in centre]
            upper = [turn(x, -EDGE) for x in centre]
            emf = emf_of([flow_strip[side, r] for r in range(9)], lower, centre, upper)
            right, left, above, below, place = stencil(centre, emf, strip_coef[side], strip_waves)
            if side == 0:
                for i in range(6):
                    inject[i] = left[i]
            else:
                for i in range(6):
                    inject[i] = jnp.where(lane % 8 == 4, right[i], inject[i])
            if store is not None:
                for i in range(6):
                    twice = (turn(right[i], -1) + turn(left[i], 1)) + (from_above(above[i]) + from_below(below[i])) + place[i]
                    store(side, i, jnp.where(strip_inside[side], twice, 0.0), centre[i])

    def main_eval(source, start, stop, store):
        def one(k, carry):
            waves = wave_at(k).astype(f32)
            centre = [source[k, i] for i in range(6)]
            emf = emf_of(
                [flow[r] for r in range(9)], [source[k - 1, i] for i in range(6)], centre, [source[k + 1, i] for i in range(6)]
            )
            right, left, above, below, place = stencil(centre, emf, main_coef, waves)
            away = 124 - EDGE * k
            for i in range(6):
                edge = pltpu.roll(inject[i], away, 1)
                next_column = turn(jnp.where(lane == 0, edge, right[i]), -1)
                last_column = turn(jnp.where(lane == 127, edge, left[i]), 1)
                twice = (next_column + last_column) + (from_above(above[i]) + from_below(below[i])) + place[i]
                store(k, i, twice, centre[i])
            return carry

        lax.fori_loop(start, stop, one, 0)

    def first_main(k, i, twice, value):
        trial[k, i] = value + 0.1 * twice
        half[k, i] = value + 0.05 * twice

    def second_main(k, i, twice, value):
        state[k, i] = half[k, i] + 0.05 * twice

    def last_main(k, i, twice, value):
        out_ref[k - GROUP, i] = half[k, i] + 0.05 * twice

    def first_strip(side, i, twice, value):
        strip_trial[side, i] = value + 0.1 * twice
        strip_half[side, i] = value + 0.05 * twice

    def second_strip(side, i, twice, value):
        strip[side, i] = strip_half[side, i] + 0.05 * twice

    strips_eval(strip, first_strip)
    for load in loads:
        load.wait()
    main_eval(state, 1, 11, first_main)
    strips_eval(strip_trial, second_strip)
    main_eval(trial, 2, 10, second_main)
    strips_eval(strip, first_strip)
    main_eval(state, 3, 9, first_main)
    strips_eval(strip_trial, None)
    main_eval(trial, 4, 8, last_main)


VMEM = pl.BlockSpec(memory_space=pltpu.VMEM)
SMEM = pl.BlockSpec(memory_space=pltpu.SMEM)
ANY = pl.BlockSpec(memory_space=pl.ANY)


def shape(*dims):
    return jax.ShapeDtypeStruct(dims, f32)


def body(magnetic, velocity_stack, wavenumber, velocity_owner):
    groups, tiles = lax.axis_size("mode"), lax.axis_size("tile")
    me, tile = lax.axis_index("mode"), lax.axis_index("tile")
    modes = groups * GROUP
    away = jnp.bitwise_xor(me, velocity_owner[0])

    def to_mode(x, step):
        return lax.ppermute(x, "mode", [(i, (i + step) % groups) for i in range(groups)])

    def across(x, bit):
        return lax.ppermute(x, "mode", [(i, i ^ bit) for i in range(groups)])

    def to_tile(x, step):
        return lax.ppermute(x, "tile", [(i, i + step) for i in range(tiles) if 0 <= i + step < tiles])

    def to_tile_across(x, step, bit):
        pairs = [
            (g * tiles + i, (g ^ bit) * tiles + i + step)
            for g in range(groups)
            for i in range(tiles)
            if 0 <= i + step < tiles
        ]
        return lax.ppermute(x, ("mode", "tile"), pairs)

    flow2 = across(velocity_stack, 1)
    low = to_mode(magnetic, 1)
    high = to_mode(magnetic, -1)
    edges = pl.pallas_call(pack_kernel, out_shape=shape(9, 8, 128), in_specs=[VMEM, VMEM], out_specs=VMEM, name="pack_edges")(
        magnetic, velocity_stack
    )
    left, right = to_tile(edges, 1), to_tile(edges, -1)
    left2, right2 = to_tile_across(edges[6:], 1, 1), to_tile_across(edges[6:], -1, 1)
    strips, message = pl.pallas_call(
        join_kernel,
        out_shape=(shape(2, 6, 8, 128), shape(312, 128)),
        in_specs=[SMEM] + [VMEM] * 7,
        out_specs=(VMEM, VMEM),
        name="join_edges",
    )(jnp.bitwise_and(away, 1).reshape(1), edges, left, right, left2, right2, velocity_stack, flow2)
    strips_low, strips_high = to_mode(strips, 1), to_mode(strips, -1)
    bit = 2
    while 2 * bit < groups:
        message = jnp.where(jnp.bitwise_and(away, bit) == 0, message, across(message, bit))
        bit *= 2
    message2 = across(message, bit)
    info = jnp.stack(
        [
            lax.rem(wavenumber[0] + modes // 2 + modes - GROUP, modes),
            tile,
            (jnp.bitwise_and(away, bit) != 0).astype(jnp.int32),
        ]
    ).astype(jnp.int32)
    return pl.pallas_call(
        functools.partial(steps_kernel, modes, tiles),
        out_shape=shape(GROUP, 6, 32, 128),
        in_specs=[SMEM] + [VMEM] * 5 + [ANY] * 3,
        out_specs=VMEM,
        scratch_shapes=[
            pltpu.VMEM((SLOTS, 6, 32, 128), f32),
            pltpu.VMEM((SLOTS, 6, 32, 128), f32),
            pltpu.VMEM((SLOTS, 6, 32, 128), f32),
            pltpu.VMEM((2, 6, 32, 128), f32),
            pltpu.VMEM((2, 6, 32, 128), f32),
            pltpu.VMEM((2, 6, 32, 128), f32),
            pltpu.VMEM((6, 32, 128), f32),
            pltpu.VMEM((9, 32, 128), f32),
            pltpu.VMEM((2, 9, 32, 128), f32),
            pltpu.SemaphoreType.DMA((3,)),
        ],
        compiler_params=pltpu.CompilerParams(vmem_limit_bytes=32 * 1024 * 1024),
        name="heun_steps",
    )(info, message, message2, strips, strips_low, strips_high, magnetic, low, high)


def solution(mesh):
    placed = (P("mode", None, None, "tile"), P("mode", None, None, "tile"), P("mode"), P())
    return jax.shard_map(
        body, mesh=mesh, in_specs=placed, out_specs=P("mode", None, None, "tile"), check_vma=False
    )
```

time: 165 us -> 53.4 us (0.32); the launches traced: 163 us -> 53.1 us
  waiting for transfers between devices: 93.2 us -> 13 us
  between operations: 14.7 us -> 0.84 us
  Pallas kernels: 0 us -> 12.7 us
  other arithmetic: 12.1 us -> 0.1 us
  local copies, waits for them, and re-layouts: 13.2 us -> 1.37 us
  starting transfers between devices: 29.5 us -> 25.1 us
    psum x1 -> x0, waiting for transfers between devices: 64.3 us -> none  [from_root(): return lax.psum(jnp.where(mine, x, jnp.zeros_like(x)), axis)]
    ppermute x16 -> x11, waiting for transfers between devices: 28.9 us -> 13 us  [the longest x4 11.8 us: to_mode(): lax.ppermute(x, 'mode', [(i, (i + step) % groups) for i in range(groups)])]
    pallas_call x0 -> x3, Pallas kernels: none -> 12.7 us  [the longest x1 9.09 us: body(): pl.pallas_call(functools.partial(steps_kernel, modes, tiles), out_shape=s...]
    slice x48 -> x1, local copies, waits for them, and re-layouts: 5.57 us -> 0.71 us  [body(): edges[6:]]
    unnamed x44 -> x0, other arithmetic: 4.81 us -> none
    ppermute x16 -> x11, starting transfers between devices: 29.5 us -> 25.1 us  [the longest x4 8.02 us: to_mode(): lax.ppermute(x, 'mode', [(i, (i + step) % groups) for i in range(groups)])]
    ppermute x8 -> x0, local copies, waits for them, and re-layouts: 2.91 us -> none  [the longest x4 1.46 us: with_halo(): lax.ppermute(tail, axis, [(i, (i + 1) % count) for i in range(ends)])]
    concatenate x4 -> x0, other arithmetic: 2.69 us -> none  [with_halo(): jnp.concatenate([lax.ppermute(tail, axis, [(i, (i + 1) % count) for i in...]
  transfers between devices with their start and end apart: 17 -> 11, of which waited for: 12 -> 3; matrix products, arithmetic and copies ran while one was open for 4% -> 2% of each run, Pallas kernels for 0% -> 3%
where the time goes in v1:
time: 53.4 us; the launch traced here: 53.1 us
  starting transfers between devices  25.1 us (47%)
  waiting for transfers between devices  13 us (24%)
  Pallas kernels  12.7 us (24%)
  local copies, waits for them, and re-layouts  1.37 us (3%)
  between operations  0.84 us (2%)
    ppermute x4, waiting for transfers between devices, to_mode(): lax.ppermute(x, 'mode', [(i, (i + step) % groups) for i in range(groups)])  11.8 us
    pallas_call x1, Pallas kernels, body(): pl.pallas_call(functools.partial(steps_kernel, modes, tiles), out_shape=s...  9.09 us
    ppermute x4, starting transfers between devices, to_mode(): lax.ppermute(x, 'mode', [(i, (i + step) % groups) for i in range(groups)])  8.02 us
    ppermute x3, starting transfers between devices, across(): return lax.ppermute(x, 'mode', [(i, i ^ bit) for i in range(groups)])  7.2 us
    ppermute x2, starting transfers between devices, to_tile_across(): return lax.ppermute(x, ('mode', 'tile'), pairs)  5.55 us
    ppermute x2, starting transfers between devices, to_tile(): lax.ppermute(x, 'tile', [(i, i + step) for i in range(tiles) if 0 <= i +...  4.31 us
    pallas_call x1, Pallas kernels, body(): pl.pallas_call(pack_kernel, out_shape=shape(9, 8, 128), in_specs=[VMEM, V...  1.84 us
    pallas_call x1, Pallas kernels, body(): pl.pallas_call(join_kernel, out_shape=(shape(2, 6, 8, 128), shape(312, 12...  1.77 us
  transfers between devices with their start and end apart: 11, of which 3 were waited for; matrix products, arithmetic and copies ran while one was open for 2% of the time, Pallas kernels for 3%

profile of v1, /device:TPU:0, one launch (start us, length us, event | category | flops | bytes accessed | tf_op | source)
XLA Modules:
  0.0 53.1 jit_solution(14235680206224216896)
XLA Ops:
  0.0 0.0 copy-start
  0.0 3.0 %collective-permute-start.4 = (f32[1,9,32,128]{3,2,1,0:T(8,128)}, f32[1,9,32,128]{3,2,1,0:T(8,128)S(1)}, u32[]{:S(2)}, u32[]{:S(2)}) collective-permute-start(f32[1,9,32,128]{3,2,1,0:T(8,128)} %flow_ref.3), channel_id=1, source_target_pairs={{0,4},{4,0},{8,12},{12,8},{16,20},{20,16},{24,28},{28,24},{1,5},{5... | collective-permute-start | bytes 442376 | tf_op jit(solution)/shard_map/ppermute | solution.py:277
  3.0 1.8 %pack_edges.1.edges_ref = f32[9,8,128]{2,1,0:T(8,128)} custom-call(f32[4,6,32,128]{3,2,1,0:T(8,128)} %own_hbm.1, f32[1,9,32,128]{3,2,1,0:T(8,128)} %flow_ref.3), custom_call_target="tpu_custom_call" | custom-call | tf_op jit(solution)/shard_map/pack_edges/pallas_call | solution.py:294
  4.8 1.3 %collective-permute-start.1 = (f32[9,8,128]{2,1,0:T(8,128)}, f32[9,8,128]{2,1,0:T(8,128)S(1)}, u32[]{:S(2)}, u32[]{:S(2)}) collective-permute-start(f32[9,8,128]{2,1,0:T(8,128)} %pack_edges.1.edges_ref), channel_id=1, source_target_pairs={{1,0},{2,1},{3,2},{5,4},{6,5},{7,6},{9,8},{10,9},{11,10},{13,12},{... | collective-permute-start | bytes 110600 | tf_op jit(solution)/shard_map/ppermute | solution.py:280
  6.1 3.0 %collective-permute-start = (f32[9,8,128]{2,1,0:T(8,128)}, f32[9,8,128]{2,1,0:T(8,128)S(1)}, u32[]{:S(2)}, u32[]{:S(2)}) collective-permute-start(f32[9,8,128]{2,1,0:T(8,128)} %pack_edges.1.edges_ref), channel_id=1, source_target_pairs={{0,1},{1,2},{2,3},{4,5},{5,6},{6,7},{8,9},{9,10},{10,11},{12,13},{... | collective-permute-start | bytes 110600 | tf_op jit(solution)/shard_map/ppermute | solution.py:280
  9.1 0.7 %slice.9 = f32[3,8,128]{2,1,0:T(8,128)S(1)} slice(f32[9,8,128]{2,1,0:T(8,128)} %pack_edges.1.edges_ref), slice={[6:9], [0:8], [0:128]} | slice | bytes 24576 | tf_op jit(solution)/shard_map/slice | solution.py:298
  9.9 1.3 %collective-permute-start.3 = (f32[3,8,128]{2,1,0:T(8,128)S(1)}, f32[3,8,128]{2,1,0:T(8,128)S(1)}, u32[]{:S(2)}, u32[]{:S(2)}) collective-permute-start(f32[3,8,128]{2,1,0:T(8,128)S(1)} %slice.9), channel_id=1, source_target_pairs={{1,4},{2,5},{3,6},{5,0},{6,1},{7,2},{9,12},{10,13},{11,14},{13,8},... | collective-permute-start | bytes 36872 | tf_op jit(solution)/shard_map/ppermute | solution.py:289
  11.1 4.3 %collective-permute-start.2 = (f32[3,8,128]{2,1,0:T(8,128)S(1)}, f32[3,8,128]{2,1,0:T(8,128)S(1)}, u32[]{:S(2)}, u32[]{:S(2)}) collective-permute-start(f32[3,8,128]{2,1,0:T(8,128)S(1)} %slice.9), channel_id=1, source_target_pairs={{0,5},{1,6},{2,7},{4,1},{5,2},{6,3},{8,13},{9,14},{10,15},{12,9},{... | collective-permute-start | bytes 36872 | tf_op jit(solution)/shard_map/ppermute | solution.py:289
  16.1 0.0 collective-permute-done.3.right2_ref
  16.1 0.0 copy-start.5
  16.1 0.7 %collective-permute-done.2.left2_ref = f32[3,8,128]{2,1,0:T(8,128)S(1)} collective-permute-done((f32[3,8,128]{2,1,0:T(8,128)S(1)}, f32[3,8,128]{2,1,0:T(8,128)S(1)}, u32[]{:S(2)}, u32[]{:S(2)}) %collective-permute-start.2) | collective-permute-done | bytes 12320 | tf_op jit(solution)/shard_map/ppermute | solution.py:289
  16.8 0.0 copy-start.6
  16.8 0.0 collective-permute-done.1.right_ref
  16.8 0.0 copy-start.3
  16.8 0.0 collective-permute-done.left_ref
  16.8 0.0 copy-start.4
  16.8 0.0 collective-permute-done.4.flow2_ref
  16.8 0.0 copy-start.2
  16.8 0.0 copy-done.5
  16.9 0.5 %copy-done.6 = f32[3,8,128]{2,1,0:T(8,128)} copy-done((f32[3,8,128]{2,1,0:T(8,128)}, f32[3,8,128]{2,1,0:T(8,128)S(1)}, u32[]{:S(2)}) %copy-start.6) | copy-done | bytes 12312
  17.4 0.0 copy-done.3
  17.4 0.0 copy-done.4
  17.4 0.1 copy-done.2
  17.5 1.8 %join_edges.1 = (f32[2,6,8,128]{3,2,1,0:T(8,128)}, f32[312,128]{1,0:T(8,128)}) custom-call(s32[1]{0:T(128)} %bitcast.5.pick_ref, f32[9,8,128]{2,1,0:T(8,128)} %pack_edges.1.edges_ref, f32[9,8,128]{2,1,0:T(8,128)} %copy-done.4, f32[9,8,128]{2,1,0:T(8,128)} %copy-done.3, f32[3,8,128]{2,1,0:T(8,128)} %copy-done.6, f32[3,8,128]{2,1,0:T(8,128)} %copy-done.5, ...), custom_call_target="tpu_custom_call" | custom-call | tf_op jit(solution)/shard_map/join_edges/pallas_call | solution.py:299
  19.3 1.6 %collective-permute-start.5 = (f32[312,128]{1,0:T(8,128)}, f32[312,128]{1,0:T(8,128)S(1)}, u32[]{:S(2)}, u32[]{:S(2)}) collective-permute-start(f32[312,128]{1,0:T(8,128)} %get-tuple-element.7), channel_id=1, source_target_pairs={{0,8},{4,12},{8,0},{12,4},{16,24},{20,28},{24,16},{28,20},{1,9},{5... | collective-permute-start | bytes 479240 | tf_op jit(solution)/shard_map/ppermute | solution.py:277
  20.8 0.0 copy-done
  20.8 1.0 %collective-permute-start.9 = (f32[4,6,32,128]{3,2,1,0:T(8,128)S(1)}, f32[4,6,32,128]{3,2,1,0:T(8,128)S(1)}, u32[]{:S(2)}, u32[]{:S(2)}) collective-permute-start(f32[4,6,32,128]{3,2,1,0:T(8,128)S(1)} %copy-done), channel_id=1, source_target_pairs={{0,4},{4,8},{8,12},{12,16},{16,20},{20,24},{24,28},{28,0},{1,5},{5... | collective-permute-start | bytes 1179656 | tf_op jit(solution)/shard_map/ppermute | solution.py:274
  21.9 3.7 %collective-permute-start.10 = (f32[4,6,32,128]{3,2,1,0:T(8,128)S(1)}, f32[4,6,32,128]{3,2,1,0:T(8,128)S(1)}, u32[]{:S(2)}, u32[]{:S(2)}) collective-permute-start(f32[4,6,32,128]{3,2,1,0:T(8,128)S(1)} %copy-done), channel_id=1, source_target_pairs={{0,28},{4,0},{8,4},{12,8},{16,12},{20,16},{24,20},{28,24},{1,29},{... | collective-permute-start | bytes 1179656 | tf_op jit(solution)/shard_map/ppermute | solution.py:274
  25.6 0.0 copy-start.1
  25.6 0.5 collective-permute-done.5
  26.1 0.0 copy-start.7
  26.1 2.7 %collective-permute-start.6 = (f32[312,128]{1,0:T(8,128)S(1)}, f32[312,128]{1,0:T(8,128)S(1)}, u32[]{:S(2)}, u32[]{:S(2)}) collective-permute-start(f32[312,128]{1,0:T(8,128)S(1)} %broadcast_select_fusion.flow_ref), channel_id=1, source_target_pairs={{0,16},{4,20},{8,24},{12,28},{16,0},{20,4},{24,8},{28,12},{1,17},{... | collective-permute-start | bytes 479240 | tf_op jit(solution)/shard_map/ppermute | solution.py:277
  28.8 0.0 copy-done.7
  28.8 0.0 copy-done.1
  28.8 3.3 %collective-permute-start.8 = (f32[2,6,8,128]{3,2,1,0:T(8,128)S(1)}, f32[2,6,8,128]{3,2,1,0:T(8,128)S(1)}, u32[]{:S(2)}, u32[]{:S(2)}) collective-permute-start(f32[2,6,8,128]{3,2,1,0:T(8,128)S(1)} %copy-done.1), channel_id=1, source_target_pairs={{0,28},{4,0},{8,4},{12,8},{16,12},{20,16},{24,20},{28,24},{1,29},{... | collective-permute-start | bytes 147464 | tf_op jit(solution)/shard_map/ppermute | solution.py:274
  32.1 0.0 collective-permute-start.7
  32.1 0.1 pad_add_fusion.info_ref
  32.2 11.7 %collective-permute-done.8.strips_high = f32[2,6,8,128]{3,2,1,0:T(8,128)S(1)} collective-permute-done((f32[2,6,8,128]{3,2,1,0:T(8,128)S(1)}, f32[2,6,8,128]{3,2,1,0:T(8,128)S(1)}, u32[]{:S(2)}, u32[]{:S(2)}) %collective-permute-start.8) | collective-permute-done | bytes 49184 | tf_op jit(solution)/shard_map/ppermute | solution.py:274
  44.0 0.0 collective-permute-done.7.strips_low
  44.0 0.0 collective-permute-done.9.low_hbm
  44.0 0.0 collective-permute-done.10.high_hbm
  44.0 0.0 collective-permute-done.6.flow2_ref
  44.0 9.1 %heun_steps.1 = f32[4,6,32,128]{3,2,1,0:T(8,128)} custom-call(s32[3]{0:T(128)S(1)} %pad_add_fusion.info_ref, f32[312,128]{1,0:T(8,128)S(1)} %broadcast_select_fusion.flow_ref, f32[312,128]{1,0:T(8,128)S(1)} %collective-permute-done.6.flow2_ref, f32[2,6,8,128]{3,2,1,0:T(8,128)S(1)} %copy-done.1, f32[2,6,8,128]{3,2,1,0:T(8,128)S(1)} %collective-permute-done.7.strips_low, ...), custom_call_target="tpu_custom_call" | custom-call | tf_op jit(solution)/shard_map/heun_steps/pallas_call | solution.py:319
  (1 shorter events, 0.0 us)
Async XLA Ops:
  0.0 20.8 %copy-start = (f32[4,6,32,128]{3,2,1,0:T(8,128)S(1)}, f32[4,6,32,128]{3,2,1,0:T(8,128)}, u32[]{:S(2)}) copy-start(f32[4,6,32,128]{3,2,1,0:T(8,128)} %own_hbm.1) | copy-start | bytes 1179652
  0.0 16.8 %collective-permute-start.4 = (f32[1,9,32,128]{3,2,1,0:T(8,128)}, f32[1,9,32,128]{3,2,1,0:T(8,128)S(1)}, u32[]{:S(2)}, u32[]{:S(2)}) collective-permute-start(f32[1,9,32,128]{3,2,1,0:T(8,128)} %flow_ref.3), channel_id=1, source_target_pairs={{0,4},{4,0},{8,12},{12,8},{16,20},{20,16},{24,28},{28,24},{1,5},{5... | collective-permute-start | bytes 442376 | tf_op jit(solution)/shard_map/ppermute | solution.py:277
  4.8 12.0 %collective-permute-start.1 = (f32[9,8,128]{2,1,0:T(8,128)}, f32[9,8,128]{2,1,0:T(8,128)S(1)}, u32[]{:S(2)}, u32[]{:S(2)}) collective-permute-start(f32[9,8,128]{2,1,0:T(8,128)} %pack_edges.1.edges_ref), channel_id=1, source_target_pairs={{1,0},{2,1},{3,2},{5,4},{6,5},{7,6},{9,8},{10,9},{11,10},{13,12},{... | collective-permute-start | bytes 110600 | tf_op jit(solution)/shard_map/ppermute | solution.py:280
  6.1 10.7 %collective-permute-start = (f32[9,8,128]{2,1,0:T(8,128)}, f32[9,8,128]{2,1,0:T(8,128)S(1)}, u32[]{:S(2)}, u32[]{:S(2)}) collective-permute-start(f32[9,8,128]{2,1,0:T(8,128)} %pack_edges.1.edges_ref), channel_id=1, source_target_pairs={{0,1},{1,2},{2,3},{4,5},{5,6},{6,7},{8,9},{9,10},{10,11},{12,13},{... | collective-permute-start | bytes 110600 | tf_op jit(solution)/shard_map/ppermute | solution.py:280
  9.9 6.2 %collective-permute-start.3 = (f32[3,8,128]{2,1,0:T(8,128)S(1)}, f32[3,8,128]{2,1,0:T(8,128)S(1)}, u32[]{:S(2)}, u32[]{:S(2)}) collective-permute-start(f32[3,8,128]{2,1,0:T(8,128)S(1)} %slice.9), channel_id=1, source_target_pairs={{1,4},{2,5},{3,6},{5,0},{6,1},{7,2},{9,12},{10,13},{11,14},{13,8},... | collective-permute-start | bytes 36872 | tf_op jit(solution)/shard_map/ppermute | solution.py:289
  11.1 5.7 %collective-permute-start.2 = (f32[3,8,128]{2,1,0:T(8,128)S(1)}, f32[3,8,128]{2,1,0:T(8,128)S(1)}, u32[]{:S(2)}, u32[]{:S(2)}) collective-permute-start(f32[3,8,128]{2,1,0:T(8,128)S(1)} %slice.9), channel_id=1, source_target_pairs={{0,5},{1,6},{2,7},{4,1},{5,2},{6,3},{8,13},{9,14},{10,15},{12,9},{... | collective-permute-start | bytes 36872 | tf_op jit(solution)/shard_map/ppermute | solution.py:289
  16.1 0.8 %copy-start.5 = (f32[3,8,128]{2,1,0:T(8,128)}, f32[3,8,128]{2,1,0:T(8,128)S(1)}, u32[]{:S(2)}) copy-start(f32[3,8,128]{2,1,0:T(8,128)S(1)} %collective-permute-done.3.right2_ref) | copy-start | bytes 36868
  16.8 0.6 %copy-start.6 = (f32[3,8,128]{2,1,0:T(8,128)}, f32[3,8,128]{2,1,0:T(8,128)S(1)}, u32[]{:S(2)}) copy-start(f32[3,8,128]{2,1,0:T(8,128)S(1)} %collective-permute-done.2.left2_ref) | copy-start | bytes 36868
  16.8 0.6 %copy-start.3 = (f32[9,8,128]{2,1,0:T(8,128)}, f32[9,8,128]{2,1,0:T(8,128)S(1)}, u32[]{:S(2)}) copy-start(f32[9,8,128]{2,1,0:T(8,128)S(1)} %collective-permute-done.1.right_ref) | copy-start | bytes 110596
  16.8 0.6 %copy-start.4 = (f32[9,8,128]{2,1,0:T(8,128)}, f32[9,8,128]{2,1,0:T(8,128)S(1)}, u32[]{:S(2)}) copy-start(f32[9,8,128]{2,1,0:T(8,128)S(1)} %collective-permute-done.left_ref) | copy-start | bytes 110596
  16.8 0.7 %copy-start.2 = (f32[1,9,32,128]{3,2,1,0:T(8,128)}, f32[1,9,32,128]{3,2,1,0:T(8,128)S(1)}, u32[]{:S(2)}) copy-start(f32[1,9,32,128]{3,2,1,0:T(8,128)S(1)} %collective-permute-done.4.flow2_ref) | copy-start | bytes 442372
  19.3 6.8 %collective-permute-start.5 = (f32[312,128]{1,0:T(8,128)}, f32[312,128]{1,0:T(8,128)S(1)}, u32[]{:S(2)}, u32[]{:S(2)}) collective-permute-start(f32[312,128]{1,0:T(8,128)} %get-tuple-element.7), channel_id=1, source_target_pairs={{0,8},{4,12},{8,0},{12,4},{16,24},{20,28},{24,16},{28,20},{1,9},{5... | collective-permute-start | bytes 479240 | tf_op jit(solution)/shard_map/ppermute | solution.py:277
  20.8 23.1 %collective-permute-start.9 = (f32[4,6,32,128]{3,2,1,0:T(8,128)S(1)}, f32[4,6,32,128]{3,2,1,0:T(8,128)S(1)}, u32[]{:S(2)}, u32[]{:S(2)}) collective-permute-start(f32[4,6,32,128]{3,2,1,0:T(8,128)S(1)} %copy-done), channel_id=1, source_target_pairs={{0,4},{4,8},{8,12},{12,16},{16,20},{20,24},{24,28},{28,0},{1,5},{5... | collective-permute-start | bytes 1179656 | tf_op jit(solution)/shard_map/ppermute | solution.py:274
  21.9 22.1 %collective-permute-start.10 = (f32[4,6,32,128]{3,2,1,0:T(8,128)S(1)}, f32[4,6,32,128]{3,2,1,0:T(8,128)S(1)}, u32[]{:S(2)}, u32[]{:S(2)}) collective-permute-start(f32[4,6,32,128]{3,2,1,0:T(8,128)S(1)} %copy-done), channel_id=1, source_target_pairs={{0,28},{4,0},{8,4},{12,8},{16,12},{20,16},{24,20},{28,24},{1,29},{... | collective-permute-start | bytes 1179656 | tf_op jit(solution)/shard_map/ppermute | solution.py:274
  25.6 3.2 %copy-start.1 = (f32[2,6,8,128]{3,2,1,0:T(8,128)S(1)}, f32[2,6,8,128]{3,2,1,0:T(8,128)}, u32[]{:S(2)}) copy-start(f32[2,6,8,128]{3,2,1,0:T(8,128)} %get-tuple-element.8.strips_own) | copy-start | bytes 147460
  26.1 2.7 %copy-start.7 = (s32[4]{0:T(128)S(1)}, s32[4]{0:T(128)}, u32[]{:S(2)}) copy-start(s32[4]{0:T(128)} %param.6) | copy-start | bytes 52
  26.1 17.9 %collective-permute-start.6 = (f32[312,128]{1,0:T(8,128)S(1)}, f32[312,128]{1,0:T(8,128)S(1)}, u32[]{:S(2)}, u32[]{:S(2)}) collective-permute-start(f32[312,128]{1,0:T(8,128)S(1)} %broadcast_select_fusion.flow_ref), channel_id=1, source_target_pairs={{0,16},{4,20},{8,24},{12,28},{16,0},{20,4},{24,8},{28,12},{1,17},{... | collective-permute-start | bytes 479240 | tf_op jit(solution)/shard_map/ppermute | solution.py:277
  28.8 15.1 %collective-permute-start.8 = (f32[2,6,8,128]{3,2,1,0:T(8,128)S(1)}, f32[2,6,8,128]{3,2,1,0:T(8,128)S(1)}, u32[]{:S(2)}, u32[]{:S(2)}) collective-permute-start(f32[2,6,8,128]{3,2,1,0:T(8,128)S(1)} %copy-done.1), channel_id=1, source_target_pairs={{0,28},{4,0},{8,4},{12,8},{16,12},{20,16},{24,20},{28,24},{1,29},{... | collective-permute-start | bytes 147464 | tf_op jit(solution)/shard_map/ppermute | solution.py:274
  32.1 11.8 %collective-permute-start.7 = (f32[2,6,8,128]{3,2,1,0:T(8,128)S(1)}, f32[2,6,8,128]{3,2,1,0:T(8,128)S(1)}, u32[]{:S(2)}, u32[]{:S(2)}) collective-permute-start(f32[2,6,8,128]{3,2,1,0:T(8,128)S(1)} %copy-done.1), channel_id=1, source_target_pairs={{0,4},{4,8},{8,12},{12,16},{16,20},{20,24},{24,28},{28,0},{1,5},{5... | collective-permute-start | bytes 147464 | tf_op jit(solution)/shard_map/ppermute | solution.py:274

commit v2 on v1

v2 whole, which is shorter than its diff:
```python
import functools

import jax
import jax.numpy as jnp
from jax import lax
from jax.experimental import pallas as pl
from jax.experimental.pallas import tpu as pltpu
from jax.sharding import PartitionSpec as P

inner_radius = 32.0
f32 = jnp.float32
GROUP = 4
EDGE = 8
SLOTS = 3 * GROUP


def lane_index(rows=8):
    return lax.broadcasted_iota(jnp.int32, (rows, 128), 1)


def turn(x, shift, axis=1):
    if isinstance(shift, int):
        shift %= x.shape[axis]
        if shift == 0:
            return x
    return pltpu.roll(x, shift, axis)


def pack_kernel(field_ref, flow_ref, edges_ref):
    lane = lane_index()
    for comp in range(6):
        total = jnp.zeros((8, 128), f32)
        for zt in range(4):
            for mode in range(GROUP):
                at = 32 * zt + 8 * mode
                piece = turn(field_ref[mode, comp, 8 * zt : 8 * zt + 8, :], at + 4)
                total = jnp.where((lane >= at) & (lane < at + 8), piece, total)
        edges_ref[comp] = total
    for block in range(3):
        total = jnp.zeros((8, 128), f32)
        for part in range(4):
            row = 4 * block + part
            if row < 9:
                for zt in range(4):
                    at = 32 * part + 8 * zt
                    piece = turn(flow_ref[0, row, 8 * zt : 8 * zt + 8, :], at + 4)
                    total = jnp.where((lane >= at) & (lane < at + 8), piece, total)
        edges_ref[6 + block] = total


def strips_kernel(edges_ref, left_ref, right_ref, strips_ref, halo_ref):
    low = lane_index() % 8 < 4
    for comp in range(6):
        strips_ref[0, comp] = jnp.where(low, left_ref[comp], edges_ref[comp])
        strips_ref[1, comp] = jnp.where(low, edges_ref[comp], right_ref[comp])
    for block in range(3):
        halo_ref[block] = jnp.where(low, left_ref[6 + block], right_ref[6 + block])


def join_kernel(pick_ref, flow_ref, flow2_ref, halo_ref, halo2_ref, strips_ref, message_ref):
    for side in range(2):
        for comp in range(6):
            at = 312 + 48 * side + 8 * comp
            message_ref[at : at + 8, :] = strips_ref[side, comp]
    for source, halo, wanted in ((flow_ref, halo_ref, 0), (flow2_ref, halo2_ref, 1)):

        @pl.when(jnp.where(pick_ref[0] == 0, 0, 1) == wanted)
        def _(source=source, halo=halo):
            for row in range(9):
                message_ref[32 * row : 32 * row + 32, :] = source[0, row]
            for block in range(3):
                message_ref[288 + 8 * block : 296 + 8 * block, :] = halo[block]


def emf_of(flow, lower, centre, upper):
    total = [lower[i] + upper[i] for i in range(6)]
    gap = [lower[i] - upper[i] for i in range(6)]
    steady = flow[0:3]
    swirl_re = (flow[3], flow[5], flow[7])
    swirl_im = (flow[4], flow[6], flow[8])
    out = []
    for comp in range(3):
        i, j = (comp + 1) % 3, (comp + 2) % 3
        real = (
            (steady[i] * centre[2 * j] - steady[j] * centre[2 * i])
            + (swirl_re[i] * total[2 * j] - swirl_re[j] * total[2 * i])
            - (swirl_im[i] * gap[2 * j + 1] - swirl_im[j] * gap[2 * i + 1])
        )
        imag = (
            (steady[i] * centre[2 * j + 1] - steady[j] * centre[2 * i + 1])
            + (swirl_re[i] * total[2 * j + 1] - swirl_re[j] * total[2 * i + 1])
            + (swirl_im[i] * gap[2 * j] - swirl_im[j] * gap[2 * i])
        )
        out += [real, imag]
    return out


def coefficients(radius):
    inner, outer = radius - 1.0, radius + 1.0
    return dict(
        up=1.0 + 0.5 / inner, down=1.0 - 0.5 / outer, flux_up=radius / inner, flux_down=radius / outer,
        inv=1.0 / radius, inv2=1.0 / (radius * radius),
    )


def stencil(field, emf, coef, waves):
    decay = -4.0 - (waves * waves + 1.0) * coef["inv2"]
    axial_decay = -4.0 - (waves * waves) * coef["inv2"]
    coupling = (2.0 * waves) * coef["inv2"]
    wave_over = (2.0 * waves) * coef["inv"]
    up, down = coef["up"], coef["down"]
    right = [field[i] * up for i in range(6)]
    left = [field[i] * down for i in range(6)]
    above = list(field)
    below = list(field)
    place = [field[i] * (decay if i < 4 else axial_decay) for i in range(6)]
    for part in range(2):
        right[2 + part] = right[2 + part] - emf[4 + part]
        left[2 + part] = left[2 + part] + emf[4 + part]
        right[4 + part] = right[4 + part] + emf[2 + part] * coef["flux_up"]
        left[4 + part] = left[4 + part] - emf[2 + part] * coef["flux_down"]
        above[part] = field[part] - emf[2 + part]
        below[part] = field[part] + emf[2 + part]
        above[2 + part] = field[2 + part] + emf[part]
        below[2 + part] = field[2 + part] - emf[part]
    place[0] = place[0] + coupling * field[3] - wave_over * emf[5]
    place[1] = place[1] - coupling * field[2] + wave_over * emf[4]
    place[2] = place[2] - coupling * field[1]
    place[3] = place[3] + coupling * field[0]
    place[4] = place[4] + wave_over * emf[1]
    place[5] = place[5] - wave_over * emf[0]
    return right, left, above, below, place


def start_loads(info_ref, own_hbm, pair_hbm, other_hbm, state, sems):
    odd = info_ref[3]
    places = (GROUP, 2 * GROUP * (1 - odd), 2 * GROUP * odd)
    loads = [
        pltpu.make_async_copy(src, state.at[pl.ds(place, GROUP)], sems.at[i])
        for i, (src, place) in enumerate(zip((own_hbm, pair_hbm, other_hbm), places))
    ]
    for load in loads:
        load.start()
    return loads


def wave_at(base, slot, modes):
    return (lax.rem(base + slot, modes) - modes // 2).astype(f32)


def column_radius(column):
    return inner_radius + 0.5 + column.astype(f32)


def from_above(x):
    row = lax.broadcasted_iota(jnp.int32, (32, 128), 0)
    return turn(jnp.where(row == 0, 0.0, x), -1, 0)


def from_below(x):
    row = lax.broadcasted_iota(jnp.int32, (32, 128), 0)
    return turn(jnp.where(row == 31, 0.0, x), 1, 0)


def main_eval(source, flow, coef, base, modes, start, stop, edges, store):
    lane = lane_index(32)

    def one(k, carry):
        centre = [source[k, i] for i in range(6)]
        emf = emf_of(
            [flow[r] for r in range(9)], [source[k - 1, i] for i in range(6)], centre, [source[k + 1, i] for i in range(6)]
        )
        right, left, above, below, place = stencil(centre, emf, coef, wave_at(base, k, modes))
        for i in range(6):
            edge = pltpu.roll(edges[i], 124 - EDGE * k, 1)
            next_column = turn(jnp.where(lane == 0, edge, right[i]), -1)
            last_column = turn(jnp.where(lane == 127, edge, left[i]), 1)
            twice = (next_column + last_column) + (from_above(above[i]) + from_below(below[i])) + place[i]
            store(k, i, twice, centre[i])
        return carry

    lax.fori_loop(start, stop, one, 0)


def steps_kernel(
    modes, tiles, info_ref, message_ref, message2_ref, strips_own, strips_other, own_hbm, pair_hbm, other_hbm,
    out_ref, state, trial, half, strip, strip_trial, strip_half, inject, flow, flow_strip, sems,
):
    loads = start_loads(info_ref, own_hbm, pair_hbm, other_hbm, state, sems)
    base, tile, take, odd = info_ref[0], info_ref[1], info_ref[2], info_ref[3]
    lane8, lane = lane_index(), lane_index(32)
    column8 = lane8 % 8

    for source, wanted in ((message_ref, 0), (message2_ref, 1)):

        @pl.when(take == wanted)
        def _(source=source):
            for r in range(9):
                flow[r] = source[32 * r : 32 * r + 32, :]
            near = jnp.where(column8 < 4, 124 + column8, column8 - 4)
            for r in range(9):
                halo = source[288 + 8 * (r // 4) : 296 + 8 * (r // 4), :]
                for zt in range(4):
                    rows = slice(8 * zt, 8 * zt + 8)
                    inside = jnp.take_along_axis(source[32 * r + 8 * zt : 32 * r + 8 * zt + 8, :], near, axis=1)
                    outside = jnp.take_along_axis(halo, 32 * (r % 4) + 8 * zt + column8, axis=1)
                    flow_strip[0, r, rows] = jnp.where(column8 < 4, outside, inside)
                    flow_strip[1, r, rows] = jnp.where(column8 < 4, inside, outside)

    for side in range(2):
        for comp in range(6):
            at = 312 + 48 * side + 8 * comp
            own, other, pair = strips_own[side, comp], strips_other[side, comp], message2_ref[at : at + 8, :]
            low, high = jnp.where(odd == 1, pair, other), jnp.where(odd == 1, other, pair)
            for zt in range(4):
                value = jnp.where(lane8 < 32, turn(low, -32 * zt), turn(own, 32 - 32 * zt))
                value = jnp.where(lane8 < 64, value, turn(high, 64 - 32 * zt))
                strip[side, comp, 8 * zt : 8 * zt + 8] = jnp.where(lane8 < 96, value, 0.0)

    first_column = tile * 128
    main_coef = coefficients(column_radius(first_column + lane8[:1]))
    strip_waves = wave_at(base, lane8[:1] // 8, modes)
    strip_coef, strip_inside = [], []
    for side in range(2):
        column = first_column + column8[:1] + (124 if side else -4)
        strip_coef.append(coefficients(column_radius(column)))
        strip_inside.append((column >= 0) & (column < tiles * 128))

    def strips_eval(source, store):
        for side in range(2):
            centre = [source[side, i] for i in range(6)]
            lower = [turn(x, EDGE) for x in centre]
            upper = [turn(x, -EDGE) for x in centre]
            emf = emf_of([flow_strip[side, r] for r in range(9)], lower, centre, upper)
            right, left, above, below, place = stencil(centre, emf, strip_coef[side], strip_waves)
            for i in range(6):
                inject[i] = jnp.where(lane % 8 == 4, right[i], inject[i]) if side else left[i]
                if store is not None:
                    twice = (turn(right[i], -1) + turn(left[i], 1)) + (from_above(above[i]) + from_below(below[i])) + place[i]
                    store(side, i, jnp.where(strip_inside[side], twice, 0.0), centre[i])

    def first_main(k, i, twice, value):
        trial[k, i] = value + 0.1 * twice
        half[k, i] = value + 0.05 * twice

    def second_main(k, i, twice, value):
        state[k, i] = half[k, i] + 0.05 * twice

    def last_main(k, i, twice, value):
        out_ref[k - GROUP, i] = half[k, i] + 0.05 * twice

    def first_strip(side, i, twice, value):
        strip_trial[side, i] = value + 0.1 * twice
        strip_half[side, i] = value + 0.05 * twice

    def second_strip(side, i, twice, value):
        strip[side, i] = strip_half[side, i] + 0.05 * twice

    main = functools.partial(main_eval, flow=flow, coef=main_coef, base=base, modes=modes, edges=inject)
    strips_eval(strip, first_strip)
    for load in loads:
        load.wait()
    main(state, start=1, stop=11, store=first_main)
    strips_eval(strip_trial, second_strip)
    main(trial, start=2, stop=10, store=second_main)
    strips_eval(strip, first_strip)
    main(state, start=3, stop=9, store=first_main)
    strips_eval(strip_trial, None)
    main(trial, start=4, stop=8, store=last_main)


VMEM = pl.BlockSpec(memory_space=pltpu.VMEM)
SMEM = pl.BlockSpec(memory_space=pltpu.SMEM)
ANY = pl.BlockSpec(memory_space=pl.ANY)


SMALL = pl.CostEstimate(flops=8, bytes_accessed=8, transcendentals=0)


def shape(*dims):
    return jax.ShapeDtypeStruct(dims, f32)


def small_kernel(kernel, name, out, in_specs):
    out_specs = (VMEM,) * len(out) if isinstance(out, tuple) else VMEM
    return pl.pallas_call(kernel, out_shape=out, in_specs=in_specs, out_specs=out_specs, cost_estimate=SMALL, name=name)


def body(magnetic, velocity_stack, wavenumber, velocity_owner):
    groups, tiles = lax.axis_size("mode"), lax.axis_size("tile")
    me, tile = lax.axis_index("mode"), lax.axis_index("tile")
    modes = groups * GROUP
    away = jnp.bitwise_xor(me, velocity_owner[0])

    def to_pair(x, first):
        pairs = []
        for i in range(first, groups, 2):
            pairs += [(i, (i + 1) % groups), ((i + 1) % groups, i)]
        return lax.ppermute(x, "mode", pairs)

    def across(x, bit):
        return lax.ppermute(x, "mode", [(i, i ^ bit) for i in range(groups)])

    def to_tile(x, step):
        return lax.ppermute(x, "tile", [(i, i + step) for i in range(tiles) if 0 <= i + step < tiles])

    bits = []
    while 2 << len(bits) < groups:
        bits.append(2 << len(bits))
    bits.append(1)
    def choose(x, y, bit):
        return jnp.where(jnp.bitwise_and(away, bit) == 0, x, y)

    pair = to_pair(magnetic, 0)
    flow = choose(velocity_stack, across(velocity_stack, bits[0]), bits[0])
    magnetic_later, flow = lax.optimization_barrier((magnetic, flow))
    other = to_pair(magnetic_later, 1)

    def small_exchanges(flow, magnetic):
        for bit in bits[1:-2]:
            flow = choose(flow, across(flow, bit), bit)
        flow2 = across(flow, bits[-2])
        edges = small_kernel(pack_kernel, "pack_edges", shape(9, 8, 128), [VMEM] * 2)(magnetic, flow)
        strips, halo = small_kernel(strips_kernel, "strips", (shape(2, 6, 8, 128), shape(3, 8, 128)), [VMEM] * 3)(
            edges, to_tile(edges, 1), to_tile(edges, -1)
        )
        halo2 = across(halo, bits[-2])
        pick = jnp.bitwise_and(away, bits[-2]).reshape(1)
        message = small_kernel(join_kernel, "join", shape(408, 128), [SMEM] + [VMEM] * 5)(
            pick, flow, flow2, halo, halo2, strips
        )
        return message, across(message, bits[-1]), strips, to_pair(strips, 1)

    def none(flow, magnetic):
        message, strips = jnp.zeros((408, 128), f32), jnp.zeros((2, 6, 8, 128), f32)
        return message, message, strips, strips

    message, message2, strips, strips_other = lax.cond(velocity_owner[0] >= 0, small_exchanges, none, flow, magnetic)
    info = jnp.stack(
        [
            lax.rem(wavenumber[0] + modes // 2 + modes - GROUP, modes),
            tile,
            jnp.bitwise_and(away, bits[-1]),
            jnp.bitwise_and(me, 1),
        ]
    ).astype(jnp.int32)
    return pl.pallas_call(
        functools.partial(steps_kernel, modes, tiles),
        out_shape=shape(GROUP, 6, 32, 128),
        in_specs=[SMEM] + [VMEM] * 4 + [ANY] * 3,
        out_specs=VMEM,
        scratch_shapes=[
            pltpu.VMEM((SLOTS, 6, 32, 128), f32),
            pltpu.VMEM((SLOTS, 6, 32, 128), f32),
            pltpu.VMEM((SLOTS, 6, 32, 128), f32),
            pltpu.VMEM((2, 6, 32, 128), f32),
            pltpu.VMEM((2, 6, 32, 128), f32),
            pltpu.VMEM((2, 6, 32, 128), f32),
            pltpu.VMEM((6, 32, 128), f32),
            pltpu.VMEM((9, 32, 128), f32),
            pltpu.VMEM((2, 9, 32, 128), f32),
            pltpu.SemaphoreType.DMA((3,)),
        ],
        compiler_params=pltpu.CompilerParams(vmem_limit_bytes=32 * 1024 * 1024),
        name="heun_steps",
    )(info, message, message2, strips, strips_other, magnetic, pair, other)


def solution(mesh):
    placed = (P("mode", None, None, "tile"), P("mode", None, None, "tile"), P("mode"), P())
    return jax.shard_map(
        body, mesh=mesh, in_specs=placed, out_specs=P("mode", None, None, "tile"), check_vma=False
    )
```

time: 53.4 us -> 47.8 us (0.90)
  waiting for transfers between devices: 13 us -> 8.42 us
  starting transfers between devices: 25.1 us -> 21.9 us
  other arithmetic: 0.1 us -> 1.01 us
  Pallas kernels: 12.7 us -> 13.5 us
  local copies, waits for them, and re-layouts: 1.37 us -> 1.94 us
    ppermute x6 -> x3, waiting for transfers between devices: 12.5 us -> 3.6 us  [to_pair(): return lax.ppermute(x, 'mode', pairs)]
    ppermute x6 -> x3, starting transfers between devices: 13.6 us -> 8.9 us  [to_pair(): return lax.ppermute(x, 'mode', pairs)]
    ppermute x3 -> x4, waiting for transfers between devices: 0.5 us -> 3.78 us  [across(): return lax.ppermute(x, 'mode', [(i, i ^ bit) for i in range(groups)])]
    ppermute x3 -> x4, starting transfers between devices: 7.2 us -> 8.66 us  [across(): return lax.ppermute(x, 'mode', [(i, i ^ bit) for i in range(groups)])]
    cond x0 -> x8, local copies, waits for them, and re-layouts: none -> 1.28 us
    ppermute x2, waiting for transfers between devices: 0.01 us -> 1.04 us  [to_tile(): lax.ppermute(x, 'tile', [(i, i + step) for i in range(tiles) if 0 <= i +...]
    select_n x1, other arithmetic: 0.02 us -> 0.93 us  [choose(): return jnp.where(jnp.bitwise_and(away, bit) == 0, x, y)]
    slice x1 -> x0, local copies, waits for them, and re-layouts: 0.71 us -> none  [body(): edges[6:]]
  transfers between devices with their start and end apart: 11 -> 9, of which waited for: 3 -> 4; matrix products, arithmetic and copies ran while one was open for 2% -> 2% of each run, Pallas kernels for 3% -> 8%
where the time goes in v2:
time: 47.8 us; the launch traced here: 47.5 us
  starting transfers between devices  21.9 us (46%)
  Pallas kernels  13.5 us (28%)
  waiting for transfers between devices  8.42 us (18%)
  local copies, waits for them, and re-layouts  1.94 us (4%)
  other arithmetic  1.01 us (2%)
  between operations  0.73 us (2%)
    pallas_call x1, Pallas kernels, body(): pl.pallas_call(functools.partial(steps_kernel, modes, tiles), out_shape=s...  9.62 us
    ppermute x3, starting transfers between devices, to_pair(): return lax.ppermute(x, 'mode', pairs)  8.9 us
    ppermute x4, starting transfers between devices, across(): return lax.ppermute(x, 'mode', [(i, i ^ bit) for i in range(groups)])  8.66 us
    ppermute x2, starting transfers between devices, to_tile(): lax.ppermute(x, 'tile', [(i, i + step) for i in range(tiles) if 0 <= i +...  4.31 us
    ppermute x4, waiting for transfers between devices, across(): return lax.ppermute(x, 'mode', [(i, i ^ bit) for i in range(groups)])  3.78 us
    ppermute x3, waiting for transfers between devices, to_pair(): return lax.ppermute(x, 'mode', pairs)  3.6 us
    pallas_call x1, Pallas kernels, small_exchanges(): small_kernel(join_kernel, 'join', shape(408, 128), [SMEM] + [VMEM] * 5)  1.63 us
    pallas_call x1, Pallas kernels, small_exchanges(): small_kernel(strips_kernel, 'strips', (shape(2, 6, 8, 128), shape(3, 8, 1...  1.44 us
  transfers between devices with their start and end apart: 9, of which 4 were waited for; matrix products, arithmetic and copies ran while one was open for 2% of the time, Pallas kernels for 8%

profile of v2, /device:TPU:0, one launch (start us, length us, event | category | flops | bytes accessed | tf_op | source)
XLA Modules:
  0.0 47.5 jit_solution(2132986398732285600)
XLA Ops:
  0.0 0.0 copy-start
  0.0 3.0 %collective-permute-start.6 = (f32[1,9,32,128]{3,2,1,0:T(8,128)}, f32[1,9,32,128]{3,2,1,0:T(8,128)S(1)}, u32[]{:S(2)}, u32[]{:S(2)}) collective-permute-start(f32[1,9,32,128]{3,2,1,0:T(8,128)} %param.7), channel_id=1, source_target_pairs={{0,8},{4,12},{8,0},{12,4},{16,24},{20,28},{24,16},{28,20},{1,9},{5... | collective-permute-start | bytes 442376 | tf_op jit(solution)/shard_map/ppermute | solution.py:302
  3.0 1.5 %collective-permute-start.7 = (f32[4,6,32,128]{3,2,1,0:T(8,128)}, f32[4,6,32,128]{3,2,1,0:T(8,128)S(1)}, u32[]{:S(2)}, u32[]{:S(2)}) collective-permute-start(f32[4,6,32,128]{3,2,1,0:T(8,128)} %own_hbm.1), channel_id=1, source_target_pairs={{0,4},{4,0},{8,12},{12,8},{16,20},{20,16},{24,28},{28,24},{1,5},{5... | collective-permute-start | bytes 1179656 | tf_op jit(solution)/shard_map/ppermute | solution.py:299
  5.2 1.9 %collective-permute-done.6 = f32[1,9,32,128]{3,2,1,0:T(8,128)S(1)} collective-permute-done((f32[1,9,32,128]{3,2,1,0:T(8,128)}, f32[1,9,32,128]{3,2,1,0:T(8,128)S(1)}, u32[]{:S(2)}, u32[]{:S(2)}) %collective-permute-start.6) | collective-permute-done | bytes 147488 | tf_op jit(solution)/shard_map/ppermute | solution.py:302
  7.1 0.9 %broadcast_select_fusion = f32[1,9,32,128]{3,2,1,0:T(8,128)S(1)} fusion(f32[1,9,32,128]{3,2,1,0:T(8,128)} %param.7, f32[1,9,32,128]{3,2,1,0:T(8,128)S(1)} %collective-permute-done.6, pred[]{:T(512)S(6)} %eq.3), kind=kLoop, calls=%fused_computation | loop fusion | flops 36864 | bytes 442369 | tf_op jit(solution)/shard_map/jit(_where)/select_n | solution.py:312
  8.0 0.0 copy-done
  8.0 3.9 %collective-permute-start.8 = (f32[4,6,32,128]{3,2,1,0:T(8,128)S(1)}, f32[4,6,32,128]{3,2,1,0:T(8,128)S(1)}, u32[]{:S(2)}, u32[]{:S(2)}) collective-permute-start(f32[4,6,32,128]{3,2,1,0:T(8,128)S(1)} %copy-done), channel_id=1, source_target_pairs={{4,8},{8,4},{12,16},{16,12},{20,24},{24,20},{28,0},{0,28},{5,9},{9... | collective-permute-start | bytes 1179656 | tf_op jit(solution)/shard_map/ppermute | solution.py:299
  11.9 0.0 copy-start.5
  11.9 0.7 %copy-done.5 = s32[4]{0:T(128)S(1)} copy-done((s32[4]{0:T(128)S(1)}, s32[4]{0:T(128)}, u32[]{:S(2)}) %copy-start.5) | copy-done | bytes 40
  12.6 0.1 pad_add_fusion.info_ref
  12.7 25.2 %conditional.1 = (f32[408,128]{1,0:T(8,128)}, f32[408,128]{1,0:T(8,128)}, f32[2,6,8,128]{3,2,1,0:T(8,128)}, f32[2,6,8,128]{3,2,1,0:T(8,128)}) conditional(s32[]{:T(128)} %convert_element_type.3, () %tuple.14, (s32[]{:T(128)}, f32[1,9,32,128]{3,2,1,0:T(8,128)S(1)}, f32[4,6,32,128]{3,2,1,0:T(8,128)S(1)}) %tuple.19), branch_computations={%region_0.1_spmd, %region_1.2_spmd} | conditional | flops 25 | bytes 2900388 | solution.py:338
  12.7 0.0 collective-permute-start
  12.7 0.8 %pack_edges.1.edges_ref = f32[9,8,128]{2,1,0:T(8,128)} custom-call(f32[4,6,32,128]{3,2,1,0:T(8,128)S(1)} %get-tuple-element.13.field_ref, f32[1,9,32,128]{3,2,1,0:T(8,128)S(1)} %get-tuple-element.12.flow_ref), custom_call_target="tpu_custom_call" | custom-call | flops 8 | bytes 8 | tf_op jit(solution)/shard_map/cond/branch_1_fun/pack_edges/pallas_call | solution.py:323
  13.6 1.3 %collective-permute-start.2 = (f32[9,8,128]{2,1,0:T(8,128)}, f32[9,8,128]{2,1,0:T(8,128)S(1)}, u32[]{:S(2)}, u32[]{:S(2)}) collective-permute-start(f32[9,8,128]{2,1,0:T(8,128)} %pack_edges.1.edges_ref), channel_id=1, source_target_pairs={{1,0},{2,1},{3,2},{5,4},{6,5},{7,6},{9,8},{10,9},{11,10},{13,12},{... | collective-permute-start | bytes 110600 | tf_op jit(solution)/shard_map/cond/branch_1_fun/ppermute | solution.py:305
  14.9 3.0 %collective-permute-start.1 = (f32[9,8,128]{2,1,0:T(8,128)}, f32[9,8,128]{2,1,0:T(8,128)S(1)}, u32[]{:S(2)}, u32[]{:S(2)}) collective-permute-start(f32[9,8,128]{2,1,0:T(8,128)} %pack_edges.1.edges_ref), channel_id=1, source_target_pairs={{0,1},{1,2},{2,3},{4,5},{5,6},{6,7},{8,9},{9,10},{10,11},{12,13},{... | collective-permute-start | bytes 110600 | tf_op jit(solution)/shard_map/cond/branch_1_fun/ppermute | solution.py:305
  17.9 0.0 collective-permute-done.2.right_ref
  17.9 0.0 copy-start.2
  17.9 1.0 %collective-permute-done.1.left_ref = f32[9,8,128]{2,1,0:T(8,128)S(1)} collective-permute-done((f32[9,8,128]{2,1,0:T(8,128)}, f32[9,8,128]{2,1,0:T(8,128)S(1)}, u32[]{:S(2)}, u32[]{:S(2)}) %collective-permute-start.1) | collective-permute-done | bytes 36896 | tf_op jit(solution)/shard_map/cond/branch_1_fun/ppermute | solution.py:305
  18.9 0.0 copy-done.2
  19.0 0.0 copy-start.3
  19.0 0.6 %copy-done.3 = f32[9,8,128]{2,1,0:T(8,128)} copy-done((f32[9,8,128]{2,1,0:T(8,128)}, f32[9,8,128]{2,1,0:T(8,128)S(1)}, u32[]{:S(2)}) %copy-start.3) | copy-done | bytes 36888 | tf_op jit(solution)/shard_map/cond
  19.6 1.4 %strips.1 = (f32[2,6,8,128]{3,2,1,0:T(8,128)}, f32[3,8,128]{2,1,0:T(8,128)}) custom-call(f32[9,8,128]{2,1,0:T(8,128)} %pack_edges.1.edges_ref, f32[9,8,128]{2,1,0:T(8,128)} %copy-done.3, f32[9,8,128]{2,1,0:T(8,128)} %copy-done.2), custom_call_target="tpu_custom_call" | custom-call | flops 8 | bytes 8 | tf_op jit(solution)/shard_map/cond/branch_1_fun/strips/pallas_call | solution.py:324
  21.0 2.9 %collective-permute-start.3 = (f32[3,8,128]{2,1,0:T(8,128)}, f32[3,8,128]{2,1,0:T(8,128)S(1)}, u32[]{:S(2)}, u32[]{:S(2)}) collective-permute-start(f32[3,8,128]{2,1,0:T(8,128)} %get-tuple-element.14.halo_ref), channel_id=1, source_target_pairs={{0,16},{4,20},{8,24},{12,28},{16,0},{20,4},{24,8},{28,12},{1,17},{... | collective-permute-start | bytes 36872 | tf_op jit(solution)/shard_map/cond/branch_1_fun/ppermute | solution.py:302
  23.9 1.9 %collective-permute-done.3.halo2_ref = f32[3,8,128]{2,1,0:T(8,128)S(1)} collective-permute-done((f32[3,8,128]{2,1,0:T(8,128)}, f32[3,8,128]{2,1,0:T(8,128)S(1)}, u32[]{:S(2)}, u32[]{:S(2)}) %collective-permute-start.3) | collective-permute-done | bytes 12320 | tf_op jit(solution)/shard_map/cond/branch_1_fun/ppermute | solution.py:302
  25.8 0.0 copy-start.4
  25.8 0.0 collective-permute-done.flow2_ref
  25.8 0.0 copy-start.1
  25.8 0.6 %copy-done.4 = f32[3,8,128]{2,1,0:T(8,128)} copy-done((f32[3,8,128]{2,1,0:T(8,128)}, f32[3,8,128]{2,1,0:T(8,128)S(1)}, u32[]{:S(2)}) %copy-start.4) | copy-done | bytes 12312 | tf_op jit(solution)/shard_map/cond
  26.4 0.1 copy-done.1
  26.5 1.6 %join.1 = f32[408,128]{1,0:T(8,128)} custom-call(s32[1]{0:T(128)} %bitcast.pick_ref, f32[1,9,32,128]{3,2,1,0:T(8,128)S(1)} %get-tuple-element.12.flow_ref, f32[1,9,32,128]{3,2,1,0:T(8,128)} %copy-done.1, f32[3,8,128]{2,1,0:T(8,128)} %get-tuple-element.14.halo_ref, f32[3,8,128]{2,1,0:T(8,128)} %copy-done.4, f32[2,6,8,128]{3,2,1,0:T(8,128)} %get-tuple-element.34.strips_ref), custom_call_target="tpu_custom_call" | custom-call | flops 8 | bytes 8 | tf_op jit(solution)/shard_map/cond/branch_1_fun/join/pallas_call | solution.py:329
  28.1 2.7 %collective-permute-start.4 = (f32[408,128]{1,0:T(8,128)}, f32[408,128]{1,0:T(8,128)}, u32[]{:S(2)}, u32[]{:S(2)}) collective-permute-start(f32[408,128]{1,0:T(8,128)} %join.1), channel_id=1, source_target_pairs={{0,4},{4,0},{8,12},{12,8},{16,20},{20,16},{24,28},{28,24},{1,5},{5... | collective-permute-start | bytes 626696 | tf_op jit(solution)/shard_map/cond/branch_1_fun/ppermute | solution.py:302
  30.8 3.5 %collective-permute-start.5 = (f32[2,6,8,128]{3,2,1,0:T(8,128)}, f32[2,6,8,128]{3,2,1,0:T(8,128)}, u32[]{:S(2)}, u32[]{:S(2)}) collective-permute-start(f32[2,6,8,128]{3,2,1,0:T(8,128)} %get-tuple-element.34.strips_ref), channel_id=1, source_target_pairs={{4,8},{8,4},{12,16},{16,12},{20,24},{24,20},{28,0},{0,28},{5,9},{9... | collective-permute-start | bytes 147464 | tf_op jit(solution)/shard_map/cond/branch_1_fun/ppermute | solution.py:299
  34.3 3.6 %collective-permute-done.5 = f32[2,6,8,128]{3,2,1,0:T(8,128)} collective-permute-done((f32[2,6,8,128]{3,2,1,0:T(8,128)}, f32[2,6,8,128]{3,2,1,0:T(8,128)}, u32[]{:S(2)}, u32[]{:S(2)}) %collective-permute-start.5) | collective-permute-done | bytes 49184 | tf_op jit(solution)/shard_map/cond/branch_1_fun/ppermute | solution.py:299
  37.9 0.0 collective-permute-done.4
  37.9 0.0 collective-permute-done.7.pair_hbm
  37.9 0.0 collective-permute-done.8.other_hbm
  37.9 9.6 %heun_steps.1 = f32[4,6,32,128]{3,2,1,0:T(8,128)} custom-call(s32[4]{0:T(128)S(1)} %pad_add_fusion.info_ref, f32[408,128]{1,0:T(8,128)} %get-tuple-element.23.message_ref, f32[408,128]{1,0:T(8,128)} %get-tuple-element.24.message2_ref, f32[2,6,8,128]{3,2,1,0:T(8,128)} %get-tuple-element.25.strips_own, f32[2,6,8,128]{3,2,1,0:T(8,128)} %get-tuple-element.26.strips_other, ...), custom_call_target="tpu_custom_call" | custom-call | tf_op jit(solution)/shard_map/heun_steps/pallas_call | solution.py:347
Async XLA Ops:
  0.0 8.0 %copy-start = (f32[4,6,32,128]{3,2,1,0:T(8,128)S(1)}, f32[4,6,32,128]{3,2,1,0:T(8,128)}, u32[]{:S(2)}) copy-start(f32[4,6,32,128]{3,2,1,0:T(8,128)} %own_hbm.1) | copy-start | bytes 1179652
  0.0 7.1 %collective-permute-start.6 = (f32[1,9,32,128]{3,2,1,0:T(8,128)}, f32[1,9,32,128]{3,2,1,0:T(8,128)S(1)}, u32[]{:S(2)}, u32[]{:S(2)}) collective-permute-start(f32[1,9,32,128]{3,2,1,0:T(8,128)} %param.7), channel_id=1, source_target_pairs={{0,8},{4,12},{8,0},{12,4},{16,24},{20,28},{24,16},{28,20},{1,9},{5... | collective-permute-start | bytes 442376 | tf_op jit(solution)/shard_map/ppermute | solution.py:302
  3.0 34.9 %collective-permute-start.7 = (f32[4,6,32,128]{3,2,1,0:T(8,128)}, f32[4,6,32,128]{3,2,1,0:T(8,128)S(1)}, u32[]{:S(2)}, u32[]{:S(2)}) collective-permute-start(f32[4,6,32,128]{3,2,1,0:T(8,128)} %own_hbm.1), channel_id=1, source_target_pairs={{0,4},{4,0},{8,12},{12,8},{16,20},{20,16},{24,28},{28,24},{1,5},{5... | collective-permute-start | bytes 1179656 | tf_op jit(solution)/shard_map/ppermute | solution.py:299
  8.0 29.9 %collective-permute-start.8 = (f32[4,6,32,128]{3,2,1,0:T(8,128)S(1)}, f32[4,6,32,128]{3,2,1,0:T(8,128)S(1)}, u32[]{:S(2)}, u32[]{:S(2)}) collective-permute-start(f32[4,6,32,128]{3,2,1,0:T(8,128)S(1)} %copy-done), channel_id=1, source_target_pairs={{4,8},{8,4},{12,16},{16,12},{20,24},{24,20},{28,0},{0,28},{5,9},{9... | collective-permute-start | bytes 1179656 | tf_op jit(solution)/shard_map/ppermute | solution.py:299
  11.9 0.7 %copy-start.5 = (s32[4]{0:T(128)S(1)}, s32[4]{0:T(128)}, u32[]{:S(2)}) copy-start(s32[4]{0:T(128)} %param.8) | copy-start | bytes 52
  12.7 13.1 %collective-permute-start = (f32[1,9,32,128]{3,2,1,0:T(8,128)S(1)}, f32[1,9,32,128]{3,2,1,0:T(8,128)S(1)}, u32[]{:S(2)}, u32[]{:S(2)}) collective-permute-start(f32[1,9,32,128]{3,2,1,0:T(8,128)S(1)} %get-tuple-element.12.flow_ref), channel_id=1, source_target_pairs={{0,16},{4,20},{8,24},{12,28},{16,0},{20,4},{24,8},{28,12},{1,17},{... | collective-permute-start | bytes 442376 | tf_op jit(solution)/shard_map/cond/branch_1_fun/ppermute | solution.py:302
  13.6 4.3 %collective-permute-start.2 = (f32[9,8,128]{2,1,0:T(8,128)}, f32[9,8,128]{2,1,0:T(8,128)S(1)}, u32[]{:S(2)}, u32[]{:S(2)}) collective-permute-start(f32[9,8,128]{2,1,0:T(8,128)} %pack_edges.1.edges_ref), channel_id=1, source_target_pairs={{1,0},{2,1},{3,2},{5,4},{6,5},{7,6},{9,8},{10,9},{11,10},{13,12},{... | collective-permute-start | bytes 110600 | tf_op jit(solution)/shard_map/cond/branch_1_fun/ppermute | solution.py:305
  14.9 4.1 %collective-permute-start.1 = (f32[9,8,128]{2,1,0:T(8,128)}, f32[9,8,128]{2,1,0:T(8,128)S(1)}, u32[]{:S(2)}, u32[]{:S(2)}) collective-permute-start(f32[9,8,128]{2,1,0:T(8,128)} %pack_edges.1.edges_ref), channel_id=1, source_target_pairs={{0,1},{1,2},{2,3},{4,5},{5,6},{6,7},{8,9},{9,10},{10,11},{12,13},{... | collective-permute-start | bytes 110600 | tf_op jit(solution)/shard_map/cond/branch_1_fun/ppermute | solution.py:305
  17.9 1.0 %copy-start.2 = (f32[9,8,128]{2,1,0:T(8,128)}, f32[9,8,128]{2,1,0:T(8,128)S(1)}, u32[]{:S(2)}) copy-start(f32[9,8,128]{2,1,0:T(8,128)S(1)} %collective-permute-done.2.right_ref) | copy-start | bytes 110596 | tf_op jit(solution)/shard_map/cond
  19.0 0.6 %copy-start.3 = (f32[9,8,128]{2,1,0:T(8,128)}, f32[9,8,128]{2,1,0:T(8,128)S(1)}, u32[]{:S(2)}) copy-start(f32[9,8,128]{2,1,0:T(8,128)S(1)} %collective-permute-done.1.left_ref) | copy-start | bytes 110596 | tf_op jit(solution)/shard_map/cond
  21.0 4.8 %collective-permute-start.3 = (f32[3,8,128]{2,1,0:T(8,128)}, f32[3,8,128]{2,1,0:T(8,128)S(1)}, u32[]{:S(2)}, u32[]{:S(2)}) collective-permute-start(f32[3,8,128]{2,1,0:T(8,128)} %get-tuple-element.14.halo_ref), channel_id=1, source_target_pairs={{0,16},{4,20},{8,24},{12,28},{16,0},{20,4},{24,8},{28,12},{1,17},{... | collective-permute-start | bytes 36872 | tf_op jit(solution)/shard_map/cond/branch_1_fun/ppermute | solution.py:302
  25.8 0.6 %copy-start.4 = (f32[3,8,128]{2,1,0:T(8,128)}, f32[3,8,128]{2,1,0:T(8,128)S(1)}, u32[]{:S(2)}) copy-start(f32[3,8,128]{2,1,0:T(8,128)S(1)} %collective-permute-done.3.halo2_ref) | copy-start | bytes 36868 | tf_op jit(solution)/shard_map/cond
  25.8 0.7 %copy-start.1 = (f32[1,9,32,128]{3,2,1,0:T(8,128)}, f32[1,9,32,128]{3,2,1,0:T(8,128)S(1)}, u32[]{:S(2)}) copy-start(f32[1,9,32,128]{3,2,1,0:T(8,128)S(1)} %collective-permute-done.flow2_ref) | copy-start | bytes 442372 | tf_op jit(solution)/shard_map/cond
  28.1 9.8 %collective-permute-start.4 = (f32[408,128]{1,0:T(8,128)}, f32[408,128]{1,0:T(8,128)}, u32[]{:S(2)}, u32[]{:S(2)}) collective-permute-start(f32[408,128]{1,0:T(8,128)} %join.1), channel_id=1, source_target_pairs={{0,4},{4,0},{8,12},{12,8},{16,20},{20,16},{24,28},{28,24},{1,5},{5... | collective-permute-start | bytes 626696 | tf_op jit(solution)/shard_map/cond/branch_1_fun/ppermute | solution.py:302
  30.8 7.1 %collective-permute-start.5 = (f32[2,6,8,128]{3,2,1,0:T(8,128)}, f32[2,6,8,128]{3,2,1,0:T(8,128)}, u32[]{:S(2)}, u32[]{:S(2)}) collective-permute-start(f32[2,6,8,128]{3,2,1,0:T(8,128)} %get-tuple-element.34.strips_ref), channel_id=1, source_target_pairs={{4,8},{8,4},{12,16},{16,12},{20,24},{24,20},{28,0},{0,28},{5,9},{9... | collective-permute-start | bytes 147464 | tf_op jit(solution)/shard_map/cond/branch_1_fun/ppermute | solution.py:299

commit v3 on v2

v3 whole, which is shorter than its diff:
```python
import functools

import jax
import jax.numpy as jnp
from jax import lax
from jax.experimental import pallas as pl
from jax.experimental.pallas import tpu as pltpu
from jax.sharding import PartitionSpec as P

inner_radius = 32.0
f32 = jnp.float32
GROUP = 4
EDGE = 8
SLOTS = 3 * GROUP


def lane_index(rows=8):
    return lax.broadcasted_iota(jnp.int32, (rows, 128), 1)


def turn(x, shift, axis=1):
    if isinstance(shift, int):
        shift %= x.shape[axis]
        if shift == 0:
            return x
    return pltpu.roll(x, shift, axis)


def pack_kernel(field_ref, flow_ref, edges_ref):
    lane = lane_index()
    for comp in range(6):
        total = jnp.zeros((8, 128), f32)
        for zt in range(4):
            for mode in range(GROUP):
                at = 32 * zt + 8 * mode
                piece = turn(field_ref[mode, comp, 8 * zt : 8 * zt + 8, :], at + 4)
                total = jnp.where((lane >= at) & (lane < at + 8), piece, total)
        edges_ref[comp] = total
    for block in range(3):
        total = jnp.zeros((8, 128), f32)
        for part in range(4):
            row = 4 * block + part
            if row < 9:
                for zt in range(4):
                    at = 32 * part + 8 * zt
                    piece = turn(flow_ref[0, row, 8 * zt : 8 * zt + 8, :], at + 4)
                    total = jnp.where((lane >= at) & (lane < at + 8), piece, total)
        edges_ref[6 + block] = total


def strips_kernel(place_ref, edges_ref, near_ref, far_ref, strips_ref, halo_ref):
    low = lane_index() % 8 < 4
    odd = place_ref[0] % 2 == 1
    for row in range(9):
        left = jnp.where(odd, near_ref[row], far_ref[row])
        right = jnp.where(odd, far_ref[row], near_ref[row])
        if row < 6:
            strips_ref[0, row] = jnp.where(low, left, edges_ref[row])
            strips_ref[1, row] = jnp.where(low, edges_ref[row], right)
        else:
            halo_ref[row - 6] = jnp.where(low, left, right)


def join_kernel(pick_ref, halo_ref, halo2_ref, strips_ref, message_ref):
    other = pick_ref[0] != 0
    for block in range(3):
        message_ref[block] = jnp.where(other, halo2_ref[block], halo_ref[block])
    for side in range(2):
        for comp in range(6):
            message_ref[3 + 6 * side + comp] = strips_ref[side, comp]


def emf_of(flow, centre, total, gap):
    steady = flow[0:3]
    swirl_re = (flow[3], flow[5], flow[7])
    swirl_im = (flow[4], flow[6], flow[8])
    out = []
    for comp in range(3):
        i, j = (comp + 1) % 3, (comp + 2) % 3
        real = (
            (steady[i] * centre[2 * j] - steady[j] * centre[2 * i])
            + (swirl_re[i] * total[2 * j] - swirl_re[j] * total[2 * i])
            - (swirl_im[i] * gap[2 * j + 1] - swirl_im[j] * gap[2 * i + 1])
        )
        imag = (
            (steady[i] * centre[2 * j + 1] - steady[j] * centre[2 * i + 1])
            + (swirl_re[i] * total[2 * j + 1] - swirl_re[j] * total[2 * i + 1])
            + (swirl_im[i] * gap[2 * j] - swirl_im[j] * gap[2 * i])
        )
        out += [real, imag]
    return out


def coefficients(radius):
    inner, outer = radius - 1.0, radius + 1.0
    return dict(
        up=1.0 + 0.5 / inner, down=1.0 - 0.5 / outer, flux_up=radius / inner, flux_down=radius / outer,
        inv=1.0 / radius, inv2=1.0 / (radius * radius),
    )


def with_waves(coef, waves):
    return dict(
        coef, waves=waves, decay=6.0 - (waves * waves + 1.0) * coef["inv2"], axial=6.0 - (waves * waves) * coef["inv2"],
        coupling=(2.0 * waves) * coef["inv2"], over=(2.0 * waves) * coef["inv"],
    )


def stencil(field, emf, coef):
    up, down, decay, axial, coupling, over = (coef[n] for n in ("up", "down", "decay", "axial", "coupling", "over"))
    right = [field[i] * up for i in range(6)]
    left = [field[i] * down for i in range(6)]
    place = [field[i] * (decay if i < 4 else axial) for i in range(6)]
    for part in range(2):
        right[2 + part] = right[2 + part] - emf[4 + part]
        left[2 + part] = left[2 + part] + emf[4 + part]
        right[4 + part] = right[4 + part] + emf[2 + part] * coef["flux_up"]
        left[4 + part] = left[4 + part] - emf[2 + part] * coef["flux_down"]
    place[0] = place[0] + (coupling * field[3] - over * emf[5])
    place[1] = place[1] - (coupling * field[2] - over * emf[4])
    place[2] = place[2] - coupling * field[1]
    place[3] = place[3] + coupling * field[0]
    place[4] = place[4] + over * emf[1]
    place[5] = place[5] - over * emf[0]
    return right, left, place


PAD = 8


def tile_rows(zt, shift=0):
    return pl.ds(PAD + 8 * zt + shift, 8)


def add_rows(total, i, get_field, get_emf):
    total = total + (get_field(i, 1) + get_field(i, -1))
    if i < 2:
        total = total - (get_emf(2 + i, 1) - get_emf(2 + i, -1))
    elif i < 4:
        total = total + (get_emf(i - 2, 1) - get_emf(i - 2, -1))
    return total


def wave_at(base, slot, modes):
    return (lax.rem(base + slot, modes) - modes // 2).astype(f32)


def column_radius(column):
    return inner_radius + 0.5 + column.astype(f32)


def steps_kernel(
    modes, tiles, info_ref, flow_hbm, flow2_hbm, message_hbm, message2_hbm, strips_hbm, own_hbm, pair_hbm, other_hbm, out_hbm,
    state, trial, out, strip, strip_trial, inject, flow, flow_strip, near_message, far_message, other_strips, emfs, emfs_strip, sums, gaps, rights, lefts, sems,
):
    base, tile, take, odd = info_ref[0], info_ref[1], info_ref[2], info_ref[3]

    places = (GROUP, 2 * GROUP * (1 - odd), 2 * GROUP * odd)
    rows = pl.ds(PAD, 32)
    loads = [
        pltpu.make_async_copy(message_hbm, near_message, sems.at[0]),
        pltpu.make_async_copy(message2_hbm, far_message, sems.at[1]),
        pltpu.make_async_copy(strips_hbm, other_strips, sems.at[2]),
    ]
    field_loads = [
        pltpu.make_async_copy(src, state.at[pl.ds(place, GROUP), :, rows], sems.at[4 + i])
        for i, (src, place) in enumerate(zip((own_hbm, pair_hbm, other_hbm), places))
    ]
    for load in loads:
        load.start()

    @pl.when(take == 0)
    def _():
        pltpu.make_async_copy(flow_hbm.at[0], flow, sems.at[3]).start()

    @pl.when(take != 0)
    def _():
        pltpu.make_async_copy(flow2_hbm.at[0], flow, sems.at[3]).start()

    for load in field_loads:
        load.start()

    lane8 = lane_index()
    column8 = lane8 % 8
    zeros = jnp.zeros((8, 128), f32)
    for array in (state, trial):

        def clear(k, carry, array=array):
            for i in range(6):
                array[k, i, 0:PAD, :] = zeros
                array[k, i, PAD + 32 : PAD + 40, :] = zeros
            return carry

        lax.fori_loop(0, SLOTS, clear, 0)
    for array in (strip, strip_trial, emfs_strip, emfs):
        for side in range(2):
            for i in range(array.shape[1]):
                array[side, i, 0:PAD, :] = zeros
                array[side, i, PAD + 32 : PAD + 40, :] = zeros

    first_column = tile * 128
    main_coef = coefficients(column_radius(first_column + lane8))
    strip_coef, strip_inside = [], []
    for side in range(2):
        column = first_column + column8 + (124 if side else -4)
        strip_coef.append(with_waves(coefficients(column_radius(column)), wave_at(base, lane8 // 8, modes)))
        strip_inside.append((column >= 0) & (column < tiles * 128))

    for load in loads:
        load.wait()
    for side in range(2):
        for comp in range(6):
            at = 3 + 6 * side + comp
            own, other, pair = near_message[at], other_strips[side, comp], far_message[at]
            low, high = jnp.where(odd == 1, pair, other), jnp.where(odd == 1, other, pair)
            for zt in range(4):
                value = jnp.where(lane8 < 32, turn(low, -32 * zt), turn(own, 32 - 32 * zt))
                value = jnp.where(lane8 < 64, value, turn(high, 64 - 32 * zt))
                strip[side, comp, tile_rows(zt), :] = jnp.where(lane8 < 96, value, 0.0)

    pltpu.make_async_copy(flow_hbm.at[0], flow, sems.at[3]).wait()
    near = jnp.where(column8 < 4, 124 + column8, column8 - 4)
    for r in range(9):
        halo = jnp.where(take == 0, near_message[r // 4], far_message[r // 4])
        for zt in range(4):
            inside = jnp.take_along_axis(flow[r, 8 * zt : 8 * zt + 8, :], near, axis=1)
            outside = jnp.take_along_axis(halo, 32 * (r % 4) + 8 * zt + column8, axis=1)
            flow_strip[0, r, 8 * zt : 8 * zt + 8, :] = jnp.where(column8 < 4, outside, inside)
            flow_strip[1, r, 8 * zt : 8 * zt + 8, :] = jnp.where(column8 < 4, inside, outside)

    def strips_eval(source, store):
        places = [(side, zt) for side in range(2) for zt in range(4)]
        for side, zt in places:
            at = slice(8 * zt, 8 * zt + 8)
            for i in range(6):
                x = source[side, i, tile_rows(zt), :]
                lower, upper = turn(x, EDGE), turn(x, -EDGE)
                sums[side, i, at], gaps[side, i, at] = lower + upper, lower - upper
        terms = {}
        for side, zt in places:
            at = slice(8 * zt, 8 * zt + 8)
            centre = [source[side, i, tile_rows(zt), :] for i in range(6)]
            velocity = [flow_strip[side, r, at, :] for r in range(9)]
            emf = emf_of(velocity, centre, [sums[side, i, at] for i in range(6)], [gaps[side, i, at] for i in range(6)])
            right, left, terms[side, zt] = stencil(centre, emf, strip_coef[side])
            for i in range(4):
                emfs_strip[side, i, tile_rows(zt), :] = emf[i]
            for i in range(6):
                rights[side, i, at], lefts[side, i, at] = right[i], left[i]
        for side, zt in places:
            at = slice(8 * zt, 8 * zt + 8)
            for i in range(6):
                if store is not None or side:
                    next_column = turn(rights[side, i, at], -1)
                if store is not None or not side:
                    last_column = turn(lefts[side, i, at], 1)
                inject[i, at] = jnp.where(column8 == 3, next_column, inject[i, at]) if side else last_column
                if store is not None:
                    total = add_rows(
                        (next_column + last_column) + terms[side, zt][i], i,
                        lambda c, d: source[side, c, tile_rows(zt, d), :],
                        lambda c, d: emfs_strip[side, c, tile_rows(zt, d), :],
                    )
                    store(side, i, zt, jnp.where(strip_inside[side], total, 0.0))

    def main_eval(source, start, stop, store, after=None):
        def one(k, buffer):
            coef = with_waves(main_coef, wave_at(base, k, modes))
            totals = []
            for zt in range(4):
                centre = [source[k, i, tile_rows(zt), :] for i in range(6)]
                lower = [source[k - 1, i, tile_rows(zt), :] for i in range(6)]
                upper = [source[k + 1, i, tile_rows(zt), :] for i in range(6)]
                total = [lower[i] + upper[i] for i in range(6)]
                gap = [lower[i] - upper[i] for i in range(6)]
                emf = emf_of([flow[r, 8 * zt : 8 * zt + 8, :] for r in range(9)], centre, total, gap)
                for i in range(4):
                    emfs[buffer, i, tile_rows(zt), :] = emf[i]
                right, left, place = stencil(centre, emf, coef)
                total = []
                for i in range(6):
                    edge = pltpu.roll(inject[i, 8 * zt : 8 * zt + 8, :], 124 - EDGE * k, 1)
                    next_column = jnp.where(lane8 == 127, edge, turn(right[i], -1))
                    last_column = jnp.where(lane8 == 0, edge, turn(left[i], 1))
                    total.append((next_column + last_column) + place[i])
                totals.append(total)
            for zt in range(4):
                for i in range(6):
                    total = add_rows(
                        totals[zt][i], i,
                        lambda c, d: source[k, c, tile_rows(zt, d), :],
                        lambda c, d: emfs[buffer, c, tile_rows(zt, d), :],
                    )
                    store(k, i, zt, total)

        def two(n, carry):
            one(start + 2 * n, 0)
            one(start + 2 * n + 1, 1)
            if after is not None:
                after(n)
            return carry

        lax.fori_loop(0, (stop - start) // 2, two, 0)

    def first_main(k, i, zt, total):
        trial[k, i, tile_rows(zt), :] = total

    def second_main(k, i, zt, total):
        state[k, i, tile_rows(zt), :] = 0.5 * state[k, i, tile_rows(zt), :] + 0.005 * total

    def last_main(k, i, zt, total):
        out[k - GROUP, i, 8 * zt : 8 * zt + 8, :] = 0.5 * state[k, i, tile_rows(zt), :] + 0.005 * total

    def first_strip(side, i, zt, total):
        strip_trial[side, i, tile_rows(zt), :] = total

    def second_strip(side, i, zt, total):
        strip[side, i, tile_rows(zt), :] = 0.5 * strip[side, i, tile_rows(zt), :] + 0.005 * total

    strips_eval(strip, first_strip)
    for load in field_loads:
        load.wait()
    main_eval(state, 1, 11, first_main)
    strips_eval(strip_trial, second_strip)
    main_eval(trial, 2, 10, second_main)
    strips_eval(strip, first_strip)
    main_eval(state, 3, 9, first_main)
    strips_eval(strip_trial, None)
    def writing(n):
        done = pl.ds(2 * n, 2)
        return pltpu.make_async_copy(out.at[done], out_hbm.at[done], sems.at[n])

    main_eval(trial, 4, 8, last_main, lambda n: writing(n).start())
    for n in range(GROUP // 2):
        writing(n).wait()


VMEM = pl.BlockSpec(memory_space=pltpu.VMEM)
SMEM = pl.BlockSpec(memory_space=pltpu.SMEM)
ANY = pl.BlockSpec(memory_space=pl.ANY)


SMALL = pl.CostEstimate(flops=8, bytes_accessed=8, transcendentals=0)


def shape(*dims):
    return jax.ShapeDtypeStruct(dims, f32)


def small_kernel(kernel, name, out, in_specs):
    out_specs = (VMEM,) * len(out) if isinstance(out, tuple) else VMEM
    return pl.pallas_call(kernel, out_shape=out, in_specs=in_specs, out_specs=out_specs, cost_estimate=SMALL, name=name)


def steps_call(kernel):
    return pl.pallas_call(
        kernel,
        out_shape=shape(GROUP, 6, 32, 128),
        in_specs=[SMEM] + [ANY] * 8,
        out_specs=ANY,
        scratch_shapes=[
            pltpu.VMEM((SLOTS, 6, 48, 128), f32),
            pltpu.VMEM((SLOTS, 6, 48, 128), f32),
            pltpu.VMEM((GROUP, 6, 32, 128), f32),
            pltpu.VMEM((2, 6, 48, 128), f32),
            pltpu.VMEM((2, 6, 48, 128), f32),
            pltpu.VMEM((6, 32, 128), f32),
            pltpu.VMEM((9, 32, 128), f32),
            pltpu.VMEM((2, 9, 32, 128), f32),
            pltpu.VMEM((15, 8, 128), f32),
            pltpu.VMEM((15, 8, 128), f32),
            pltpu.VMEM((2, 6, 8, 128), f32),
            pltpu.VMEM((2, 4, 48, 128), f32),
            pltpu.VMEM((2, 4, 48, 128), f32),
            pltpu.VMEM((2, 6, 32, 128), f32),
            pltpu.VMEM((2, 6, 32, 128), f32),
            pltpu.VMEM((2, 6, 32, 128), f32),
            pltpu.VMEM((2, 6, 32, 128), f32),
            pltpu.SemaphoreType.DMA((8,)),
        ],
        compiler_params=pltpu.CompilerParams(vmem_limit_bytes=32 * 1024 * 1024),
        name="heun_steps",
    )


def body(magnetic, velocity_stack, wavenumber, velocity_owner):
    groups, tiles = lax.axis_size("mode"), lax.axis_size("tile")
    me, tile = lax.axis_index("mode"), lax.axis_index("tile")
    modes = groups * GROUP
    away = jnp.bitwise_xor(me, velocity_owner[0])

    def to_pair(x, first):
        pairs = []
        for i in range(first, groups, 2):
            pairs += [(i, (i + 1) % groups), ((i + 1) % groups, i)]
        return lax.ppermute(x, "mode", pairs)

    def across(x, bit):
        return lax.ppermute(x, "mode", [(i, i ^ bit) for i in range(groups)])

    def to_tile(x, first):
        pairs = []
        for i in range(first, tiles - 1, 2):
            pairs += [(i, i + 1), (i + 1, i)]
        return lax.ppermute(x, "tile", pairs)

    bits = []
    while 2 << len(bits) < groups:
        bits.append(2 << len(bits))
    bits.append(1)
    def choose(x, y, bit):
        return jnp.where(jnp.bitwise_and(away, bit) == 0, x, y)

    pair = to_pair(magnetic, 0)
    flow = choose(velocity_stack, across(velocity_stack, bits[0]), bits[0])
    magnetic_later, flow = lax.optimization_barrier((magnetic, flow))
    other = to_pair(magnetic_later, 1)

    def small_exchanges(flow, magnetic):
        for bit in bits[1:-2]:
            flow = choose(flow, across(flow, bit), bit)
        flow2 = across(flow, bits[-2])
        edges = small_kernel(pack_kernel, "pack_edges", shape(9, 8, 128), [VMEM] * 2)(magnetic, flow)
        strips, halo = small_kernel(
            strips_kernel, "strips", (shape(2, 6, 8, 128), shape(3, 8, 128)), [SMEM] + [VMEM] * 3
        )(tile.reshape(1), edges, to_tile(edges, 0), to_tile(edges, 1))
        halo2 = across(halo, bits[-2])
        flow, flow2, halo, halo2 = lax.optimization_barrier((flow, flow2, halo, halo2))
        pick = jnp.bitwise_and(away, bits[-2]).reshape(1)
        message = small_kernel(join_kernel, "join", shape(15, 8, 128), [SMEM] + [VMEM] * 3)(pick, halo, halo2, strips)
        flow = choose(flow, flow2, bits[-2])
        return flow, across(flow, bits[-1]), message, across(message, bits[-1]), to_pair(strips, 1)

    def none(flow, magnetic):
        message, strips = jnp.zeros((15, 8, 128), f32), jnp.zeros((2, 6, 8, 128), f32)
        return flow, flow, message, message, strips

    *flows, strips_other = lax.cond(velocity_owner[0] >= 0, small_exchanges, none, flow, magnetic)
    info = jnp.stack(
        [
            lax.rem(wavenumber[0] + modes // 2 + modes - GROUP, modes),
            tile,
            jnp.bitwise_and(away, bits[-1]),
            jnp.bitwise_and(me, 1),
        ]
    ).astype(jnp.int32)
    return steps_call(functools.partial(steps_kernel, modes, tiles))(info, *flows, strips_other, magnetic, pair, other)


def solution(mesh):
    placed = (P("mode", None, None, "tile"), P("mode", None, None, "tile"), P("mode"), P())
    return jax.shard_map(
        body, mesh=mesh, in_specs=placed, out_specs=P("mode", None, None, "tile"), check_vma=False
    )
```

time: 47.8 us -> 45.6 us (0.954)
  Pallas kernels: 13.5 us -> 10.9 us
  waiting for transfers between devices: 8.42 us -> 9.9 us
  other arithmetic: 1.01 us -> 0.14 us
    pallas_call x2, Pallas kernels: 11.3 us -> 8.63 us  [the longest x1 7.14 us: body(): steps_call(functools.partial(steps_kernel, modes, tiles))]
    ppermute x3, starting transfers between devices: 8.9 us -> 10.2 us  [to_pair(): return lax.ppermute(x, 'mode', pairs)]
    ppermute x4 -> x5, waiting for transfers between devices: 3.78 us -> 4.91 us  [across(): return lax.ppermute(x, 'mode', [(i, i ^ bit) for i in range(groups)])]
    select_n x1 -> x2, other arithmetic: 0.93 us -> 0.06 us  [choose(): return jnp.where(jnp.bitwise_and(away, bit) == 0, x, y)]
    ppermute x2, starting transfers between devices: 4.31 us -> 3.57 us  [to_tile(): return lax.ppermute(x, 'tile', pairs)]
    ppermute x4 -> x5, starting transfers between devices: 8.66 us -> 7.99 us  [across(): return lax.ppermute(x, 'mode', [(i, i ^ bit) for i in range(groups)])]
  transfers between devices with their start and end apart: 9 -> 10, of which waited for: 4 -> 4; matrix products, arithmetic and copies ran while one was open for 2% -> 0% of each run, Pallas kernels for 8% -> 8%
where the time goes in v3:
time: 45.6 us; the launch traced here: 45.3 us
  starting transfers between devices  21.8 us (48%)
  Pallas kernels  10.9 us (24%)
  waiting for transfers between devices  9.9 us (22%)
  local copies, waits for them, and re-layouts  1.81 us (4%)
  between operations  0.74 us (2%)
    ppermute x3, starting transfers between devices, to_pair(): return lax.ppermute(x, 'mode', pairs)  10.2 us
    ppermute x5, starting transfers between devices, across(): return lax.ppermute(x, 'mode', [(i, i ^ bit) for i in range(groups)])  7.99 us
    pallas_call x1, Pallas kernels, body(): steps_call(functools.partial(steps_kernel, modes, tiles))  7.14 us
    ppermute x5, waiting for transfers between devices, across(): return lax.ppermute(x, 'mode', [(i, i ^ bit) for i in range(groups)])  4.91 us
    ppermute x3, waiting for transfers between devices, to_pair(): return lax.ppermute(x, 'mode', pairs)  3.92 us
    ppermute x2, starting transfers between devices, to_tile(): return lax.ppermute(x, 'tile', pairs)  3.57 us
    pallas_call x1, Pallas kernels, small_exchanges(): small_kernel(join_kernel, 'join', shape(15, 8, 128), [SMEM] + [VMEM] * 3)  1.49 us
    pallas_call x1, Pallas kernels, small_exchanges(): small_kernel(strips_kernel, 'strips', (shape(2, 6, 8, 128), shape(3, 8, 1...  1.43 us
  transfers between devices with their start and end apart: 10, of which 4 were waited for; matrix products, arithmetic and copies ran while one was open for 0% of the time, Pallas kernels for 8%

profile of v3, /device:TPU:0, one launch (start us, length us, event | category | flops | bytes accessed | tf_op | source)
XLA Modules:
  0.0 45.3 jit_solution(16633745124841340595)
XLA Ops:
  0.0 0.0 copy-start
  0.0 3.0 %collective-permute-start.7 = (f32[1,9,32,128]{3,2,1,0:T(8,128)}, f32[1,9,32,128]{3,2,1,0:T(8,128)S(1)}, u32[]{:S(2)}, u32[]{:S(2)}) collective-permute-start(f32[1,9,32,128]{3,2,1,0:T(8,128)} %param.7), channel_id=1, source_target_pairs={{0,8},{4,12},{8,0},{12,4},{16,24},{20,28},{24,16},{28,20},{1,9},{5... | collective-permute-start | bytes 442376 | tf_op jit(solution)/shard_map/ppermute | solution.py:399
  3.0 1.5 %collective-permute-start.8 = (f32[4,6,32,128]{3,2,1,0:T(8,128)}, f32[4,6,32,128]{3,2,1,0:T(8,128)S(1)}, u32[]{:S(2)}, u32[]{:S(2)}) collective-permute-start(f32[4,6,32,128]{3,2,1,0:T(8,128)} %own_hbm.1), channel_id=1, source_target_pairs={{0,4},{4,0},{8,12},{12,8},{16,20},{20,16},{24,28},{28,24},{1,5},{5... | collective-permute-start | bytes 1179656 | tf_op jit(solution)/shard_map/ppermute | solution.py:396
  5.2 1.9 %collective-permute-done.7 = f32[1,9,32,128]{3,2,1,0:T(8,128)S(1)} collective-permute-done((f32[1,9,32,128]{3,2,1,0:T(8,128)}, f32[1,9,32,128]{3,2,1,0:T(8,128)S(1)}, u32[]{:S(2)}, u32[]{:S(2)}) %collective-permute-start.7) | collective-permute-done | bytes 147488 | tf_op jit(solution)/shard_map/ppermute | solution.py:399
  7.1 0.0 copy-done
  7.1 5.7 %collective-permute-start.9 = (f32[4,6,32,128]{3,2,1,0:T(8,128)S(1)}, f32[4,6,32,128]{3,2,1,0:T(8,128)S(1)}, u32[]{:S(2)}, u32[]{:S(2)}) collective-permute-start(f32[4,6,32,128]{3,2,1,0:T(8,128)S(1)} %copy-done), channel_id=1, source_target_pairs={{4,8},{8,4},{12,16},{16,12},{20,24},{24,20},{28,0},{0,28},{5,9},{9... | collective-permute-start | bytes 1179656 | tf_op jit(solution)/shard_map/ppermute | solution.py:396
  12.8 0.0 copy-start.5
  12.8 0.7 %copy-done.5 = s32[4]{0:T(128)S(1)} copy-done((s32[4]{0:T(128)S(1)}, s32[4]{0:T(128)}, u32[]{:S(2)}) %copy-start.5) | copy-done | bytes 40
  13.5 0.1 pad_add_fusion.info_ref
  13.6 24.5 %conditional.1 = (f32[1,9,32,128]{3,2,1,0:T(8,128)S(1)}, f32[1,9,32,128]{3,2,1,0:T(8,128)}, f32[15,8,128]{2,1,0:T(8,128)}, f32[15,8,128]{2,1,0:T(8,128)}, f32[2,6,8,128]{3,2,1,0:T(8,128)}) conditional(s32[]{:T(128)} %convert_element_type.3, f32[1,9,32,128]{3,2,1,0:T(8,128)S(1)} %broadcast_select_fusion.1, (s32[]{:T(128)}, ...), branch_computations={%region_0.1_spmd, %region_1.2_spmd} | conditional | flops 36890 | bytes 2949598 | solution.py:438
  13.6 0.0 collective-permute-start
  13.6 0.8 %pack_edges.1.edges_ref = f32[9,8,128]{2,1,0:T(8,128)} custom-call(f32[4,6,32,128]{3,2,1,0:T(8,128)S(1)} %get-tuple-element.17.field_ref, f32[1,9,32,128]{3,2,1,0:T(8,128)S(1)} %get-tuple-element.19.flow_ref), custom_call_target="tpu_custom_call" | custom-call | flops 8 | bytes 8 | tf_op jit(solution)/shard_map/cond/branch_1_fun/pack_edges/pallas_call | solution.py:423
  14.5 0.7 %collective-permute-start.2 = (f32[9,8,128]{2,1,0:T(8,128)}, f32[9,8,128]{2,1,0:T(8,128)S(1)}, u32[]{:S(2)}, u32[]{:S(2)}) collective-permute-start(f32[9,8,128]{2,1,0:T(8,128)} %pack_edges.1.edges_ref), channel_id=1, source_target_pairs={{1,2},{2,1},{5,6},{6,5},{9,10},{10,9},{13,14},{14,13},{17,18},{18,... | collective-permute-start | bytes 110600 | tf_op jit(solution)/shard_map/cond/branch_1_fun/ppermute | solution.py:405
  15.1 2.9 %collective-permute-start.1 = (f32[9,8,128]{2,1,0:T(8,128)}, f32[9,8,128]{2,1,0:T(8,128)S(1)}, u32[]{:S(2)}, u32[]{:S(2)}) collective-permute-start(f32[9,8,128]{2,1,0:T(8,128)} %pack_edges.1.edges_ref), channel_id=1, source_target_pairs={{0,1},{1,0},{2,3},{3,2},{4,5},{5,4},{6,7},{7,6},{8,9},{9,8},{10,11... | collective-permute-start | bytes 110600 | tf_op jit(solution)/shard_map/cond/branch_1_fun/ppermute | solution.py:405
  18.1 0.0 collective-permute-done.2.far_ref
  18.1 0.0 copy-start.2
  18.1 1.1 %collective-permute-done.1.near_ref = f32[9,8,128]{2,1,0:T(8,128)S(1)} collective-permute-done((f32[9,8,128]{2,1,0:T(8,128)}, f32[9,8,128]{2,1,0:T(8,128)S(1)}, u32[]{:S(2)}, u32[]{:S(2)}) %collective-permute-start.1) | collective-permute-done | bytes 36896 | tf_op jit(solution)/shard_map/cond/branch_1_fun/ppermute | solution.py:405
  19.1 0.0 copy-start.3
  19.1 0.0 copy-done.2
  19.1 0.6 %copy-done.3 = f32[9,8,128]{2,1,0:T(8,128)} copy-done((f32[9,8,128]{2,1,0:T(8,128)}, f32[9,8,128]{2,1,0:T(8,128)S(1)}, u32[]{:S(2)}) %copy-start.3) | copy-done | bytes 36888 | tf_op jit(solution)/shard_map/cond
  19.7 1.4 %strips.1 = (f32[2,6,8,128]{3,2,1,0:T(8,128)}, f32[3,8,128]{2,1,0:T(8,128)}) custom-call(s32[1]{0:T(128)} %bitcast.place_ref, f32[9,8,128]{2,1,0:T(8,128)} %pack_edges.1.edges_ref, f32[9,8,128]{2,1,0:T(8,128)} %copy-done.3, f32[9,8,128]{2,1,0:T(8,128)} %copy-done.2), custom_call_target="tpu_custom_call" | custom-call | flops 8 | bytes 8 | tf_op jit(solution)/shard_map/cond/branch_1_fun/strips/pallas_call | solution.py:424
  21.2 2.9 %collective-permute-start.3 = (f32[3,8,128]{2,1,0:T(8,128)}, f32[3,8,128]{2,1,0:T(8,128)S(1)}, u32[]{:S(2)}, u32[]{:S(2)}) collective-permute-start(f32[3,8,128]{2,1,0:T(8,128)} %get-tuple-element.21.halo_ref), channel_id=1, source_target_pairs={{0,16},{4,20},{8,24},{12,28},{16,0},{20,4},{24,8},{28,12},{1,17},{... | collective-permute-start | bytes 36872 | tf_op jit(solution)/shard_map/cond/branch_1_fun/ppermute | solution.py:399
  24.1 3.0 %collective-permute-done.3.halo2_ref = f32[3,8,128]{2,1,0:T(8,128)S(1)} collective-permute-done((f32[3,8,128]{2,1,0:T(8,128)}, f32[3,8,128]{2,1,0:T(8,128)S(1)}, u32[]{:S(2)}, u32[]{:S(2)}) %collective-permute-start.3) | collective-permute-done | bytes 12320 | tf_op jit(solution)/shard_map/cond/branch_1_fun/ppermute | solution.py:399
  27.1 0.0 copy-start.4
  27.1 0.0 collective-permute-done
  27.1 0.5 %copy-done.4 = f32[3,8,128]{2,1,0:T(8,128)} copy-done((f32[3,8,128]{2,1,0:T(8,128)}, f32[3,8,128]{2,1,0:T(8,128)S(1)}, u32[]{:S(2)}) %copy-start.4) | copy-done | bytes 12312 | tf_op jit(solution)/shard_map/cond
  27.7 1.4 %collective-permute-start.4 = (f32[1,9,32,128]{3,2,1,0:T(8,128)S(1)}, f32[1,9,32,128]{3,2,1,0:T(8,128)}, u32[]{:S(2)}, u32[]{:S(2)}) collective-permute-start(f32[1,9,32,128]{3,2,1,0:T(8,128)S(1)} %broadcast_select_fusion), channel_id=1, source_target_pairs={{0,4},{4,0},{8,12},{12,8},{16,20},{20,16},{24,28},{28,24},{1,5},{5... | collective-permute-start | bytes 442376 | tf_op jit(solution)/shard_map/cond/branch_1_fun/ppermute | solution.py:399
  29.1 0.0 copy-start.1
  29.1 1.5 %join.1 = f32[15,8,128]{2,1,0:T(8,128)} custom-call(s32[1]{0:T(128)} %bitcast.1.pick_ref, f32[3,8,128]{2,1,0:T(8,128)} %get-tuple-element.21.halo_ref, f32[3,8,128]{2,1,0:T(8,128)} %copy-done.4, f32[2,6,8,128]{3,2,1,0:T(8,128)} %get-tuple-element.23.strips_ref), custom_call_target="tpu_custom_call" | custom-call | flops 8 | bytes 8 | tf_op jit(solution)/shard_map/cond/branch_1_fun/join/pallas_call | solution.py:430
  30.6 0.7 %collective-permute-start.5 = (f32[15,8,128]{2,1,0:T(8,128)}, f32[15,8,128]{2,1,0:T(8,128)}, u32[]{:S(2)}, u32[]{:S(2)}) collective-permute-start(f32[15,8,128]{2,1,0:T(8,128)} %join.1), channel_id=1, source_target_pairs={{0,4},{4,0},{8,12},{12,8},{16,20},{20,16},{24,28},{28,24},{1,5},{5... | collective-permute-start | bytes 184328 | tf_op jit(solution)/shard_map/cond/branch_1_fun/ppermute | solution.py:399
  31.2 0.0 copy-done.1
  31.2 3.0 %collective-permute-start.6 = (f32[2,6,8,128]{3,2,1,0:T(8,128)S(1)}, f32[2,6,8,128]{3,2,1,0:T(8,128)}, u32[]{:S(2)}, u32[]{:S(2)}) collective-permute-start(f32[2,6,8,128]{3,2,1,0:T(8,128)S(1)} %copy-done.1), channel_id=1, source_target_pairs={{4,8},{8,4},{12,16},{16,12},{20,24},{24,20},{28,0},{0,28},{5,9},{9... | collective-permute-start | bytes 147464 | tf_op jit(solution)/shard_map/cond/branch_1_fun/ppermute | solution.py:396
  34.2 3.9 %collective-permute-done.6 = f32[2,6,8,128]{3,2,1,0:T(8,128)} collective-permute-done((f32[2,6,8,128]{3,2,1,0:T(8,128)S(1)}, f32[2,6,8,128]{3,2,1,0:T(8,128)}, u32[]{:S(2)}, u32[]{:S(2)}) %collective-permute-start.6) | collective-permute-done | bytes 49184 | tf_op jit(solution)/shard_map/cond/branch_1_fun/ppermute | solution.py:396
  38.1 0.0 collective-permute-done.5
  38.1 0.0 collective-permute-done.4
  38.1 0.0 collective-permute-done.8.pair_hbm
  38.1 0.0 collective-permute-done.9.other_hbm
  38.1 7.1 %heun_steps.1 = f32[4,6,32,128]{3,2,1,0:T(8,128)} custom-call(s32[4]{0:T(128)S(1)} %pad_add_fusion.info_ref, f32[1,9,32,128]{3,2,1,0:T(8,128)S(1)} %get-tuple-element.32.flow_hbm, f32[1,9,32,128]{3,2,1,0:T(8,128)} %get-tuple-element.33.flow2_hbm, f32[15,8,128]{2,1,0:T(8,128)} %get-tuple-element.34.message_hbm, f32[15,8,128]{2,1,0:T(8,128)} %get-tuple-element.35.message2_hbm, ...), custom_call_target="tpu_custom_call" | custom-call | tf_op jit(solution)/shard_map/heun_steps/pallas_call | solution.py:447
  (2 shorter events, 0.1 us)
Async XLA Ops:
  0.0 7.1 %copy-start = (f32[4,6,32,128]{3,2,1,0:T(8,128)S(1)}, f32[4,6,32,128]{3,2,1,0:T(8,128)}, u32[]{:S(2)}) copy-start(f32[4,6,32,128]{3,2,1,0:T(8,128)} %own_hbm.1) | copy-start | bytes 1179652
  0.0 7.1 %collective-permute-start.7 = (f32[1,9,32,128]{3,2,1,0:T(8,128)}, f32[1,9,32,128]{3,2,1,0:T(8,128)S(1)}, u32[]{:S(2)}, u32[]{:S(2)}) collective-permute-start(f32[1,9,32,128]{3,2,1,0:T(8,128)} %param.7), channel_id=1, source_target_pairs={{0,8},{4,12},{8,0},{12,4},{16,24},{20,28},{24,16},{28,20},{1,9},{5... | collective-permute-start | bytes 442376 | tf_op jit(solution)/shard_map/ppermute | solution.py:399
  3.0 35.1 %collective-permute-start.8 = (f32[4,6,32,128]{3,2,1,0:T(8,128)}, f32[4,6,32,128]{3,2,1,0:T(8,128)S(1)}, u32[]{:S(2)}, u32[]{:S(2)}) collective-permute-start(f32[4,6,32,128]{3,2,1,0:T(8,128)} %own_hbm.1), channel_id=1, source_target_pairs={{0,4},{4,0},{8,12},{12,8},{16,20},{20,16},{24,28},{28,24},{1,5},{5... | collective-permute-start | bytes 1179656 | tf_op jit(solution)/shard_map/ppermute | solution.py:396
  7.1 31.0 %collective-permute-start.9 = (f32[4,6,32,128]{3,2,1,0:T(8,128)S(1)}, f32[4,6,32,128]{3,2,1,0:T(8,128)S(1)}, u32[]{:S(2)}, u32[]{:S(2)}) collective-permute-start(f32[4,6,32,128]{3,2,1,0:T(8,128)S(1)} %copy-done), channel_id=1, source_target_pairs={{4,8},{8,4},{12,16},{16,12},{20,24},{24,20},{28,0},{0,28},{5,9},{9... | collective-permute-start | bytes 1179656 | tf_op jit(solution)/shard_map/ppermute | solution.py:396
  12.8 0.7 %copy-start.5 = (s32[4]{0:T(128)S(1)}, s32[4]{0:T(128)}, u32[]{:S(2)}) copy-start(s32[4]{0:T(128)} %param.8) | copy-start | bytes 52
  13.6 13.5 %collective-permute-start = (f32[1,9,32,128]{3,2,1,0:T(8,128)S(1)}, f32[1,9,32,128]{3,2,1,0:T(8,128)S(1)}, u32[]{:S(2)}, u32[]{:S(2)}) collective-permute-start(f32[1,9,32,128]{3,2,1,0:T(8,128)S(1)} %get-tuple-element.19.flow_ref), channel_id=1, source_target_pairs={{0,16},{4,20},{8,24},{12,28},{16,0},{20,4},{24,8},{28,12},{1,17},{... | collective-permute-start | bytes 442376 | tf_op jit(solution)/shard_map/cond/branch_1_fun/ppermute | solution.py:399
  14.5 3.6 %collective-permute-start.2 = (f32[9,8,128]{2,1,0:T(8,128)}, f32[9,8,128]{2,1,0:T(8,128)S(1)}, u32[]{:S(2)}, u32[]{:S(2)}) collective-permute-start(f32[9,8,128]{2,1,0:T(8,128)} %pack_edges.1.edges_ref), channel_id=1, source_target_pairs={{1,2},{2,1},{5,6},{6,5},{9,10},{10,9},{13,14},{14,13},{17,18},{18,... | collective-permute-start | bytes 110600 | tf_op jit(solution)/shard_map/cond/branch_1_fun/ppermute | solution.py:405
  15.1 4.0 %collective-permute-start.1 = (f32[9,8,128]{2,1,0:T(8,128)}, f32[9,8,128]{2,1,0:T(8,128)S(1)}, u32[]{:S(2)}, u32[]{:S(2)}) collective-permute-start(f32[9,8,128]{2,1,0:T(8,128)} %pack_edges.1.edges_ref), channel_id=1, source_target_pairs={{0,1},{1,0},{2,3},{3,2},{4,5},{5,4},{6,7},{7,6},{8,9},{9,8},{10,11... | collective-permute-start | bytes 110600 | tf_op jit(solution)/shard_map/cond/branch_1_fun/ppermute | solution.py:405
  18.1 1.1 %copy-start.2 = (f32[9,8,128]{2,1,0:T(8,128)}, f32[9,8,128]{2,1,0:T(8,128)S(1)}, u32[]{:S(2)}) copy-start(f32[9,8,128]{2,1,0:T(8,128)S(1)} %collective-permute-done.2.far_ref) | copy-start | bytes 110596 | tf_op jit(solution)/shard_map/cond
  19.1 0.6 %copy-start.3 = (f32[9,8,128]{2,1,0:T(8,128)}, f32[9,8,128]{2,1,0:T(8,128)S(1)}, u32[]{:S(2)}) copy-start(f32[9,8,128]{2,1,0:T(8,128)S(1)} %collective-permute-done.1.near_ref) | copy-start | bytes 110596 | tf_op jit(solution)/shard_map/cond
  21.2 5.9 %collective-permute-start.3 = (f32[3,8,128]{2,1,0:T(8,128)}, f32[3,8,128]{2,1,0:T(8,128)S(1)}, u32[]{:S(2)}, u32[]{:S(2)}) collective-permute-start(f32[3,8,128]{2,1,0:T(8,128)} %get-tuple-element.21.halo_ref), channel_id=1, source_target_pairs={{0,16},{4,20},{8,24},{12,28},{16,0},{20,4},{24,8},{28,12},{1,17},{... | collective-permute-start | bytes 36872 | tf_op jit(solution)/shard_map/cond/branch_1_fun/ppermute | solution.py:399
  27.1 0.6 %copy-start.4 = (f32[3,8,128]{2,1,0:T(8,128)}, f32[3,8,128]{2,1,0:T(8,128)S(1)}, u32[]{:S(2)}) copy-start(f32[3,8,128]{2,1,0:T(8,128)S(1)} %collective-permute-done.3.halo2_ref) | copy-start | bytes 36868 | tf_op jit(solution)/shard_map/cond
  27.7 10.4 %collective-permute-start.4 = (f32[1,9,32,128]{3,2,1,0:T(8,128)S(1)}, f32[1,9,32,128]{3,2,1,0:T(8,128)}, u32[]{:S(2)}, u32[]{:S(2)}) collective-permute-start(f32[1,9,32,128]{3,2,1,0:T(8,128)S(1)} %broadcast_select_fusion), channel_id=1, source_target_pairs={{0,4},{4,0},{8,12},{12,8},{16,20},{20,16},{24,28},{28,24},{1,5},{5... | collective-permute-start | bytes 442376 | tf_op jit(solution)/shard_map/cond/branch_1_fun/ppermute | solution.py:399
  29.1 2.2 %copy-start.1 = (f32[2,6,8,128]{3,2,1,0:T(8,128)S(1)}, f32[2,6,8,128]{3,2,1,0:T(8,128)}, u32[]{:S(2)}) copy-start(f32[2,6,8,128]{3,2,1,0:T(8,128)} %get-tuple-element.23.strips_ref) | copy-start | bytes 147460 | tf_op jit(solution)/shard_map/cond
  30.6 7.6 %collective-permute-start.5 = (f32[15,8,128]{2,1,0:T(8,128)}, f32[15,8,128]{2,1,0:T(8,128)}, u32[]{:S(2)}, u32[]{:S(2)}) collective-permute-start(f32[15,8,128]{2,1,0:T(8,128)} %join.1), channel_id=1, source_target_pairs={{0,4},{4,0},{8,12},{12,8},{16,20},{20,16},{24,28},{28,24},{1,5},{5... | collective-permute-start | bytes 184328 | tf_op jit(solution)/shard_map/cond/branch_1_fun/ppermute | solution.py:399
  31.2 6.9 %collective-permute-start.6 = (f32[2,6,8,128]{3,2,1,0:T(8,128)S(1)}, f32[2,6,8,128]{3,2,1,0:T(8,128)}, u32[]{:S(2)}, u32[]{:S(2)}) collective-permute-start(f32[2,6,8,128]{3,2,1,0:T(8,128)S(1)} %copy-done.1), channel_id=1, source_target_pairs={{4,8},{8,4},{12,16},{16,12},{20,24},{24,20},{28,0},{0,28},{5,9},{9... | collective-permute-start | bytes 147464 | tf_op jit(solution)/shard_map/cond/branch_1_fun/ppermute | solution.py:396

commit v4 on v3

--- a/solution.py
+++ b/solution.py
@@ -341,15 +341,16 @@
 
 
 SMALL = pl.CostEstimate(flops=8, bytes_accessed=8, transcendentals=0)
+LONG = pl.CostEstimate(flops=1_000_000_000, bytes_accessed=100_000_000, transcendentals=0)
 
 
 def shape(*dims):
     return jax.ShapeDtypeStruct(dims, f32)
 
 
-def small_kernel(kernel, name, out, in_specs):
+def small_kernel(kernel, name, out, in_specs, cost=SMALL):
     out_specs = (VMEM,) * len(out) if isinstance(out, tuple) else VMEM
-    return pl.pallas_call(kernel, out_shape=out, in_specs=in_specs, out_specs=out_specs, cost_estimate=SMALL, name=name)
+    return pl.pallas_call(kernel, out_shape=out, in_specs=in_specs, out_specs=out_specs, cost_estimate=cost, name=name)
 
 
 def steps_call(kernel):
@@ -413,29 +414,31 @@
 
     pair = to_pair(magnetic, 0)
     flow = choose(velocity_stack, across(velocity_stack, bits[0]), bits[0])
-    magnetic_later, flow = lax.optimization_barrier((magnetic, flow))
-    other = to_pair(magnetic_later, 1)
-
-    def small_exchanges(flow, magnetic):
+    other = to_pair(magnetic, 1)
+    edges = small_kernel(pack_kernel, "pack_edges", shape(9, 8, 128), [VMEM] * 2, LONG)(magnetic, flow)
+
+    def small_exchanges(flow, edges):
         for bit in bits[1:-2]:
             flow = choose(flow, across(flow, bit), bit)
         flow2 = across(flow, bits[-2])
-        edges = small_kernel(pack_kernel, "pack_edges", shape(9, 8, 128), [VMEM] * 2)(magnetic, flow)
-        strips, halo = small_kernel(
-            strips_kernel, "strips", (shape(2, 6, 8, 128), shape(3, 8, 128)), [SMEM] + [VMEM] * 3
-        )(tile.reshape(1), edges, to_tile(edges, 0), to_tile(edges, 1))
+        near, far = to_tile(edges, 0), to_tile(edges, 1)
+        odd = tile % 2 == 1
+        left, right = jnp.where(odd, near, far), jnp.where(odd, far, near)
+        low = lax.broadcasted_iota(jnp.int32, (9, 8, 128), 2) % 8 < 4
+        halo = jnp.where(low[6:], left[6:], right[6:])
+        strips = jnp.stack([jnp.where(low[:6], left[:6], edges[:6]), jnp.where(low[:6], edges[:6], right[:6])])
         halo2 = across(halo, bits[-2])
-        flow, flow2, halo, halo2 = lax.optimization_barrier((flow, flow2, halo, halo2))
-        pick = jnp.bitwise_and(away, bits[-2]).reshape(1)
-        message = small_kernel(join_kernel, "join", shape(15, 8, 128), [SMEM] + [VMEM] * 3)(pick, halo, halo2, strips)
-        flow = choose(flow, flow2, bits[-2])
-        return flow, across(flow, bits[-1]), message, across(message, bits[-1]), to_pair(strips, 1)
-
-    def none(flow, magnetic):
+        strips_other = to_pair(strips, 1)
+        flow, flow2, halo, halo2, strips_other = lax.optimization_barrier((flow, flow2, halo, halo2, strips_other))
+        flow, halo = choose(flow, flow2, bits[-2]), choose(halo, halo2, bits[-2])
+        message = jnp.concatenate([halo, strips.reshape(12, 8, 128)])
+        return flow, across(flow, bits[-1]), message, across(message, bits[-1]), strips_other
+
+    def none(flow, edges):
         message, strips = jnp.zeros((15, 8, 128), f32), jnp.zeros((2, 6, 8, 128), f32)
         return flow, flow, message, message, strips
 
-    *flows, strips_other = lax.cond(velocity_owner[0] >= 0, small_exchanges, none, flow, magnetic)
+    *flows, strips_other = lax.cond(velocity_owner[0] >= 0, small_exchanges, none, flow, edges)
     info = jnp.stack(
         [
             lax.rem(wavenumber[0] + modes // 2 + modes - GROUP, modes),

time: 45.6 us -> 40.5 us (0.89)
  Pallas kernels: 10.9 us -> 8.34 us
  starting transfers between devices: 21.8 us -> 20.5 us
  waiting for transfers between devices: 9.9 us -> 8.7 us
  other arithmetic: 0.14 us -> 0.81 us
  local copies, waits for them, and re-layouts: 1.81 us -> 1.23 us
    ppermute x3, waiting for transfers between devices: 3.92 us -> 0.01 us  [to_pair(): return lax.ppermute(x, 'mode', pairs)]
    ppermute x5, waiting for transfers between devices: 4.91 us -> 8.69 us  [across(): return lax.ppermute(x, 'mode', [(i, i ^ bit) for i in range(groups)])]
    pallas_call x3 -> x1, Pallas kernels: 3.76 us -> 1.2 us  [body(): small_kernel(pack_kernel, 'pack_edges', shape(9, 8, 128), [VMEM] * 2, LONG)]
    ppermute x3, starting transfers between devices: 10.2 us -> 8.19 us  [to_pair(): return lax.ppermute(x, 'mode', pairs)]
    ppermute x2, waiting for transfers between devices: 1.07 us -> 0.01 us  [to_tile(): return lax.ppermute(x, 'tile', pairs)]
    concatenate x0 -> x1, other arithmetic: none -> 0.62 us  [small_exchanges(): message = jnp.concatenate([halo, strips.reshape(12, 8, 128)])]
    cond x8 -> x4, local copies, waits for them, and re-layouts: 1.16 us -> 0.57 us
    ppermute x5, starting transfers between devices: 7.99 us -> 8.57 us  [across(): return lax.ppermute(x, 'mode', [(i, i ^ bit) for i in range(groups)])]
  transfers between devices with their start and end apart: 10 -> 10, of which waited for: 4 -> 2; matrix products, arithmetic and copies ran while one was open for 0% -> 2% of each run, Pallas kernels for 8% -> 3%
where the time goes in v4:
time: 40.5 us; the launch traced here: 40.4 us
  starting transfers between devices  20.5 us (51%)
  waiting for transfers between devices  8.7 us (21%)
  Pallas kernels  8.34 us (21%)
  local copies, waits for them, and re-layouts  1.23 us (3%)
  other arithmetic  0.81 us (2%)
  between operations  0.76 us (2%)
    ppermute x5, waiting for transfers between devices, across(): return lax.ppermute(x, 'mode', [(i, i ^ bit) for i in range(groups)])  8.69 us
    ppermute x5, starting transfers between devices, across(): return lax.ppermute(x, 'mode', [(i, i ^ bit) for i in range(groups)])  8.57 us
    ppermute x3, starting transfers between devices, to_pair(): return lax.ppermute(x, 'mode', pairs)  8.19 us
    pallas_call x1, Pallas kernels, body(): steps_call(functools.partial(steps_kernel, modes, tiles))  7.14 us
    ppermute x2, starting transfers between devices, to_tile(): return lax.ppermute(x, 'tile', pairs)  3.71 us
    pallas_call x1, Pallas kernels, body(): small_kernel(pack_kernel, 'pack_edges', shape(9, 8, 128), [VMEM] * 2, LONG)  1.2 us
  transfers between devices with their start and end apart: 10, of which 2 were waited for; matrix products, arithmetic and copies ran while one was open for 2% of the time, Pallas kernels for 3%

profile of v4, /device:TPU:0, one launch (start us, length us, event | category | flops | bytes accessed | tf_op | source)
XLA Modules:
  0.0 40.4 jit_solution(9113256533408228822)
XLA Ops:
  0.0 3.0 %collective-permute-start.7 = (f32[1,9,32,128]{3,2,1,0:T(8,128)}, f32[1,9,32,128]{3,2,1,0:T(8,128)S(1)}, u32[]{:S(2)}, u32[]{:S(2)}) collective-permute-start(f32[1,9,32,128]{3,2,1,0:T(8,128)} %param.7), channel_id=1, source_target_pairs={{0,8},{4,12},{8,0},{12,4},{16,24},{20,28},{24,16},{28,20},{1,9},{5... | collective-permute-start | bytes 442376 | tf_op jit(solution)/shard_map/ppermute | solution.py:400
  3.0 1.5 %collective-permute-start.8 = (f32[4,6,32,128]{3,2,1,0:T(8,128)}, f32[4,6,32,128]{3,2,1,0:T(8,128)S(1)}, u32[]{:S(2)}, u32[]{:S(2)}) collective-permute-start(f32[4,6,32,128]{3,2,1,0:T(8,128)} %own_hbm.1), channel_id=1, source_target_pairs={{0,4},{4,0},{8,12},{12,8},{16,20},{20,16},{24,28},{28,24},{1,5},{5... | collective-permute-start | bytes 1179656 | tf_op jit(solution)/shard_map/ppermute | solution.py:397
  4.5 2.4 %collective-permute-start.9 = (f32[4,6,32,128]{3,2,1,0:T(8,128)}, f32[4,6,32,128]{3,2,1,0:T(8,128)S(1)}, u32[]{:S(2)}, u32[]{:S(2)}) collective-permute-start(f32[4,6,32,128]{3,2,1,0:T(8,128)} %own_hbm.1), channel_id=1, source_target_pairs={{4,8},{8,4},{12,16},{16,12},{20,24},{24,20},{28,0},{0,28},{5,9},{9... | collective-permute-start | bytes 1179656 | tf_op jit(solution)/shard_map/ppermute | solution.py:397
  7.6 0.0 copy-start.3
  7.6 0.6 %copy-done.3 = s32[4]{0:T(128)S(1)} copy-done((s32[4]{0:T(128)S(1)}, s32[4]{0:T(128)}, u32[]{:S(2)}) %copy-start.3) | copy-done | bytes 40
  8.3 0.1 pad_add_fusion.info_ref
  8.4 0.0 collective-permute-done.7
  8.4 1.2 %pack_edges.1 = f32[9,8,128]{2,1,0:T(8,128)S(1)} custom-call(f32[4,6,32,128]{3,2,1,0:T(8,128)} %own_hbm.1, f32[1,9,32,128]{3,2,1,0:T(8,128)S(1)} %broadcast_select_fusion.4.flow_ref), custom_call_target="tpu_custom_call" | custom-call | flops 1000000000 | bytes 100000000 | tf_op jit(solution)/shard_map/pack_edges/pallas_call | solution.py:418
  9.6 0.0 copy-start
  9.7 23.6 %conditional.1 = (f32[1,9,32,128]{3,2,1,0:T(8,128)S(1)}, f32[1,9,32,128]{3,2,1,0:T(8,128)}, f32[15,8,128]{2,1,0:T(8,128)}, f32[15,8,128]{2,1,0:T(8,128)}, f32[2,6,8,128]{3,2,1,0:T(8,128)S(1)}) conditional(s32[]{:T(128)} %convert_element_type.3, f32[1,9,32,128]{3,2,1,0:T(8,128)S(1)} %broadcast_select_fusion.4.flow_ref, (s32[]{:T(128)}, ...), branch_computations={%region_0.1_spmd, %region_1.2_spmd} | conditional | flops 120590 | bytes 3388166 | solution.py:441
  9.7 0.8 %collective-permute-start.2 = (f32[9,8,128]{2,1,0:T(8,128)S(1)}, f32[9,8,128]{2,1,0:T(8,128)S(1)}, u32[]{:S(2)}, u32[]{:S(2)}) collective-permute-start(f32[9,8,128]{2,1,0:T(8,128)S(1)} %get-tuple-element.17), channel_id=1, source_target_pairs={{1,2},{2,1},{5,6},{6,5},{9,10},{10,9},{13,14},{14,13},{17,18},{18,... | collective-permute-start | bytes 110600 | tf_op jit(solution)/shard_map/cond/branch_1_fun/ppermute | solution.py:406
  10.5 2.9 %collective-permute-start.1 = (f32[9,8,128]{2,1,0:T(8,128)S(1)}, f32[9,8,128]{2,1,0:T(8,128)S(1)}, u32[]{:S(2)}, u32[]{:S(2)}) collective-permute-start(f32[9,8,128]{2,1,0:T(8,128)S(1)} %get-tuple-element.17), channel_id=1, source_target_pairs={{0,1},{1,0},{2,3},{3,2},{4,5},{5,4},{6,7},{7,6},{8,9},{9,8},{10,11... | collective-permute-start | bytes 110600 | tf_op jit(solution)/shard_map/cond/branch_1_fun/ppermute | solution.py:406
  13.4 2.1 %collective-permute-start = (f32[1,9,32,128]{3,2,1,0:T(8,128)S(1)}, f32[1,9,32,128]{3,2,1,0:T(8,128)S(1)}, u32[]{:S(2)}, u32[]{:S(2)}) collective-permute-start(f32[1,9,32,128]{3,2,1,0:T(8,128)S(1)} %get-tuple-element.18), channel_id=1, source_target_pairs={{0,16},{4,20},{8,24},{12,28},{16,0},{20,4},{24,8},{28,12},{1,17},{... | collective-permute-start | bytes 442376 | tf_op jit(solution)/shard_map/cond/branch_1_fun/ppermute | solution.py:400
  15.5 0.0 collective-permute-done.2
  15.5 0.0 collective-permute-done.1
  15.6 4.3 %collective-permute-start.4 = (f32[2,6,8,128]{3,2,1,0:T(8,128)S(1)}, f32[2,6,8,128]{3,2,1,0:T(8,128)S(1)}, u32[]{:S(2)}, u32[]{:S(2)}) collective-permute-start(f32[2,6,8,128]{3,2,1,0:T(8,128)S(1)} %pad_maximum_fusion.1), channel_id=1, source_target_pairs={{4,8},{8,4},{12,16},{16,12},{20,24},{24,20},{28,0},{0,28},{5,9},{9... | collective-permute-start | bytes 147464 | tf_op jit(solution)/shard_map/cond/branch_1_fun/ppermute | solution.py:397
  19.8 1.2 %collective-permute-start.3 = (f32[3,8,128]{2,1,0:T(8,128)S(1)}, f32[3,8,128]{2,1,0:T(8,128)S(1)}, u32[]{:S(2)}, u32[]{:S(2)}) collective-permute-start(f32[3,8,128]{2,1,0:T(8,128)S(1)} %slice_select_fusion.2), channel_id=1, source_target_pairs={{0,16},{4,20},{8,24},{12,28},{16,0},{20,4},{24,8},{28,12},{1,17},{... | collective-permute-start | bytes 36872 | tf_op jit(solution)/shard_map/cond/branch_1_fun/ppermute | solution.py:400
  21.0 3.8 %collective-permute-done.3 = f32[3,8,128]{2,1,0:T(8,128)S(1)} collective-permute-done((f32[3,8,128]{2,1,0:T(8,128)S(1)}, f32[3,8,128]{2,1,0:T(8,128)S(1)}, u32[]{:S(2)}, u32[]{:S(2)}) %collective-permute-start.3) | collective-permute-done | bytes 12320 | tf_op jit(solution)/shard_map/cond/branch_1_fun/ppermute | solution.py:400
  24.9 0.0 collective-permute-done.4
  24.9 0.0 copy-start.1
  24.9 0.0 collective-permute-done
  24.9 0.6 %copy-done.1 = f32[2,6,8,128]{3,2,1,0:T(8,128)} copy-done((f32[2,6,8,128]{3,2,1,0:T(8,128)}, f32[2,6,8,128]{3,2,1,0:T(8,128)S(1)}, u32[]{:S(2)}) %copy-start.1) | copy-done | bytes 49176 | tf_op jit(solution)/shard_map/cond
  25.5 2.2 %collective-permute-start.5 = (f32[1,9,32,128]{3,2,1,0:T(8,128)S(1)}, f32[1,9,32,128]{3,2,1,0:T(8,128)}, u32[]{:S(2)}, u32[]{:S(2)}) collective-permute-start(f32[1,9,32,128]{3,2,1,0:T(8,128)S(1)} %broadcast_select_fusion), channel_id=1, source_target_pairs={{0,4},{4,0},{8,12},{12,8},{16,20},{20,16},{24,28},{28,24},{1,5},{5... | collective-permute-start | bytes 442376 | tf_op jit(solution)/shard_map/cond/branch_1_fun/ppermute | solution.py:400
  27.7 0.0 copy-start.2
  27.8 0.6 %pad_maximum_fusion = f32[15,8,128]{2,1,0:T(8,128)} fusion(f32[12,8,128]{2,1,0:T(8,128)S(1)} %bitcast.14, f32[3,8,128]{2,1,0:T(8,128)S(1)} %broadcast_select_fusion.3), kind=kLoop, calls=%fused_computation.1 | loop fusion | flops 15360 | bytes 122880 | tf_op jit(solution)/shard_map/cond/branch_1_fun/concatenate | solution.py:434
  28.4 0.0 collective-permute-start.6
  28.4 4.9 %collective-permute-done.6 = f32[15,8,128]{2,1,0:T(8,128)} collective-permute-done((f32[15,8,128]{2,1,0:T(8,128)}, f32[15,8,128]{2,1,0:T(8,128)}, u32[]{:S(2)}, u32[]{:S(2)}) %collective-permute-start.6) | collective-permute-done | bytes 61472 | tf_op jit(solution)/shard_map/cond/branch_1_fun/ppermute | solution.py:400
  33.2 0.0 collective-permute-done.5
  33.2 0.0 copy-done.2
  33.2 0.0 collective-permute-done.8.pair_hbm
  33.2 0.0 collective-permute-done.9.other_hbm
  33.3 0.0 copy-done
  33.3 7.1 %heun_steps.1 = f32[4,6,32,128]{3,2,1,0:T(8,128)} custom-call(s32[4]{0:T(128)S(1)} %pad_add_fusion.info_ref, f32[1,9,32,128]{3,2,1,0:T(8,128)S(1)} %get-tuple-element.28.flow_hbm, f32[1,9,32,128]{3,2,1,0:T(8,128)} %get-tuple-element.29.flow2_hbm, f32[15,8,128]{2,1,0:T(8,128)} %get-tuple-element.30.message_hbm, f32[15,8,128]{2,1,0:T(8,128)} %get-tuple-element.31.message2_hbm, ...), custom_call_target="tpu_custom_call" | custom-call | tf_op jit(solution)/shard_map/heun_steps/pallas_call | solution.py:450
  (10 shorter events, 0.1 us)
Async XLA Ops:
  0.0 8.4 %collective-permute-start.7 = (f32[1,9,32,128]{3,2,1,0:T(8,128)}, f32[1,9,32,128]{3,2,1,0:T(8,128)S(1)}, u32[]{:S(2)}, u32[]{:S(2)}) collective-permute-start(f32[1,9,32,128]{3,2,1,0:T(8,128)} %param.7), channel_id=1, source_target_pairs={{0,8},{4,12},{8,0},{12,4},{16,24},{20,28},{24,16},{28,20},{1,9},{5... | collective-permute-start | bytes 442376 | tf_op jit(solution)/shard_map/ppermute | solution.py:400
  3.0 30.2 %collective-permute-start.8 = (f32[4,6,32,128]{3,2,1,0:T(8,128)}, f32[4,6,32,128]{3,2,1,0:T(8,128)S(1)}, u32[]{:S(2)}, u32[]{:S(2)}) collective-permute-start(f32[4,6,32,128]{3,2,1,0:T(8,128)} %own_hbm.1), channel_id=1, source_target_pairs={{0,4},{4,0},{8,12},{12,8},{16,20},{20,16},{24,28},{28,24},{1,5},{5... | collective-permute-start | bytes 1179656 | tf_op jit(solution)/shard_map/ppermute | solution.py:397
  4.5 28.7 %collective-permute-start.9 = (f32[4,6,32,128]{3,2,1,0:T(8,128)}, f32[4,6,32,128]{3,2,1,0:T(8,128)S(1)}, u32[]{:S(2)}, u32[]{:S(2)}) collective-permute-start(f32[4,6,32,128]{3,2,1,0:T(8,128)} %own_hbm.1), channel_id=1, source_target_pairs={{4,8},{8,4},{12,16},{16,12},{20,24},{24,20},{28,0},{0,28},{5,9},{9... | collective-permute-start | bytes 1179656 | tf_op jit(solution)/shard_map/ppermute | solution.py:397
  7.6 0.7 %copy-start.3 = (s32[4]{0:T(128)S(1)}, s32[4]{0:T(128)}, u32[]{:S(2)}) copy-start(s32[4]{0:T(128)} %param.8) | copy-start | bytes 52
  9.6 23.6 %copy-start = (f32[4,6,32,128]{3,2,1,0:T(8,128)S(1)}, f32[4,6,32,128]{3,2,1,0:T(8,128)}, u32[]{:S(2)}) copy-start(f32[4,6,32,128]{3,2,1,0:T(8,128)} %own_hbm.1) | copy-start | bytes 1179652
  9.7 5.8 %collective-permute-start.2 = (f32[9,8,128]{2,1,0:T(8,128)S(1)}, f32[9,8,128]{2,1,0:T(8,128)S(1)}, u32[]{:S(2)}, u32[]{:S(2)}) collective-permute-start(f32[9,8,128]{2,1,0:T(8,128)S(1)} %get-tuple-element.17), channel_id=1, source_target_pairs={{1,2},{2,1},{5,6},{6,5},{9,10},{10,9},{13,14},{14,13},{17,18},{18,... | collective-permute-start | bytes 110600 | tf_op jit(solution)/shard_map/cond/branch_1_fun/ppermute | solution.py:406
  10.5 5.0 %collective-permute-start.1 = (f32[9,8,128]{2,1,0:T(8,128)S(1)}, f32[9,8,128]{2,1,0:T(8,128)S(1)}, u32[]{:S(2)}, u32[]{:S(2)}) collective-permute-start(f32[9,8,128]{2,1,0:T(8,128)S(1)} %get-tuple-element.17), channel_id=1, source_target_pairs={{0,1},{1,0},{2,3},{3,2},{4,5},{5,4},{6,7},{7,6},{8,9},{9,8},{10,11... | collective-permute-start | bytes 110600 | tf_op jit(solution)/shard_map/cond/branch_1_fun/ppermute | solution.py:406
  13.4 11.5 %collective-permute-start = (f32[1,9,32,128]{3,2,1,0:T(8,128)S(1)}, f32[1,9,32,128]{3,2,1,0:T(8,128)S(1)}, u32[]{:S(2)}, u32[]{:S(2)}) collective-permute-start(f32[1,9,32,128]{3,2,1,0:T(8,128)S(1)} %get-tuple-element.18), channel_id=1, source_target_pairs={{0,16},{4,20},{8,24},{12,28},{16,0},{20,4},{24,8},{28,12},{1,17},{... | collective-permute-start | bytes 442376 | tf_op jit(solution)/shard_map/cond/branch_1_fun/ppermute | solution.py:400
  15.6 9.3 %collective-permute-start.4 = (f32[2,6,8,128]{3,2,1,0:T(8,128)S(1)}, f32[2,6,8,128]{3,2,1,0:T(8,128)S(1)}, u32[]{:S(2)}, u32[]{:S(2)}) collective-permute-start(f32[2,6,8,128]{3,2,1,0:T(8,128)S(1)} %pad_maximum_fusion.1), channel_id=1, source_target_pairs={{4,8},{8,4},{12,16},{16,12},{20,24},{24,20},{28,0},{0,28},{5,9},{9... | collective-permute-start | bytes 147464 | tf_op jit(solution)/shard_map/cond/branch_1_fun/ppermute | solution.py:397
  19.8 5.1 %collective-permute-start.3 = (f32[3,8,128]{2,1,0:T(8,128)S(1)}, f32[3,8,128]{2,1,0:T(8,128)S(1)}, u32[]{:S(2)}, u32[]{:S(2)}) collective-permute-start(f32[3,8,128]{2,1,0:T(8,128)S(1)} %slice_select_fusion.2), channel_id=1, source_target_pairs={{0,16},{4,20},{8,24},{12,28},{16,0},{20,4},{24,8},{28,12},{1,17},{... | collective-permute-start | bytes 36872 | tf_op jit(solution)/shard_map/cond/branch_1_fun/ppermute | solution.py:400
  24.9 0.6 %copy-start.1 = (f32[2,6,8,128]{3,2,1,0:T(8,128)}, f32[2,6,8,128]{3,2,1,0:T(8,128)S(1)}, u32[]{:S(2)}) copy-start(f32[2,6,8,128]{3,2,1,0:T(8,128)S(1)} %collective-permute-done.4) | copy-start | bytes 147460 | tf_op jit(solution)/shard_map/cond
  25.5 7.7 %collective-permute-start.5 = (f32[1,9,32,128]{3,2,1,0:T(8,128)S(1)}, f32[1,9,32,128]{3,2,1,0:T(8,128)}, u32[]{:S(2)}, u32[]{:S(2)}) collective-permute-start(f32[1,9,32,128]{3,2,1,0:T(8,128)S(1)} %broadcast_select_fusion), channel_id=1, source_target_pairs={{0,4},{4,0},{8,12},{12,8},{16,20},{20,16},{24,28},{28,24},{1,5},{5... | collective-permute-start | bytes 442376 | tf_op jit(solution)/shard_map/cond/branch_1_fun/ppermute | solution.py:400
  27.7 5.5 %copy-start.2 = (f32[2,6,8,128]{3,2,1,0:T(8,128)S(1)}, f32[2,6,8,128]{3,2,1,0:T(8,128)}, u32[]{:S(2)}) copy-start(f32[2,6,8,128]{3,2,1,0:T(8,128)} %copy-done.1) | copy-start | bytes 147460 | tf_op jit(solution)/shard_map/cond
  28.4 4.9 %collective-permute-start.6 = (f32[15,8,128]{2,1,0:T(8,128)}, f32[15,8,128]{2,1,0:T(8,128)}, u32[]{:S(2)}, u32[]{:S(2)}) collective-permute-start(f32[15,8,128]{2,1,0:T(8,128)} %pad_maximum_fusion), channel_id=1, source_target_pairs={{0,4},{4,0},{8,12},{12,8},{16,20},{20,16},{24,28},{28,24},{1,5},{5... | collective-permute-start | bytes 184328 | tf_op jit(solution)/shard_map/cond/branch_1_fun/ppermute | solution.py:400

commit v5 on v4

--- a/solution.py
+++ b/solution.py
@@ -48,26 +48,17 @@
         edges_ref[6 + block] = total
 
 
-def strips_kernel(place_ref, edges_ref, near_ref, far_ref, strips_ref, halo_ref):
-    low = lane_index() % 8 < 4
-    odd = place_ref[0] % 2 == 1
-    for row in range(9):
-        left = jnp.where(odd, near_ref[row], far_ref[row])
-        right = jnp.where(odd, far_ref[row], near_ref[row])
-        if row < 6:
-            strips_ref[0, row] = jnp.where(low, left, edges_ref[row])
-            strips_ref[1, row] = jnp.where(low, edges_ref[row], right)
-        else:
-            halo_ref[row - 6] = jnp.where(low, left, right)
-
-
-def join_kernel(pick_ref, halo_ref, halo2_ref, strips_ref, message_ref):
-    other = pick_ref[0] != 0
-    for block in range(3):
-        message_ref[block] = jnp.where(other, halo2_ref[block], halo_ref[block])
-    for side in range(2):
+def pack_fields_kernel(pair_ref, other_ref, edges_ref):
+    lane = lane_index()
+    for group, field_ref in enumerate((pair_ref, other_ref)):
         for comp in range(6):
-            message_ref[3 + 6 * side + comp] = strips_ref[side, comp]
+            total = jnp.zeros((8, 128), f32)
+            for zt in range(4):
+                for mode in range(GROUP):
+                    at = 32 * zt + 8 * mode
+                    piece = turn(field_ref[mode, comp, 8 * zt : 8 * zt + 8, :], at + 4)
+                    total = jnp.where((lane >= at) & (lane < at + 8), piece, total)
+            edges_ref[group, comp] = total
 
 
 def emf_of(flow, centre, total, gap):
@@ -150,33 +141,17 @@
 
 
 def steps_kernel(
-    modes, tiles, info_ref, flow_hbm, flow2_hbm, message_hbm, message2_hbm, strips_hbm, own_hbm, pair_hbm, other_hbm, out_hbm,
-    state, trial, out, strip, strip_trial, inject, flow, flow_strip, near_message, far_message, other_strips, emfs, emfs_strip, sums, gaps, rights, lefts, sems,
+    modes, tiles, info_ref, flow_ref, flow2_ref, strips_ref, edges_ref, near_ref, far_ref, own_hbm, pair_hbm, other_hbm, out_hbm,
+    state, trial, out, strip, strip_trial, inject, flow, flow_strip, emfs, emfs_strip, sums, gaps, rights, lefts, sems,
 ):
     base, tile, take, odd = info_ref[0], info_ref[1], info_ref[2], info_ref[3]
 
     places = (GROUP, 2 * GROUP * (1 - odd), 2 * GROUP * odd)
     rows = pl.ds(PAD, 32)
-    loads = [
-        pltpu.make_async_copy(message_hbm, near_message, sems.at[0]),
-        pltpu.make_async_copy(message2_hbm, far_message, sems.at[1]),
-        pltpu.make_async_copy(strips_hbm, other_strips, sems.at[2]),
-    ]
     field_loads = [
         pltpu.make_async_copy(src, state.at[pl.ds(place, GROUP), :, rows], sems.at[4 + i])
         for i, (src, place) in enumerate(zip((own_hbm, pair_hbm, other_hbm), places))
     ]
-    for load in loads:
-        load.start()
-
-    @pl.when(take == 0)
-    def _():
-        pltpu.make_async_copy(flow_hbm.at[0], flow, sems.at[3]).start()
-
-    @pl.when(take != 0)
-    def _():
-        pltpu.make_async_copy(flow2_hbm.at[0], flow, sems.at[3]).start()
-
     for load in field_loads:
         load.start()
 
@@ -206,27 +181,35 @@
         strip_coef.append(with_waves(coefficients(column_radius(column)), wave_at(base, lane8 // 8, modes)))
         strip_inside.append((column >= 0) & (column < tiles * 128))
 
-    for load in loads:
-        load.wait()
-    for side in range(2):
-        for comp in range(6):
-            at = 3 + 6 * side + comp
-            own, other, pair = near_message[at], other_strips[side, comp], far_message[at]
+    tile_odd = lax.rem(tile, 2) == 1
+    for comp in range(6):
+        sides = []
+        for group in range(2):
+            edges, near, far = edges_ref[group, comp], near_ref[group, comp], far_ref[group, comp]
+            left = jnp.where(tile == 0, 0.0, jnp.where(tile_odd, near, far))
+            right = jnp.where(tile == tiles - 1, 0.0, jnp.where(tile_odd, far, near))
+            sides.append((jnp.where(column8 < 4, left, edges), jnp.where(column8 < 4, edges, right)))
+        for side in range(2):
+            own, pair, other = strips_ref[side, comp], sides[0][side], sides[1][side]
             low, high = jnp.where(odd == 1, pair, other), jnp.where(odd == 1, other, pair)
             for zt in range(4):
                 value = jnp.where(lane8 < 32, turn(low, -32 * zt), turn(own, 32 - 32 * zt))
                 value = jnp.where(lane8 < 64, value, turn(high, 64 - 32 * zt))
                 strip[side, comp, tile_rows(zt), :] = jnp.where(lane8 < 96, value, 0.0)
 
-    pltpu.make_async_copy(flow_hbm.at[0], flow, sems.at[3]).wait()
     near = jnp.where(column8 < 4, 124 + column8, column8 - 4)
-    for r in range(9):
-        halo = jnp.where(take == 0, near_message[r // 4], far_message[r // 4])
-        for zt in range(4):
-            inside = jnp.take_along_axis(flow[r, 8 * zt : 8 * zt + 8, :], near, axis=1)
-            outside = jnp.take_along_axis(halo, 32 * (r % 4) + 8 * zt + column8, axis=1)
-            flow_strip[0, r, 8 * zt : 8 * zt + 8, :] = jnp.where(column8 < 4, outside, inside)
-            flow_strip[1, r, 8 * zt : 8 * zt + 8, :] = jnp.where(column8 < 4, inside, outside)
+    for source, wanted in ((flow_ref, 0), (flow2_ref, 1)):
+
+        @pl.when(jnp.where(take == 0, 0, 1) == wanted)
+        def _(source=source):
+            for r in range(9):
+                for zt in range(4):
+                    at = slice(8 * zt, 8 * zt + 8)
+                    flow[r, at] = source[4 * r + zt]
+                    inside = jnp.take_along_axis(source[4 * r + zt], near, axis=1)
+                    outside = jnp.take_along_axis(source[36 + r // 4], 32 * (r % 4) + 8 * zt + column8, axis=1)
+                    flow_strip[0, r, at] = jnp.where(column8 < 4, outside, inside)
+                    flow_strip[1, r, at] = jnp.where(column8 < 4, inside, outside)
 
     def strips_eval(source, store):
         places = [(side, zt) for side in range(2) for zt in range(4)]
@@ -357,7 +340,7 @@
     return pl.pallas_call(
         kernel,
         out_shape=shape(GROUP, 6, 32, 128),
-        in_specs=[SMEM] + [ANY] * 8,
+        in_specs=[SMEM] + [VMEM] * 6 + [ANY] * 3,
         out_specs=ANY,
         scratch_shapes=[
             pltpu.VMEM((SLOTS, 6, 48, 128), f32),
@@ -368,9 +351,6 @@
             pltpu.VMEM((6, 32, 128), f32),
             pltpu.VMEM((9, 32, 128), f32),
             pltpu.VMEM((2, 9, 32, 128), f32),
-            pltpu.VMEM((15, 8, 128), f32),
-            pltpu.VMEM((15, 8, 128), f32),
-            pltpu.VMEM((2, 6, 8, 128), f32),
             pltpu.VMEM((2, 4, 48, 128), f32),
             pltpu.VMEM((2, 4, 48, 128), f32),
             pltpu.VMEM((2, 6, 32, 128), f32),
@@ -401,8 +381,8 @@
 
     def to_tile(x, first):
         pairs = []
-        for i in range(first, tiles - 1, 2):
-            pairs += [(i, i + 1), (i + 1, i)]
+        for i in range(first, tiles, 2):
+            pairs += [(i, (i + 1) % tiles), ((i + 1) % tiles, i)]
         return lax.ppermute(x, "tile", pairs)
 
     bits = []
@@ -415,30 +395,6 @@
     pair = to_pair(magnetic, 0)
     flow = choose(velocity_stack, across(velocity_stack, bits[0]), bits[0])
     other = to_pair(magnetic, 1)
-    edges = small_kernel(pack_kernel, "pack_edges", shape(9, 8, 128), [VMEM] * 2, LONG)(magnetic, flow)
-
-    def small_exchanges(flow, edges):
-        for bit in bits[1:-2]:
-            flow = choose(flow, across(flow, bit), bit)
-        flow2 = across(flow, bits[-2])
-        near, far = to_tile(edges, 0), to_tile(edges, 1)
-        odd = tile % 2 == 1
-        left, right = jnp.where(odd, near, far), jnp.where(odd, far, near)
-        low = lax.broadcasted_iota(jnp.int32, (9, 8, 128), 2) % 8 < 4
-        halo = jnp.where(low[6:], left[6:], right[6:])
-        strips = jnp.stack([jnp.where(low[:6], left[:6], edges[:6]), jnp.where(low[:6], edges[:6], right[:6])])
-        halo2 = across(halo, bits[-2])
-        strips_other = to_pair(strips, 1)
-        flow, flow2, halo, halo2, strips_other = lax.optimization_barrier((flow, flow2, halo, halo2, strips_other))
-        flow, halo = choose(flow, flow2, bits[-2]), choose(halo, halo2, bits[-2])
-        message = jnp.concatenate([halo, strips.reshape(12, 8, 128)])
-        return flow, across(flow, bits[-1]), message, across(message, bits[-1]), strips_other
-
-    def none(flow, edges):
-        message, strips = jnp.zeros((15, 8, 128), f32), jnp.zeros((2, 6, 8, 128), f32)
-        return flow, flow, message, message, strips
-
-    *flows, strips_other = lax.cond(velocity_owner[0] >= 0, small_exchanges, none, flow, edges)
     info = jnp.stack(
         [
             lax.rem(wavenumber[0] + modes // 2 + modes - GROUP, modes),
@@ -447,7 +403,49 @@
             jnp.bitwise_and(me, 1),
         ]
     ).astype(jnp.int32)
-    return steps_call(functools.partial(steps_kernel, modes, tiles))(info, *flows, strips_other, magnetic, pair, other)
+    flow, info = lax.optimization_barrier((flow, info))
+    edges = small_kernel(pack_kernel, "pack_edges", shape(9, 8, 128), [VMEM] * 2, LONG)(magnetic, flow)
+
+    def beyond(edges):
+        near, far = to_tile(edges, 0), to_tile(edges, 1)
+        odd = tile % 2 == 1
+        left = jnp.where(tile == 0, 0.0, jnp.where(odd, near, far))
+        right = jnp.where(tile == tiles - 1, 0.0, jnp.where(odd, far, near))
+        return left, right, lax.broadcasted_iota(jnp.int32, edges.shape, edges.ndim - 1) % 8 < 4
+
+    def as_strips(edges, left, right, low):
+        return jnp.stack([jnp.where(low, left, edges), jnp.where(low, edges, right)])
+
+    def middle_rounds(flow, edges):
+        for bit in bits[1:-2]:
+            flow = choose(flow, across(flow, bit), bit)
+        flow2 = across(flow, bits[-2])
+        left, right, low = beyond(edges)
+        strips = as_strips(edges[:6], left[:6], right[:6], low[:6])
+        halo = jnp.where(low[6:], left[6:], right[6:])
+        for bit in bits[1:-2]:
+            halo = choose(halo, across(halo, bit), bit)
+        halo2 = across(halo, bits[-2])
+        flow, flow2, halo, halo2 = lax.optimization_barrier((flow, flow2, halo, halo2))
+        flow, halo = choose(flow, flow2, bits[-2]), choose(halo, halo2, bits[-2])
+        return jnp.concatenate([flow.reshape(36, 8, 128), halo]), strips
+
+    def no_rounds(flow, edges):
+        return jnp.zeros((39, 8, 128), f32), jnp.zeros((2, 6, 8, 128), f32)
+
+    def neighbours(pair, other):
+        edges = small_kernel(pack_fields_kernel, "pack_field_edges", shape(2, 6, 8, 128), [VMEM] * 2)(pair, other)
+        near, far = to_tile(edges, 0), to_tile(edges, 1)
+        return edges, near, far
+
+    def no_neighbours(pair, other):
+        edges = jnp.zeros((2, 6, 8, 128), f32)
+        return edges, edges, edges
+
+    flow, strips = lax.cond(velocity_owner[0] >= 0, middle_rounds, no_rounds, flow, edges)
+    flow2 = across(flow, 1)
+    edges, near, far = lax.cond(velocity_owner[0] < groups, neighbours, no_neighbours, pair, other)
+    return steps_call(functools.partial(steps_kernel, modes, tiles))(info, flow, flow2, strips, edges, near, far, magnetic, pair, other)
 
 
 def solution(mesh):

time: 40.5 us -> 38.6 us (0.953)
  starting transfers between devices: 20.5 us -> 17.7 us
  waiting for transfers between devices: 8.7 us -> 9.92 us
  Pallas kernels: 8.34 us -> 9.02 us
  other arithmetic: 0.81 us -> 0.19 us
  local copies, waits for them, and re-layouts: 1.23 us -> 0.65 us
    ppermute x3 -> x2, starting transfers between devices: 8.19 us -> 3.94 us  [to_pair(): return lax.ppermute(x, 'mode', pairs)]
    ppermute x2 -> x4, waiting for transfers between devices: 0.01 us -> 2.73 us  [to_tile(): return lax.ppermute(x, 'tile', pairs)]
    ppermute x5 -> x4, starting transfers between devices: 8.57 us -> 10.5 us  [across(): return lax.ppermute(x, 'mode', [(i, i ^ bit) for i in range(groups)])]
    ppermute x5 -> x4, waiting for transfers between devices: 8.69 us -> 7.19 us  [across(): return lax.ppermute(x, 'mode', [(i, i ^ bit) for i in range(groups)])]
    pallas_call x0 -> x1, Pallas kernels: none -> 0.9 us  [neighbours(): small_kernel(pack_fields_kernel, 'pack_field_edges', shape(2, 6, 8, 128),...]
    concatenate x1, other arithmetic: 0.62 us -> 0.01 us  [middle_rounds(): return (jnp.concatenate([flow.reshape(36, 8, 128), halo]), strips)]
    cond x4 -> x0, local copies, waits for them, and re-layouts: 0.57 us -> none
    ppermute x2 -> x4, starting transfers between devices: 3.71 us -> 3.28 us  [to_tile(): return lax.ppermute(x, 'tile', pairs)]
  transfers between devices with their start and end apart: 10 -> 10, of which waited for: 2 -> 2; matrix products, arithmetic and copies ran while one was open for 2% -> 1% of each run, Pallas kernels for 3% -> 5%
where the time goes in v5:
time: 38.6 us; the launch traced here: 38.4 us
  starting transfers between devices  17.7 us (46%)
  waiting for transfers between devices  9.92 us (26%)
  Pallas kernels  9.02 us (23%)
  between operations  0.75 us (2%)
  local copies, waits for them, and re-layouts  0.65 us (2%)
    ppermute x4, starting transfers between devices, across(): return lax.ppermute(x, 'mode', [(i, i ^ bit) for i in range(groups)])  10.5 us
    ppermute x4, waiting for transfers between devices, across(): return lax.ppermute(x, 'mode', [(i, i ^ bit) for i in range(groups)])  7.19 us
    pallas_call x1, Pallas kernels, body(): steps_call(functools.partial(steps_kernel, modes, tiles))  6.92 us
    ppermute x2, starting transfers between devices, to_pair(): return lax.ppermute(x, 'mode', pairs)  3.94 us
    ppermute x4, starting transfers between devices, to_tile(): return lax.ppermute(x, 'tile', pairs)  3.28 us
    ppermute x4, waiting for transfers between devices, to_tile(): return lax.ppermute(x, 'tile', pairs)  2.73 us
    pallas_call x1, Pallas kernels, body(): small_kernel(pack_kernel, 'pack_edges', shape(9, 8, 128), [VMEM] * 2, LONG)  1.2 us
    pallas_call x1, Pallas kernels, neighbours(): small_kernel(pack_fields_kernel, 'pack_field_edges', shape(2, 6, 8, 128),...  0.9 us
  transfers between devices with their start and end apart: 10, of which 2 were waited for; matrix products, arithmetic and copies ran while one was open for 1% of the time, Pallas kernels for 5%

profile of v5, /device:TPU:0, one launch (start us, length us, event | category | flops | bytes accessed | tf_op | source)
XLA Modules:
  0.0 38.4 jit_solution(8326754102166936094)
XLA Ops:
  0.0 3.0 %collective-permute-start.6 = (f32[1,9,32,128]{3,2,1,0:T(8,128)}, f32[1,9,32,128]{3,2,1,0:T(8,128)S(1)}, u32[]{:S(2)}, u32[]{:S(2)}) collective-permute-start(f32[1,9,32,128]{3,2,1,0:T(8,128)} %param.9), channel_id=1, source_target_pairs={{0,8},{4,12},{8,0},{12,4},{16,24},{20,28},{24,16},{28,20},{1,9},{5... | collective-permute-start | bytes 442376 | tf_op jit(solution)/shard_map/ppermute | solution.py:380
  3.0 1.5 %collective-permute-start.8 = (f32[4,6,32,128]{3,2,1,0:T(8,128)}, f32[4,6,32,128]{3,2,1,0:T(8,128)S(1)}, u32[]{:S(2)}, u32[]{:S(2)}) collective-permute-start(f32[4,6,32,128]{3,2,1,0:T(8,128)} %own_hbm.1), channel_id=1, source_target_pairs={{0,4},{4,0},{8,12},{12,8},{16,20},{20,16},{24,28},{28,24},{1,5},{5... | collective-permute-start | bytes 1179656 | tf_op jit(solution)/shard_map/ppermute | solution.py:377
  4.5 2.4 %collective-permute-start.9 = (f32[4,6,32,128]{3,2,1,0:T(8,128)}, f32[4,6,32,128]{3,2,1,0:T(8,128)S(1)}, u32[]{:S(2)}, u32[]{:S(2)}) collective-permute-start(f32[4,6,32,128]{3,2,1,0:T(8,128)} %own_hbm.1), channel_id=1, source_target_pairs={{4,8},{8,4},{12,16},{16,12},{20,24},{24,20},{28,0},{0,28},{5,9},{9... | collective-permute-start | bytes 1179656 | tf_op jit(solution)/shard_map/ppermute | solution.py:377
  7.6 0.0 copy-start.1
  7.6 0.6 %copy-done.1 = s32[4]{0:T(128)S(1)} copy-done((s32[4]{0:T(128)S(1)}, s32[4]{0:T(128)}, u32[]{:S(2)}) %copy-start.1) | copy-done | bytes 40
  8.3 0.1 pad_add_fusion.info_ref
  8.4 0.0 collective-permute-done.6
  8.4 1.2 %pack_edges.1 = f32[9,8,128]{2,1,0:T(8,128)S(1)} custom-call(f32[4,6,32,128]{3,2,1,0:T(8,128)} %own_hbm.1, f32[1,9,32,128]{3,2,1,0:T(8,128)S(1)} %broadcast_select_fusion.2.flow_ref), custom_call_target="tpu_custom_call" | custom-call | flops 1000000000 | bytes 100000000 | tf_op jit(solution)/shard_map/pack_edges/pallas_call | solution.py:407
  9.6 13.2 %conditional.2 = (f32[39,8,128]{2,1,0:T(8,128)S(1)}, f32[2,6,8,128]{3,2,1,0:T(8,128)S(1)}) conditional(s32[]{:T(128)} %convert_element_type.6, () %tuple.24, (s32[]{:T(128)}, f32[1,9,32,128]{3,2,1,0:T(8,128)S(1)}, s32[]{:T(128)}, f32[9,8,128]{2,1,0:T(8,128)S(1)}) %tuple.25), branch_computations={%region_0.1_spmd, %region_1.2_spmd} | conditional | flops 163600 | bytes 2159186 | solution.py:445
  9.7 0.2 collective-permute-start.4
  9.8 1.5 %collective-permute-start.3 = (f32[9,8,128]{2,1,0:T(8,128)S(1)}, f32[9,8,128]{2,1,0:T(8,128)S(1)}, u32[]{:S(2)}, u32[]{:S(2)}) collective-permute-start(f32[9,8,128]{2,1,0:T(8,128)S(1)} %get-tuple-element.20), channel_id=1, source_target_pairs={{0,1},{1,0},{2,3},{3,2},{4,5},{5,4},{6,7},{7,6},{8,9},{9,8},{10,11... | collective-permute-start | bytes 110600 | tf_op jit(solution)/shard_map/cond/branch_1_fun/ppermute | solution.py:386
  11.3 2.1 %collective-permute-start.2 = (f32[1,9,32,128]{3,2,1,0:T(8,128)S(1)}, f32[1,9,32,128]{3,2,1,0:T(8,128)S(1)}, u32[]{:S(2)}, u32[]{:S(2)}) collective-permute-start(f32[1,9,32,128]{3,2,1,0:T(8,128)S(1)} %get-tuple-element.21), channel_id=1, source_target_pairs={{0,16},{4,20},{8,24},{12,28},{16,0},{20,4},{24,8},{28,12},{1,17},{... | collective-permute-start | bytes 442376 | tf_op jit(solution)/shard_map/cond/branch_1_fun/ppermute | solution.py:380
  13.4 0.0 collective-permute-done.4
  13.5 0.0 collective-permute-done.3
  13.5 2.1 %collective-permute-start.5 = (f32[3,8,128]{2,1,0:T(8,128)S(1)}, f32[3,8,128]{2,1,0:T(8,128)S(1)}, u32[]{:S(2)}, u32[]{:S(2)}) collective-permute-start(f32[3,8,128]{2,1,0:T(8,128)S(1)} %slice_select_fusion.2), channel_id=1, source_target_pairs={{0,16},{4,20},{8,24},{12,28},{16,0},{20,4},{24,8},{28,12},{1,17},{... | collective-permute-start | bytes 36872 | tf_op jit(solution)/shard_map/cond/branch_1_fun/ppermute | solution.py:380
  15.6 7.2 %collective-permute-done.5 = f32[3,8,128]{2,1,0:T(8,128)S(1)} collective-permute-done((f32[3,8,128]{2,1,0:T(8,128)S(1)}, f32[3,8,128]{2,1,0:T(8,128)S(1)}, u32[]{:S(2)}, u32[]{:S(2)}) %collective-permute-start.5) | collective-permute-done | bytes 12320 | tf_op jit(solution)/shard_map/cond/branch_1_fun/ppermute | solution.py:380
  22.8 0.0 collective-permute-done.2
  22.9 3.3 %collective-permute-start.7 = (f32[39,8,128]{2,1,0:T(8,128)S(1)}, f32[39,8,128]{2,1,0:T(8,128)S(1)}, u32[]{:S(2)}, u32[]{:S(2)}) collective-permute-start(f32[39,8,128]{2,1,0:T(8,128)S(1)} %get-tuple-element.36.flow_ref), channel_id=1, source_target_pairs={{0,4},{4,0},{8,12},{12,8},{16,20},{20,16},{24,28},{28,24},{1,5},{5... | collective-permute-start | bytes 479240 | tf_op jit(solution)/shard_map/ppermute | solution.py:380
  26.2 0.0 collective-permute-done.8.pair_hbm
  26.2 0.0 collective-permute-done.9.other_hbm
  26.2 0.0 copy-start
  26.2 5.2 %conditional.3 = (f32[2,6,8,128]{3,2,1,0:T(8,128)}, f32[2,6,8,128]{3,2,1,0:T(8,128)}, f32[2,6,8,128]{3,2,1,0:T(8,128)}) conditional(s32[]{:T(128)} %convert_element_type.7, () %tuple.26, (f32[4,6,32,128]{3,2,1,0:T(8,128)S(1)}, f32[4,6,32,128]{3,2,1,0:T(8,128)S(1)}) %tuple.27), branch_computations={%region_2.3_spmd, %region_3.4_spmd} | conditional | flops 8 | bytes 393328 | solution.py:447
  26.2 0.9 %pack_field_edges.1 = f32[2,6,8,128]{3,2,1,0:T(8,128)} custom-call(f32[4,6,32,128]{3,2,1,0:T(8,128)S(1)} %get-tuple-element.25.pair_ref, f32[4,6,32,128]{3,2,1,0:T(8,128)S(1)} %get-tuple-element.26.other_ref), custom_call_target="tpu_custom_call" | custom-call | flops 8 | bytes 8 | tf_op jit(solution)/shard_map/cond/branch_1_fun/pack_field_edges/pallas_call | solution.py:437
  27.1 0.9 %collective-permute-start.1 = (f32[2,6,8,128]{3,2,1,0:T(8,128)}, f32[2,6,8,128]{3,2,1,0:T(8,128)}, u32[]{:S(2)}, u32[]{:S(2)}) collective-permute-start(f32[2,6,8,128]{3,2,1,0:T(8,128)} %pack_field_edges.1), channel_id=1, source_target_pairs={{1,2},{2,1},{3,0},{0,3},{5,6},{6,5},{7,4},{4,7},{9,10},{10,9},{11,... | collective-permute-start | bytes 147464 | tf_op jit(solution)/shard_map/cond/branch_1_fun/ppermute | solution.py:386
  28.0 0.7 %collective-permute-start = (f32[2,6,8,128]{3,2,1,0:T(8,128)}, f32[2,6,8,128]{3,2,1,0:T(8,128)}, u32[]{:S(2)}, u32[]{:S(2)}) collective-permute-start(f32[2,6,8,128]{3,2,1,0:T(8,128)} %pack_field_edges.1), channel_id=1, source_target_pairs={{0,1},{1,0},{2,3},{3,2},{4,5},{5,4},{6,7},{7,6},{8,9},{9,8},{10,11... | collective-permute-start | bytes 147464 | tf_op jit(solution)/shard_map/cond/branch_1_fun/ppermute | solution.py:386
  28.7 2.7 %collective-permute-done.1 = f32[2,6,8,128]{3,2,1,0:T(8,128)} collective-permute-done((f32[2,6,8,128]{3,2,1,0:T(8,128)}, f32[2,6,8,128]{3,2,1,0:T(8,128)}, u32[]{:S(2)}, u32[]{:S(2)}) %collective-permute-start.1) | collective-permute-done | bytes 49184 | tf_op jit(solution)/shard_map/cond/branch_1_fun/ppermute | solution.py:386
  31.4 0.0 collective-permute-done
  31.4 0.0 collective-permute-done.7.flow2_ref
  31.4 0.0 copy-done
  31.4 6.9 %heun_steps.1 = f32[4,6,32,128]{3,2,1,0:T(8,128)} custom-call(s32[4]{0:T(128)S(1)} %pad_add_fusion.info_ref, f32[39,8,128]{2,1,0:T(8,128)S(1)} %get-tuple-element.36.flow_ref, f32[39,8,128]{2,1,0:T(8,128)S(1)} %collective-permute-done.7.flow2_ref, f32[2,6,8,128]{3,2,1,0:T(8,128)S(1)} %get-tuple-element.37.strips_ref, ...), custom_call_target="tpu_custom_call" | custom-call | tf_op jit(solution)/shard_map/heun_steps/pallas_call | solution.py:448
  (11 shorter events, 0.1 us)
Async XLA Ops:
  0.0 8.4 %collective-permute-start.6 = (f32[1,9,32,128]{3,2,1,0:T(8,128)}, f32[1,9,32,128]{3,2,1,0:T(8,128)S(1)}, u32[]{:S(2)}, u32[]{:S(2)}) collective-permute-start(f32[1,9,32,128]{3,2,1,0:T(8,128)} %param.9), channel_id=1, source_target_pairs={{0,8},{4,12},{8,0},{12,4},{16,24},{20,28},{24,16},{28,20},{1,9},{5... | collective-permute-start | bytes 442376 | tf_op jit(solution)/shard_map/ppermute | solution.py:380
  3.0 23.2 %collective-permute-start.8 = (f32[4,6,32,128]{3,2,1,0:T(8,128)}, f32[4,6,32,128]{3,2,1,0:T(8,128)S(1)}, u32[]{:S(2)}, u32[]{:S(2)}) collective-permute-start(f32[4,6,32,128]{3,2,1,0:T(8,128)} %own_hbm.1), channel_id=1, source_target_pairs={{0,4},{4,0},{8,12},{12,8},{16,20},{20,16},{24,28},{28,24},{1,5},{5... | collective-permute-start | bytes 1179656 | tf_op jit(solution)/shard_map/ppermute | solution.py:377
  4.5 21.7 %collective-permute-start.9 = (f32[4,6,32,128]{3,2,1,0:T(8,128)}, f32[4,6,32,128]{3,2,1,0:T(8,128)S(1)}, u32[]{:S(2)}, u32[]{:S(2)}) collective-permute-start(f32[4,6,32,128]{3,2,1,0:T(8,128)} %own_hbm.1), channel_id=1, source_target_pairs={{4,8},{8,4},{12,16},{16,12},{20,24},{24,20},{28,0},{0,28},{5,9},{9... | collective-permute-start | bytes 1179656 | tf_op jit(solution)/shard_map/ppermute | solution.py:377
  7.6 0.7 %copy-start.1 = (s32[4]{0:T(128)S(1)}, s32[4]{0:T(128)}, u32[]{:S(2)}) copy-start(s32[4]{0:T(128)} %param.10) | copy-start | bytes 52
  9.7 3.8 %collective-permute-start.4 = (f32[9,8,128]{2,1,0:T(8,128)S(1)}, f32[9,8,128]{2,1,0:T(8,128)S(1)}, u32[]{:S(2)}, u32[]{:S(2)}) collective-permute-start(f32[9,8,128]{2,1,0:T(8,128)S(1)} %get-tuple-element.20), channel_id=1, source_target_pairs={{1,2},{2,1},{3,0},{0,3},{5,6},{6,5},{7,4},{4,7},{9,10},{10,9},{11,... | collective-permute-start | bytes 110600 | tf_op jit(solution)/shard_map/cond/branch_1_fun/ppermute | solution.py:386
  9.8 3.6 %collective-permute-start.3 = (f32[9,8,128]{2,1,0:T(8,128)S(1)}, f32[9,8,128]{2,1,0:T(8,128)S(1)}, u32[]{:S(2)}, u32[]{:S(2)}) collective-permute-start(f32[9,8,128]{2,1,0:T(8,128)S(1)} %get-tuple-element.20), channel_id=1, source_target_pairs={{0,1},{1,0},{2,3},{3,2},{4,5},{5,4},{6,7},{7,6},{8,9},{9,8},{10,11... | collective-permute-start | bytes 110600 | tf_op jit(solution)/shard_map/cond/branch_1_fun/ppermute | solution.py:386
  11.3 11.5 %collective-permute-start.2 = (f32[1,9,32,128]{3,2,1,0:T(8,128)S(1)}, f32[1,9,32,128]{3,2,1,0:T(8,128)S(1)}, u32[]{:S(2)}, u32[]{:S(2)}) collective-permute-start(f32[1,9,32,128]{3,2,1,0:T(8,128)S(1)} %get-tuple-element.21), channel_id=1, source_target_pairs={{0,16},{4,20},{8,24},{12,28},{16,0},{20,4},{24,8},{28,12},{1,17},{... | collective-permute-start | bytes 442376 | tf_op jit(solution)/shard_map/cond/branch_1_fun/ppermute | solution.py:380
  13.5 9.3 %collective-permute-start.5 = (f32[3,8,128]{2,1,0:T(8,128)S(1)}, f32[3,8,128]{2,1,0:T(8,128)S(1)}, u32[]{:S(2)}, u32[]{:S(2)}) collective-permute-start(f32[3,8,128]{2,1,0:T(8,128)S(1)} %slice_select_fusion.2), channel_id=1, source_target_pairs={{0,16},{4,20},{8,24},{12,28},{16,0},{20,4},{24,8},{28,12},{1,17},{... | collective-permute-start | bytes 36872 | tf_op jit(solution)/shard_map/cond/branch_1_fun/ppermute | solution.py:380
  22.9 8.6 %collective-permute-start.7 = (f32[39,8,128]{2,1,0:T(8,128)S(1)}, f32[39,8,128]{2,1,0:T(8,128)S(1)}, u32[]{:S(2)}, u32[]{:S(2)}) collective-permute-start(f32[39,8,128]{2,1,0:T(8,128)S(1)} %get-tuple-element.36.flow_ref), channel_id=1, source_target_pairs={{0,4},{4,0},{8,12},{12,8},{16,20},{20,16},{24,28},{28,24},{1,5},{5... | collective-permute-start | bytes 479240 | tf_op jit(solution)/shard_map/ppermute | solution.py:380
  26.2 5.2 %copy-start = (f32[4,6,32,128]{3,2,1,0:T(8,128)S(1)}, f32[4,6,32,128]{3,2,1,0:T(8,128)}, u32[]{:S(2)}) copy-start(f32[4,6,32,128]{3,2,1,0:T(8,128)} %own_hbm.1) | copy-start | bytes 1179652
  27.1 4.3 %collective-permute-start.1 = (f32[2,6,8,128]{3,2,1,0:T(8,128)}, f32[2,6,8,128]{3,2,1,0:T(8,128)}, u32[]{:S(2)}, u32[]{:S(2)}) collective-permute-start(f32[2,6,8,128]{3,2,1,0:T(8,128)} %pack_field_edges.1), channel_id=1, source_target_pairs={{1,2},{2,1},{3,0},{0,3},{5,6},{6,5},{7,4},{4,7},{9,10},{10,9},{11,... | collective-permute-start | bytes 147464 | tf_op jit(solution)/shard_map/cond/branch_1_fun/ppermute | solution.py:386
  28.0 3.5 %collective-permute-start = (f32[2,6,8,128]{3,2,1,0:T(8,128)}, f32[2,6,8,128]{3,2,1,0:T(8,128)}, u32[]{:S(2)}, u32[]{:S(2)}) collective-permute-start(f32[2,6,8,128]{3,2,1,0:T(8,128)} %pack_field_edges.1), channel_id=1, source_target_pairs={{0,1},{1,0},{2,3},{3,2},{4,5},{5,4},{6,7},{7,6},{8,9},{9,8},{10,11... | collective-permute-start | bytes 147464 | tf_op jit(solution)/shard_map/cond/branch_1_fun/ppermute | solution.py:386

commit v6 on v5

--- a/solution.py
+++ b/solution.py
@@ -226,10 +226,14 @@
             velocity = [flow_strip[side, r, at, :] for r in range(9)]
             emf = emf_of(velocity, centre, [sums[side, i, at] for i in range(6)], [gaps[side, i, at] for i in range(6)])
             right, left, terms[side, zt] = stencil(centre, emf, strip_coef[side])
-            for i in range(4):
-                emfs_strip[side, i, tile_rows(zt), :] = emf[i]
+            if store is not None:
+                for i in range(4):
+                    emfs_strip[side, i, tile_rows(zt), :] = emf[i]
             for i in range(6):
-                rights[side, i, at], lefts[side, i, at] = right[i], left[i]
+                if store is not None or side:
+                    rights[side, i, at] = right[i]
+                if store is not None or not side:
+                    lefts[side, i, at] = left[i]
         for side, zt in places:
             at = slice(8 * zt, 8 * zt + 8)
             for i in range(6):
@@ -283,7 +287,8 @@
                 after(n)
             return carry
 
-        lax.fori_loop(0, (stop - start) // 2, two, 0)
+        for n in range((stop - start) // 2):
+            two(n, 0)
 
     def first_main(k, i, zt, total):
         trial[k, i, tile_rows(zt), :] = total

time: 38.6 us -> 38.1 us (0.987)
  other arithmetic: 0.19 us -> 1.1 us
  waiting for transfers between devices: 9.92 us -> 9.02 us
  Pallas kernels: 9.02 us -> 8.5 us
    select_n x3, other arithmetic: 0.05 us -> 0.96 us  [choose(): return jnp.where(jnp.bitwise_and(away, bit) == 0, x, y)]
    ppermute x4, waiting for transfers between devices: 7.19 us -> 6.28 us  [across(): return lax.ppermute(x, 'mode', [(i, i ^ bit) for i in range(groups)])]
    pallas_call x1, Pallas kernels: 6.92 us -> 6.41 us  [body(): steps_call(functools.partial(steps_kernel, modes, tiles))]
  transfers between devices with their start and end apart: 10 -> 10, of which waited for: 2 -> 2; matrix products, arithmetic and copies ran while one was open for 1% -> 3% of each run, Pallas kernels for 5% -> 6%
where the time goes in v6:
time: 38.1 us; the launch traced here: 37.9 us
  starting transfers between devices  17.7 us (46%)
  waiting for transfers between devices  9.02 us (24%)
  Pallas kernels  8.5 us (22%)
  other arithmetic  1.1 us (3%)
  between operations  0.75 us (2%)
  local copies, waits for them, and re-layouts  0.65 us (2%)
    ppermute x4, starting transfers between devices, across(): return lax.ppermute(x, 'mode', [(i, i ^ bit) for i in range(groups)])  10.5 us
    pallas_call x1, Pallas kernels, body(): steps_call(functools.partial(steps_kernel, modes, tiles))  6.41 us
    ppermute x4, waiting for transfers between devices, across(): return lax.ppermute(x, 'mode', [(i, i ^ bit) for i in range(groups)])  6.28 us
    ppermute x2, starting transfers between devices, to_pair(): return lax.ppermute(x, 'mode', pairs)  3.94 us
    ppermute x4, starting transfers between devices, to_tile(): return lax.ppermute(x, 'tile', pairs)  3.28 us
    ppermute x4, waiting for transfers between devices, to_tile(): return lax.ppermute(x, 'tile', pairs)  2.73 us
    pallas_call x1, Pallas kernels, body(): small_kernel(pack_kernel, 'pack_edges', shape(9, 8, 128), [VMEM] * 2, LONG)  1.2 us
    select_n x3, other arithmetic, choose(): return jnp.where(jnp.bitwise_and(away, bit) == 0, x, y)  0.96 us
  transfers between devices with their start and end apart: 10, of which 2 were waited for; matrix products, arithmetic and copies ran while one was open for 3% of the time, Pallas kernels for 6%

profile of v6, /device:TPU:0, one launch (start us, length us, event | category | flops | bytes accessed | tf_op | source)
XLA Modules:
  0.0 37.9 jit_solution(3443264752342279380)
XLA Ops:
  0.0 3.0 %collective-permute-start.6 = (f32[1,9,32,128]{3,2,1,0:T(8,128)}, f32[1,9,32,128]{3,2,1,0:T(8,128)S(1)}, u32[]{:S(2)}, u32[]{:S(2)}) collective-permute-start(f32[1,9,32,128]{3,2,1,0:T(8,128)} %param.9), channel_id=1, source_target_pairs={{0,8},{4,12},{8,0},{12,4},{16,24},{20,28},{24,16},{28,20},{1,9},{5... | collective-permute-start | bytes 442376 | tf_op jit(solution)/shard_map/ppermute | solution.py:385
  3.0 1.5 %collective-permute-start.8 = (f32[4,6,32,128]{3,2,1,0:T(8,128)}, f32[4,6,32,128]{3,2,1,0:T(8,128)S(1)}, u32[]{:S(2)}, u32[]{:S(2)}) collective-permute-start(f32[4,6,32,128]{3,2,1,0:T(8,128)} %own_hbm.1), channel_id=1, source_target_pairs={{0,4},{4,0},{8,12},{12,8},{16,20},{20,16},{24,28},{28,24},{1,5},{5... | collective-permute-start | bytes 1179656 | tf_op jit(solution)/shard_map/ppermute | solution.py:382
  4.5 2.4 %collective-permute-start.9 = (f32[4,6,32,128]{3,2,1,0:T(8,128)}, f32[4,6,32,128]{3,2,1,0:T(8,128)S(1)}, u32[]{:S(2)}, u32[]{:S(2)}) collective-permute-start(f32[4,6,32,128]{3,2,1,0:T(8,128)} %own_hbm.1), channel_id=1, source_target_pairs={{4,8},{8,4},{12,16},{16,12},{20,24},{24,20},{28,0},{0,28},{5,9},{9... | collective-permute-start | bytes 1179656 | tf_op jit(solution)/shard_map/ppermute | solution.py:382
  7.6 0.0 copy-start.1
  7.6 0.6 %copy-done.1 = s32[4]{0:T(128)S(1)} copy-done((s32[4]{0:T(128)S(1)}, s32[4]{0:T(128)}, u32[]{:S(2)}) %copy-start.1) | copy-done | bytes 40
  8.3 0.1 pad_add_fusion.info_ref
  8.4 0.0 collective-permute-done.6
  8.4 0.9 %broadcast_select_fusion.2.flow_ref = f32[1,9,32,128]{3,2,1,0:T(8,128)S(1)} fusion(f32[1,9,32,128]{3,2,1,0:T(8,128)} %param.9, f32[1,9,32,128]{3,2,1,0:T(8,128)S(1)} %collective-permute-done.6, pred[]{:T(512)S(6)} %eq.20), kind=kLoop, calls=%fused_computation.15 | loop fusion | flops 36864 | bytes 442369 | tf_op jit(solution)/shard_map/jit(_where)/select_n | solution.py:398
  9.3 1.2 %pack_edges.1 = f32[9,8,128]{2,1,0:T(8,128)S(1)} custom-call(f32[4,6,32,128]{3,2,1,0:T(8,128)} %own_hbm.1, f32[1,9,32,128]{3,2,1,0:T(8,128)S(1)} %broadcast_select_fusion.2.flow_ref), custom_call_target="tpu_custom_call" | custom-call | flops 1000000000 | bytes 100000000 | tf_op jit(solution)/shard_map/pack_edges/pallas_call | solution.py:412
  10.6 12.3 %conditional.2 = (f32[39,8,128]{2,1,0:T(8,128)S(1)}, f32[2,6,8,128]{3,2,1,0:T(8,128)S(1)}) conditional(s32[]{:T(128)} %convert_element_type.6, () %tuple.24, (s32[]{:T(128)}, f32[1,9,32,128]{3,2,1,0:T(8,128)S(1)}, s32[]{:T(128)}, f32[9,8,128]{2,1,0:T(8,128)S(1)}) %tuple.25), branch_computations={%region_0.1_spmd, %region_1.2_spmd} | conditional | flops 163600 | bytes 2159186 | solution.py:450
  10.6 0.2 collective-permute-start.4
  10.7 1.5 %collective-permute-start.3 = (f32[9,8,128]{2,1,0:T(8,128)S(1)}, f32[9,8,128]{2,1,0:T(8,128)S(1)}, u32[]{:S(2)}, u32[]{:S(2)}) collective-permute-start(f32[9,8,128]{2,1,0:T(8,128)S(1)} %get-tuple-element.20), channel_id=1, source_target_pairs={{0,1},{1,0},{2,3},{3,2},{4,5},{5,4},{6,7},{7,6},{8,9},{9,8},{10,11... | collective-permute-start | bytes 110600 | tf_op jit(solution)/shard_map/cond/branch_1_fun/ppermute | solution.py:391
  12.2 2.1 %collective-permute-start.2 = (f32[1,9,32,128]{3,2,1,0:T(8,128)S(1)}, f32[1,9,32,128]{3,2,1,0:T(8,128)S(1)}, u32[]{:S(2)}, u32[]{:S(2)}) collective-permute-start(f32[1,9,32,128]{3,2,1,0:T(8,128)S(1)} %get-tuple-element.21), channel_id=1, source_target_pairs={{0,16},{4,20},{8,24},{12,28},{16,0},{20,4},{24,8},{28,12},{1,17},{... | collective-permute-start | bytes 442376 | tf_op jit(solution)/shard_map/cond/branch_1_fun/ppermute | solution.py:385
  14.3 0.0 collective-permute-done.4
  14.4 0.0 collective-permute-done.3
  14.4 2.1 %collective-permute-start.5 = (f32[3,8,128]{2,1,0:T(8,128)S(1)}, f32[3,8,128]{2,1,0:T(8,128)S(1)}, u32[]{:S(2)}, u32[]{:S(2)}) collective-permute-start(f32[3,8,128]{2,1,0:T(8,128)S(1)} %slice_select_fusion.2), channel_id=1, source_target_pairs={{0,16},{4,20},{8,24},{12,28},{16,0},{20,4},{24,8},{28,12},{1,17},{... | collective-permute-start | bytes 36872 | tf_op jit(solution)/shard_map/cond/branch_1_fun/ppermute | solution.py:385
  16.5 6.3 %collective-permute-done.5 = f32[3,8,128]{2,1,0:T(8,128)S(1)} collective-permute-done((f32[3,8,128]{2,1,0:T(8,128)S(1)}, f32[3,8,128]{2,1,0:T(8,128)S(1)}, u32[]{:S(2)}, u32[]{:S(2)}) %collective-permute-start.5) | collective-permute-done | bytes 12320 | tf_op jit(solution)/shard_map/cond/branch_1_fun/ppermute | solution.py:385
  22.8 0.0 collective-permute-done.2
  22.9 3.3 %collective-permute-start.7 = (f32[39,8,128]{2,1,0:T(8,128)S(1)}, f32[39,8,128]{2,1,0:T(8,128)S(1)}, u32[]{:S(2)}, u32[]{:S(2)}) collective-permute-start(f32[39,8,128]{2,1,0:T(8,128)S(1)} %get-tuple-element.36.flow_ref), channel_id=1, source_target_pairs={{0,4},{4,0},{8,12},{12,8},{16,20},{20,16},{24,28},{28,24},{1,5},{5... | collective-permute-start | bytes 479240 | tf_op jit(solution)/shard_map/ppermute | solution.py:385
  26.2 0.0 collective-permute-done.8.pair_hbm
  26.2 0.0 collective-permute-done.9.other_hbm
  26.2 0.0 copy-start
  26.2 5.2 %conditional.3 = (f32[2,6,8,128]{3,2,1,0:T(8,128)}, f32[2,6,8,128]{3,2,1,0:T(8,128)}, f32[2,6,8,128]{3,2,1,0:T(8,128)}) conditional(s32[]{:T(128)} %convert_element_type.7, () %tuple.26, (f32[4,6,32,128]{3,2,1,0:T(8,128)S(1)}, f32[4,6,32,128]{3,2,1,0:T(8,128)S(1)}) %tuple.27), branch_computations={%region_2.3_spmd, %region_3.4_spmd} | conditional | flops 8 | bytes 393328 | solution.py:452
  26.2 0.9 %pack_field_edges.1 = f32[2,6,8,128]{3,2,1,0:T(8,128)} custom-call(f32[4,6,32,128]{3,2,1,0:T(8,128)S(1)} %get-tuple-element.25.pair_ref, f32[4,6,32,128]{3,2,1,0:T(8,128)S(1)} %get-tuple-element.26.other_ref), custom_call_target="tpu_custom_call" | custom-call | flops 8 | bytes 8 | tf_op jit(solution)/shard_map/cond/branch_1_fun/pack_field_edges/pallas_call | solution.py:442
  27.1 0.9 %collective-permute-start.1 = (f32[2,6,8,128]{3,2,1,0:T(8,128)}, f32[2,6,8,128]{3,2,1,0:T(8,128)}, u32[]{:S(2)}, u32[]{:S(2)}) collective-permute-start(f32[2,6,8,128]{3,2,1,0:T(8,128)} %pack_field_edges.1), channel_id=1, source_target_pairs={{1,2},{2,1},{3,0},{0,3},{5,6},{6,5},{7,4},{4,7},{9,10},{10,9},{11,... | collective-permute-start | bytes 147464 | tf_op jit(solution)/shard_map/cond/branch_1_fun/ppermute | solution.py:391
  28.0 0.7 %collective-permute-start = (f32[2,6,8,128]{3,2,1,0:T(8,128)}, f32[2,6,8,128]{3,2,1,0:T(8,128)}, u32[]{:S(2)}, u32[]{:S(2)}) collective-permute-start(f32[2,6,8,128]{3,2,1,0:T(8,128)} %pack_field_edges.1), channel_id=1, source_target_pairs={{0,1},{1,0},{2,3},{3,2},{4,5},{5,4},{6,7},{7,6},{8,9},{9,8},{10,11... | collective-permute-start | bytes 147464 | tf_op jit(solution)/shard_map/cond/branch_1_fun/ppermute | solution.py:391
  28.7 2.7 %collective-permute-done.1 = f32[2,6,8,128]{3,2,1,0:T(8,128)} collective-permute-done((f32[2,6,8,128]{3,2,1,0:T(8,128)}, f32[2,6,8,128]{3,2,1,0:T(8,128)}, u32[]{:S(2)}, u32[]{:S(2)}) %collective-permute-start.1) | collective-permute-done | bytes 49184 | tf_op jit(solution)/shard_map/cond/branch_1_fun/ppermute | solution.py:391
  31.4 0.0 collective-permute-done
  31.4 0.0 collective-permute-done.7.flow2_ref
  31.4 0.0 copy-done
  31.4 6.4 %heun_steps.1 = f32[4,6,32,128]{3,2,1,0:T(8,128)} custom-call(s32[4]{0:T(128)S(1)} %pad_add_fusion.info_ref, f32[39,8,128]{2,1,0:T(8,128)S(1)} %get-tuple-element.36.flow_ref, f32[39,8,128]{2,1,0:T(8,128)S(1)} %collective-permute-done.7.flow2_ref, f32[2,6,8,128]{3,2,1,0:T(8,128)S(1)} %get-tuple-element.37.strips_ref, ...), custom_call_target="tpu_custom_call" | custom-call | tf_op jit(solution)/shard_map/heun_steps/pallas_call | solution.py:453
  (10 shorter events, 0.1 us)
Async XLA Ops:
  0.0 8.4 %collective-permute-start.6 = (f32[1,9,32,128]{3,2,1,0:T(8,128)}, f32[1,9,32,128]{3,2,1,0:T(8,128)S(1)}, u32[]{:S(2)}, u32[]{:S(2)}) collective-permute-start(f32[1,9,32,128]{3,2,1,0:T(8,128)} %param.9), channel_id=1, source_target_pairs={{0,8},{4,12},{8,0},{12,4},{16,24},{20,28},{24,16},{28,20},{1,9},{5... | collective-permute-start | bytes 442376 | tf_op jit(solution)/shard_map/ppermute | solution.py:385
  3.0 23.2 %collective-permute-start.8 = (f32[4,6,32,128]{3,2,1,0:T(8,128)}, f32[4,6,32,128]{3,2,1,0:T(8,128)S(1)}, u32[]{:S(2)}, u32[]{:S(2)}) collective-permute-start(f32[4,6,32,128]{3,2,1,0:T(8,128)} %own_hbm.1), channel_id=1, source_target_pairs={{0,4},{4,0},{8,12},{12,8},{16,20},{20,16},{24,28},{28,24},{1,5},{5... | collective-permute-start | bytes 1179656 | tf_op jit(solution)/shard_map/ppermute | solution.py:382
  4.5 21.7 %collective-permute-start.9 = (f32[4,6,32,128]{3,2,1,0:T(8,128)}, f32[4,6,32,128]{3,2,1,0:T(8,128)S(1)}, u32[]{:S(2)}, u32[]{:S(2)}) collective-permute-start(f32[4,6,32,128]{3,2,1,0:T(8,128)} %own_hbm.1), channel_id=1, source_target_pairs={{4,8},{8,4},{12,16},{16,12},{20,24},{24,20},{28,0},{0,28},{5,9},{9... | collective-permute-start | bytes 1179656 | tf_op jit(solution)/shard_map/ppermute | solution.py:382
  7.6 0.7 %copy-start.1 = (s32[4]{0:T(128)S(1)}, s32[4]{0:T(128)}, u32[]{:S(2)}) copy-start(s32[4]{0:T(128)} %param.10) | copy-start | bytes 52
  10.6 3.8 %collective-permute-start.4 = (f32[9,8,128]{2,1,0:T(8,128)S(1)}, f32[9,8,128]{2,1,0:T(8,128)S(1)}, u32[]{:S(2)}, u32[]{:S(2)}) collective-permute-start(f32[9,8,128]{2,1,0:T(8,128)S(1)} %get-tuple-element.20), channel_id=1, source_target_pairs={{1,2},{2,1},{3,0},{0,3},{5,6},{6,5},{7,4},{4,7},{9,10},{10,9},{11,... | collective-permute-start | bytes 110600 | tf_op jit(solution)/shard_map/cond/branch_1_fun/ppermute | solution.py:391
  10.7 3.6 %collective-permute-start.3 = (f32[9,8,128]{2,1,0:T(8,128)S(1)}, f32[9,8,128]{2,1,0:T(8,128)S(1)}, u32[]{:S(2)}, u32[]{:S(2)}) collective-permute-start(f32[9,8,128]{2,1,0:T(8,128)S(1)} %get-tuple-element.20), channel_id=1, source_target_pairs={{0,1},{1,0},{2,3},{3,2},{4,5},{5,4},{6,7},{7,6},{8,9},{9,8},{10,11... | collective-permute-start | bytes 110600 | tf_op jit(solution)/shard_map/cond/branch_1_fun/ppermute | solution.py:391
  12.2 10.6 %collective-permute-start.2 = (f32[1,9,32,128]{3,2,1,0:T(8,128)S(1)}, f32[1,9,32,128]{3,2,1,0:T(8,128)S(1)}, u32[]{:S(2)}, u32[]{:S(2)}) collective-permute-start(f32[1,9,32,128]{3,2,1,0:T(8,128)S(1)} %get-tuple-element.21), channel_id=1, source_target_pairs={{0,16},{4,20},{8,24},{12,28},{16,0},{20,4},{24,8},{28,12},{1,17},{... | collective-permute-start | bytes 442376 | tf_op jit(solution)/shard_map/cond/branch_1_fun/ppermute | solution.py:385
  14.4 8.4 %collective-permute-start.5 = (f32[3,8,128]{2,1,0:T(8,128)S(1)}, f32[3,8,128]{2,1,0:T(8,128)S(1)}, u32[]{:S(2)}, u32[]{:S(2)}) collective-permute-start(f32[3,8,128]{2,1,0:T(8,128)S(1)} %slice_select_fusion.2), channel_id=1, source_target_pairs={{0,16},{4,20},{8,24},{12,28},{16,0},{20,4},{24,8},{28,12},{1,17},{... | collective-permute-start | bytes 36872 | tf_op jit(solution)/shard_map/cond/branch_1_fun/ppermute | solution.py:385
  22.9 8.6 %collective-permute-start.7 = (f32[39,8,128]{2,1,0:T(8,128)S(1)}, f32[39,8,128]{2,1,0:T(8,128)S(1)}, u32[]{:S(2)}, u32[]{:S(2)}) collective-permute-start(f32[39,8,128]{2,1,0:T(8,128)S(1)} %get-tuple-element.36.flow_ref), channel_id=1, source_target_pairs={{0,4},{4,0},{8,12},{12,8},{16,20},{20,16},{24,28},{28,24},{1,5},{5... | collective-permute-start | bytes 479240 | tf_op jit(solution)/shard_map/ppermute | solution.py:385
  26.2 5.2 %copy-start = (f32[4,6,32,128]{3,2,1,0:T(8,128)S(1)}, f32[4,6,32,128]{3,2,1,0:T(8,128)}, u32[]{:S(2)}) copy-start(f32[4,6,32,128]{3,2,1,0:T(8,128)} %own_hbm.1) | copy-start | bytes 1179652
  27.1 4.3 %collective-permute-start.1 = (f32[2,6,8,128]{3,2,1,0:T(8,128)}, f32[2,6,8,128]{3,2,1,0:T(8,128)}, u32[]{:S(2)}, u32[]{:S(2)}) collective-permute-start(f32[2,6,8,128]{3,2,1,0:T(8,128)} %pack_field_edges.1), channel_id=1, source_target_pairs={{1,2},{2,1},{3,0},{0,3},{5,6},{6,5},{7,4},{4,7},{9,10},{10,9},{11,... | collective-permute-start | bytes 147464 | tf_op jit(solution)/shard_map/cond/branch_1_fun/ppermute | solution.py:391
  28.0 3.5 %collective-permute-start = (f32[2,6,8,128]{3,2,1,0:T(8,128)}, f32[2,6,8,128]{3,2,1,0:T(8,128)}, u32[]{:S(2)}, u32[]{:S(2)}) collective-permute-start(f32[2,6,8,128]{3,2,1,0:T(8,128)} %pack_field_edges.1), channel_id=1, source_target_pairs={{0,1},{1,0},{2,3},{3,2},{4,5},{5,4},{6,7},{7,6},{8,9},{9,8},{10,11... | collective-permute-start | bytes 147464 | tf_op jit(solution)/shard_map/cond/branch_1_fun/ppermute | solution.py:391

commit v7 on v6

--- a/solution.py
+++ b/solution.py
@@ -158,15 +158,11 @@
     lane8 = lane_index()
     column8 = lane8 % 8
     zeros = jnp.zeros((8, 128), f32)
-    for array in (state, trial):
-
-        def clear(k, carry, array=array):
+    for array, slots in ((state, range(1, 11)), (trial, range(2, 10))):
+        for k in slots:
             for i in range(6):
                 array[k, i, 0:PAD, :] = zeros
                 array[k, i, PAD + 32 : PAD + 40, :] = zeros
-            return carry
-
-        lax.fori_loop(0, SLOTS, clear, 0)
     for array in (strip, strip_trial, emfs_strip, emfs):
         for side in range(2):
             for i in range(array.shape[1]):
@@ -198,18 +194,16 @@
                 strip[side, comp, tile_rows(zt), :] = jnp.where(lane8 < 96, value, 0.0)
 
     near = jnp.where(column8 < 4, 124 + column8, column8 - 4)
-    for source, wanted in ((flow_ref, 0), (flow2_ref, 1)):
-
-        @pl.when(jnp.where(take == 0, 0, 1) == wanted)
-        def _(source=source):
-            for r in range(9):
-                for zt in range(4):
-                    at = slice(8 * zt, 8 * zt + 8)
-                    flow[r, at] = source[4 * r + zt]
-                    inside = jnp.take_along_axis(source[4 * r + zt], near, axis=1)
-                    outside = jnp.take_along_axis(source[36 + r // 4], 32 * (r % 4) + 8 * zt + column8, axis=1)
-                    flow_strip[0, r, at] = jnp.where(column8 < 4, outside, inside)
-                    flow_strip[1, r, at] = jnp.where(column8 < 4, inside, outside)
+    halos = [jnp.where(take == 0, flow_ref[36 + block], flow2_ref[36 + block]) for block in range(3)]
+    for r in range(9):
+        for zt in range(4):
+            at = slice(8 * zt, 8 * zt + 8)
+            value = jnp.where(take == 0, flow_ref[4 * r + zt], flow2_ref[4 * r + zt])
+            flow[r, at] = value
+            inside = jnp.take_along_axis(value, near, axis=1)
+            outside = jnp.take_along_axis(halos[r // 4], 32 * (r % 4) + 8 * zt + column8, axis=1)
+            flow_strip[0, r, at] = jnp.where(column8 < 4, outside, inside)
+            flow_strip[1, r, at] = jnp.where(column8 < 4, inside, outside)
 
     def strips_eval(source, store):
         places = [(side, zt) for side in range(2) for zt in range(4)]

time: 38.1 us -> 37.7 us (0.990)
  other arithmetic: 1.1 us -> 0.19 us
  waiting for transfers between devices: 9.02 us -> 9.92 us
    select_n x3, other arithmetic: 0.96 us -> 0.05 us  [choose(): return jnp.where(jnp.bitwise_and(away, bit) == 0, x, y)]
    ppermute x4, waiting for transfers between devices: 6.28 us -> 7.19 us  [across(): return lax.ppermute(x, 'mode', [(i, i ^ bit) for i in range(groups)])]
  transfers between devices with their start and end apart: 10 -> 10, of which waited for: 2 -> 2; matrix products, arithmetic and copies ran while one was open for 3% -> 1% of each run, Pallas kernels for 6% -> 6%
where the time goes in v7:
time: 37.7 us; the launch traced here: 37.5 us
  starting transfers between devices  17.7 us (47%)
  waiting for transfers between devices  9.92 us (26%)
  Pallas kernels  8.14 us (22%)
  between operations  0.75 us (2%)
  local copies, waits for them, and re-layouts  0.65 us (2%)
    ppermute x4, starting transfers between devices, across(): return lax.ppermute(x, 'mode', [(i, i ^ bit) for i in range(groups)])  10.5 us
    ppermute x4, waiting for transfers between devices, across(): return lax.ppermute(x, 'mode', [(i, i ^ bit) for i in range(groups)])  7.19 us
    pallas_call x1, Pallas kernels, body(): steps_call(functools.partial(steps_kernel, modes, tiles))  6.04 us
    ppermute x2, starting transfers between devices, to_pair(): return lax.ppermute(x, 'mode', pairs)  3.94 us
    ppermute x4, starting transfers between devices, to_tile(): return lax.ppermute(x, 'tile', pairs)  3.28 us
    ppermute x4, waiting for transfers between devices, to_tile(): return lax.ppermute(x, 'tile', pairs)  2.73 us
    pallas_call x1, Pallas kernels, body(): small_kernel(pack_kernel, 'pack_edges', shape(9, 8, 128), [VMEM] * 2, LONG)  1.2 us
    pallas_call x1, Pallas kernels, neighbours(): small_kernel(pack_fields_kernel, 'pack_field_edges', shape(2, 6, 8, 128),...  0.9 us
  transfers between devices with their start and end apart: 10, of which 2 were waited for; matrix products, arithmetic and copies ran while one was open for 1% of the time, Pallas kernels for 6%

profile of v7, /device:TPU:0, one launch (start us, length us, event | category | flops | bytes accessed | tf_op | source)
XLA Modules:
  0.0 37.5 jit_solution(10183960035683011470)
XLA Ops:
  0.0 3.0 %collective-permute-start.6 = (f32[1,9,32,128]{3,2,1,0:T(8,128)}, f32[1,9,32,128]{3,2,1,0:T(8,128)S(1)}, u32[]{:S(2)}, u32[]{:S(2)}) collective-permute-start(f32[1,9,32,128]{3,2,1,0:T(8,128)} %param.9), channel_id=1, source_target_pairs={{0,8},{4,12},{8,0},{12,4},{16,24},{20,28},{24,16},{28,20},{1,9},{5... | collective-permute-start | bytes 442376 | tf_op jit(solution)/shard_map/ppermute | solution.py:379
  3.0 1.5 %collective-permute-start.8 = (f32[4,6,32,128]{3,2,1,0:T(8,128)}, f32[4,6,32,128]{3,2,1,0:T(8,128)S(1)}, u32[]{:S(2)}, u32[]{:S(2)}) collective-permute-start(f32[4,6,32,128]{3,2,1,0:T(8,128)} %own_hbm.1), channel_id=1, source_target_pairs={{0,4},{4,0},{8,12},{12,8},{16,20},{20,16},{24,28},{28,24},{1,5},{5... | collective-permute-start | bytes 1179656 | tf_op jit(solution)/shard_map/ppermute | solution.py:376
  4.5 2.4 %collective-permute-start.9 = (f32[4,6,32,128]{3,2,1,0:T(8,128)}, f32[4,6,32,128]{3,2,1,0:T(8,128)S(1)}, u32[]{:S(2)}, u32[]{:S(2)}) collective-permute-start(f32[4,6,32,128]{3,2,1,0:T(8,128)} %own_hbm.1), channel_id=1, source_target_pairs={{4,8},{8,4},{12,16},{16,12},{20,24},{24,20},{28,0},{0,28},{5,9},{9... | collective-permute-start | bytes 1179656 | tf_op jit(solution)/shard_map/ppermute | solution.py:376
  7.6 0.0 copy-start.1
  7.6 0.6 %copy-done.1 = s32[4]{0:T(128)S(1)} copy-done((s32[4]{0:T(128)S(1)}, s32[4]{0:T(128)}, u32[]{:S(2)}) %copy-start.1) | copy-done | bytes 40
  8.3 0.1 pad_add_fusion.info_ref
  8.4 0.0 collective-permute-done.6
  8.4 1.2 %pack_edges.1 = f32[9,8,128]{2,1,0:T(8,128)S(1)} custom-call(f32[4,6,32,128]{3,2,1,0:T(8,128)} %own_hbm.1, f32[1,9,32,128]{3,2,1,0:T(8,128)S(1)} %broadcast_select_fusion.2.flow_ref), custom_call_target="tpu_custom_call" | custom-call | flops 1000000000 | bytes 100000000 | tf_op jit(solution)/shard_map/pack_edges/pallas_call | solution.py:406
  9.6 13.2 %conditional.2 = (f32[39,8,128]{2,1,0:T(8,128)S(1)}, f32[2,6,8,128]{3,2,1,0:T(8,128)S(1)}) conditional(s32[]{:T(128)} %convert_element_type.6, () %tuple.24, (s32[]{:T(128)}, f32[1,9,32,128]{3,2,1,0:T(8,128)S(1)}, s32[]{:T(128)}, f32[9,8,128]{2,1,0:T(8,128)S(1)}) %tuple.25), branch_computations={%region_0.1_spmd, %region_1.2_spmd} | conditional | flops 163600 | bytes 2159186 | solution.py:444
  9.7 0.2 collective-permute-start.4
  9.8 1.5 %collective-permute-start.3 = (f32[9,8,128]{2,1,0:T(8,128)S(1)}, f32[9,8,128]{2,1,0:T(8,128)S(1)}, u32[]{:S(2)}, u32[]{:S(2)}) collective-permute-start(f32[9,8,128]{2,1,0:T(8,128)S(1)} %get-tuple-element.20), channel_id=1, source_target_pairs={{0,1},{1,0},{2,3},{3,2},{4,5},{5,4},{6,7},{7,6},{8,9},{9,8},{10,11... | collective-permute-start | bytes 110600 | tf_op jit(solution)/shard_map/cond/branch_1_fun/ppermute | solution.py:385
  11.3 2.1 %collective-permute-start.2 = (f32[1,9,32,128]{3,2,1,0:T(8,128)S(1)}, f32[1,9,32,128]{3,2,1,0:T(8,128)S(1)}, u32[]{:S(2)}, u32[]{:S(2)}) collective-permute-start(f32[1,9,32,128]{3,2,1,0:T(8,128)S(1)} %get-tuple-element.21), channel_id=1, source_target_pairs={{0,16},{4,20},{8,24},{12,28},{16,0},{20,4},{24,8},{28,12},{1,17},{... | collective-permute-start | bytes 442376 | tf_op jit(solution)/shard_map/cond/branch_1_fun/ppermute | solution.py:379
  13.4 0.0 collective-permute-done.4
  13.5 0.0 collective-permute-done.3
  13.5 2.1 %collective-permute-start.5 = (f32[3,8,128]{2,1,0:T(8,128)S(1)}, f32[3,8,128]{2,1,0:T(8,128)S(1)}, u32[]{:S(2)}, u32[]{:S(2)}) collective-permute-start(f32[3,8,128]{2,1,0:T(8,128)S(1)} %slice_select_fusion.2), channel_id=1, source_target_pairs={{0,16},{4,20},{8,24},{12,28},{16,0},{20,4},{24,8},{28,12},{1,17},{... | collective-permute-start | bytes 36872 | tf_op jit(solution)/shard_map/cond/branch_1_fun/ppermute | solution.py:379
  15.6 7.2 %collective-permute-done.5 = f32[3,8,128]{2,1,0:T(8,128)S(1)} collective-permute-done((f32[3,8,128]{2,1,0:T(8,128)S(1)}, f32[3,8,128]{2,1,0:T(8,128)S(1)}, u32[]{:S(2)}, u32[]{:S(2)}) %collective-permute-start.5) | collective-permute-done | bytes 12320 | tf_op jit(solution)/shard_map/cond/branch_1_fun/ppermute | solution.py:379
  22.8 0.0 collective-permute-done.2
  22.9 3.3 %collective-permute-start.7 = (f32[39,8,128]{2,1,0:T(8,128)S(1)}, f32[39,8,128]{2,1,0:T(8,128)S(1)}, u32[]{:S(2)}, u32[]{:S(2)}) collective-permute-start(f32[39,8,128]{2,1,0:T(8,128)S(1)} %get-tuple-element.36.flow_ref), channel_id=1, source_target_pairs={{0,4},{4,0},{8,12},{12,8},{16,20},{20,16},{24,28},{28,24},{1,5},{5... | collective-permute-start | bytes 479240 | tf_op jit(solution)/shard_map/ppermute | solution.py:379
  26.2 0.0 collective-permute-done.8.pair_hbm
  26.2 0.0 collective-permute-done.9.other_hbm
  26.2 0.0 copy-start
  26.2 5.2 %conditional.3 = (f32[2,6,8,128]{3,2,1,0:T(8,128)}, f32[2,6,8,128]{3,2,1,0:T(8,128)}, f32[2,6,8,128]{3,2,1,0:T(8,128)}) conditional(s32[]{:T(128)} %convert_element_type.7, () %tuple.26, (f32[4,6,32,128]{3,2,1,0:T(8,128)S(1)}, f32[4,6,32,128]{3,2,1,0:T(8,128)S(1)}) %tuple.27), branch_computations={%region_2.3_spmd, %region_3.4_spmd} | conditional | flops 8 | bytes 393328 | solution.py:446
  26.2 0.9 %pack_field_edges.1 = f32[2,6,8,128]{3,2,1,0:T(8,128)} custom-call(f32[4,6,32,128]{3,2,1,0:T(8,128)S(1)} %get-tuple-element.25.pair_ref, f32[4,6,32,128]{3,2,1,0:T(8,128)S(1)} %get-tuple-element.26.other_ref), custom_call_target="tpu_custom_call" | custom-call | flops 8 | bytes 8 | tf_op jit(solution)/shard_map/cond/branch_1_fun/pack_field_edges/pallas_call | solution.py:436
  27.1 0.9 %collective-permute-start.1 = (f32[2,6,8,128]{3,2,1,0:T(8,128)}, f32[2,6,8,128]{3,2,1,0:T(8,128)}, u32[]{:S(2)}, u32[]{:S(2)}) collective-permute-start(f32[2,6,8,128]{3,2,1,0:T(8,128)} %pack_field_edges.1), channel_id=1, source_target_pairs={{1,2},{2,1},{3,0},{0,3},{5,6},{6,5},{7,4},{4,7},{9,10},{10,9},{11,... | collective-permute-start | bytes 147464 | tf_op jit(solution)/shard_map/cond/branch_1_fun/ppermute | solution.py:385
  28.0 0.7 %collective-permute-start = (f32[2,6,8,128]{3,2,1,0:T(8,128)}, f32[2,6,8,128]{3,2,1,0:T(8,128)}, u32[]{:S(2)}, u32[]{:S(2)}) collective-permute-start(f32[2,6,8,128]{3,2,1,0:T(8,128)} %pack_field_edges.1), channel_id=1, source_target_pairs={{0,1},{1,0},{2,3},{3,2},{4,5},{5,4},{6,7},{7,6},{8,9},{9,8},{10,11... | collective-permute-start | bytes 147464 | tf_op jit(solution)/shard_map/cond/branch_1_fun/ppermute | solution.py:385
  28.7 2.7 %collective-permute-done.1 = f32[2,6,8,128]{3,2,1,0:T(8,128)} collective-permute-done((f32[2,6,8,128]{3,2,1,0:T(8,128)}, f32[2,6,8,128]{3,2,1,0:T(8,128)}, u32[]{:S(2)}, u32[]{:S(2)}) %collective-permute-start.1) | collective-permute-done | bytes 49184 | tf_op jit(solution)/shard_map/cond/branch_1_fun/ppermute | solution.py:385
  31.4 0.0 collective-permute-done
  31.4 0.0 collective-permute-done.7.flow2_ref
  31.4 0.0 copy-done
  31.4 6.0 %heun_steps.1 = f32[4,6,32,128]{3,2,1,0:T(8,128)} custom-call(s32[4]{0:T(128)S(1)} %pad_add_fusion.info_ref, f32[39,8,128]{2,1,0:T(8,128)S(1)} %get-tuple-element.36.flow_ref, f32[39,8,128]{2,1,0:T(8,128)S(1)} %collective-permute-done.7.flow2_ref, f32[2,6,8,128]{3,2,1,0:T(8,128)S(1)} %get-tuple-element.37.strips_ref, ...), custom_call_target="tpu_custom_call" | custom-call | tf_op jit(solution)/shard_map/heun_steps/pallas_call | solution.py:447
  (11 shorter events, 0.1 us)
Async XLA Ops:
  0.0 8.4 %collective-permute-start.6 = (f32[1,9,32,128]{3,2,1,0:T(8,128)}, f32[1,9,32,128]{3,2,1,0:T(8,128)S(1)}, u32[]{:S(2)}, u32[]{:S(2)}) collective-permute-start(f32[1,9,32,128]{3,2,1,0:T(8,128)} %param.9), channel_id=1, source_target_pairs={{0,8},{4,12},{8,0},{12,4},{16,24},{20,28},{24,16},{28,20},{1,9},{5... | collective-permute-start | bytes 442376 | tf_op jit(solution)/shard_map/ppermute | solution.py:379
  3.0 23.2 %collective-permute-start.8 = (f32[4,6,32,128]{3,2,1,0:T(8,128)}, f32[4,6,32,128]{3,2,1,0:T(8,128)S(1)}, u32[]{:S(2)}, u32[]{:S(2)}) collective-permute-start(f32[4,6,32,128]{3,2,1,0:T(8,128)} %own_hbm.1), channel_id=1, source_target_pairs={{0,4},{4,0},{8,12},{12,8},{16,20},{20,16},{24,28},{28,24},{1,5},{5... | collective-permute-start | bytes 1179656 | tf_op jit(solution)/shard_map/ppermute | solution.py:376
  4.5 21.7 %collective-permute-start.9 = (f32[4,6,32,128]{3,2,1,0:T(8,128)}, f32[4,6,32,128]{3,2,1,0:T(8,128)S(1)}, u32[]{:S(2)}, u32[]{:S(2)}) collective-permute-start(f32[4,6,32,128]{3,2,1,0:T(8,128)} %own_hbm.1), channel_id=1, source_target_pairs={{4,8},{8,4},{12,16},{16,12},{20,24},{24,20},{28,0},{0,28},{5,9},{9... | collective-permute-start | bytes 1179656 | tf_op jit(solution)/shard_map/ppermute | solution.py:376
  7.6 0.7 %copy-start.1 = (s32[4]{0:T(128)S(1)}, s32[4]{0:T(128)}, u32[]{:S(2)}) copy-start(s32[4]{0:T(128)} %param.10) | copy-start | bytes 52
  9.7 3.8 %collective-permute-start.4 = (f32[9,8,128]{2,1,0:T(8,128)S(1)}, f32[9,8,128]{2,1,0:T(8,128)S(1)}, u32[]{:S(2)}, u32[]{:S(2)}) collective-permute-start(f32[9,8,128]{2,1,0:T(8,128)S(1)} %get-tuple-element.20), channel_id=1, source_target_pairs={{1,2},{2,1},{3,0},{0,3},{5,6},{6,5},{7,4},{4,7},{9,10},{10,9},{11,... | collective-permute-start | bytes 110600 | tf_op jit(solution)/shard_map/cond/branch_1_fun/ppermute | solution.py:385
  9.8 3.6 %collective-permute-start.3 = (f32[9,8,128]{2,1,0:T(8,128)S(1)}, f32[9,8,128]{2,1,0:T(8,128)S(1)}, u32[]{:S(2)}, u32[]{:S(2)}) collective-permute-start(f32[9,8,128]{2,1,0:T(8,128)S(1)} %get-tuple-element.20), channel_id=1, source_target_pairs={{0,1},{1,0},{2,3},{3,2},{4,5},{5,4},{6,7},{7,6},{8,9},{9,8},{10,11... | collective-permute-start | bytes 110600 | tf_op jit(solution)/shard_map/cond/branch_1_fun/ppermute | solution.py:385
  11.3 11.5 %collective-permute-start.2 = (f32[1,9,32,128]{3,2,1,0:T(8,128)S(1)}, f32[1,9,32,128]{3,2,1,0:T(8,128)S(1)}, u32[]{:S(2)}, u32[]{:S(2)}) collective-permute-start(f32[1,9,32,128]{3,2,1,0:T(8,128)S(1)} %get-tuple-element.21), channel_id=1, source_target_pairs={{0,16},{4,20},{8,24},{12,28},{16,0},{20,4},{24,8},{28,12},{1,17},{... | collective-permute-start | bytes 442376 | tf_op jit(solution)/shard_map/cond/branch_1_fun/ppermute | solution.py:379
  13.5 9.3 %collective-permute-start.5 = (f32[3,8,128]{2,1,0:T(8,128)S(1)}, f32[3,8,128]{2,1,0:T(8,128)S(1)}, u32[]{:S(2)}, u32[]{:S(2)}) collective-permute-start(f32[3,8,128]{2,1,0:T(8,128)S(1)} %slice_select_fusion.2), channel_id=1, source_target_pairs={{0,16},{4,20},{8,24},{12,28},{16,0},{20,4},{24,8},{28,12},{1,17},{... | collective-permute-start | bytes 36872 | tf_op jit(solution)/shard_map/cond/branch_1_fun/ppermute | solution.py:379
  22.9 8.6 %collective-permute-start.7 = (f32[39,8,128]{2,1,0:T(8,128)S(1)}, f32[39,8,128]{2,1,0:T(8,128)S(1)}, u32[]{:S(2)}, u32[]{:S(2)}) collective-permute-start(f32[39,8,128]{2,1,0:T(8,128)S(1)} %get-tuple-element.36.flow_ref), channel_id=1, source_target_pairs={{0,4},{4,0},{8,12},{12,8},{16,20},{20,16},{24,28},{28,24},{1,5},{5... | collective-permute-start | bytes 479240 | tf_op jit(solution)/shard_map/ppermute | solution.py:379
  26.2 5.2 %copy-start = (f32[4,6,32,128]{3,2,1,0:T(8,128)S(1)}, f32[4,6,32,128]{3,2,1,0:T(8,128)}, u32[]{:S(2)}) copy-start(f32[4,6,32,128]{3,2,1,0:T(8,128)} %own_hbm.1) | copy-start | bytes 1179652
  27.1 4.3 %collective-permute-start.1 = (f32[2,6,8,128]{3,2,1,0:T(8,128)}, f32[2,6,8,128]{3,2,1,0:T(8,128)}, u32[]{:S(2)}, u32[]{:S(2)}) collective-permute-start(f32[2,6,8,128]{3,2,1,0:T(8,128)} %pack_field_edges.1), channel_id=1, source_target_pairs={{1,2},{2,1},{3,0},{0,3},{5,6},{6,5},{7,4},{4,7},{9,10},{10,9},{11,... | collective-permute-start | bytes 147464 | tf_op jit(solution)/shard_map/cond/branch_1_fun/ppermute | solution.py:385
  28.0 3.5 %collective-permute-start = (f32[2,6,8,128]{3,2,1,0:T(8,128)}, f32[2,6,8,128]{3,2,1,0:T(8,128)}, u32[]{:S(2)}, u32[]{:S(2)}) collective-permute-start(f32[2,6,8,128]{3,2,1,0:T(8,128)} %pack_field_edges.1), channel_id=1, source_target_pairs={{0,1},{1,0},{2,3},{3,2},{4,5},{5,4},{6,7},{7,6},{8,9},{9,8},{10,11... | collective-permute-start | bytes 147464 | tf_op jit(solution)/shard_map/cond/branch_1_fun/ppermute | solution.py:385

commit v8 on v7

--- a/solution.py
+++ b/solution.py
@@ -275,10 +275,10 @@
                     store(k, i, zt, total)
 
         def two(n, carry):
-            one(start + 2 * n, 0)
-            one(start + 2 * n + 1, 1)
-            if after is not None:
-                after(n)
+            for m in range(2):
+                one(start + 2 * n + m, m)
+                if after is not None:
+                    after(2 * n + m)
             return carry
 
         for n in range((stop - start) // 2):
@@ -309,11 +309,11 @@
     main_eval(state, 3, 9, first_main)
     strips_eval(strip_trial, None)
     def writing(n):
-        done = pl.ds(2 * n, 2)
+        done = pl.ds(n, 1)
         return pltpu.make_async_copy(out.at[done], out_hbm.at[done], sems.at[n])
 
     main_eval(trial, 4, 8, last_main, lambda n: writing(n).start())
-    for n in range(GROUP // 2):
+    for n in range(GROUP):
         writing(n).wait()
 
 

time: 37.7 us -> 37.7 us (level)
  other arithmetic: 0.19 us -> 1.1 us
  waiting for transfers between devices: 9.92 us -> 9.02 us
    select_n x3, other arithmetic: 0.05 us -> 0.96 us  [choose(): return jnp.where(jnp.bitwise_and(away, bit) == 0, x, y)]
    ppermute x4, waiting for transfers between devices: 7.19 us -> 6.28 us  [across(): return lax.ppermute(x, 'mode', [(i, i ^ bit) for i in range(groups)])]
  transfers between devices with their start and end apart: 10 -> 10, of which waited for: 2 -> 2; matrix products, arithmetic and copies ran while one was open for 1% -> 3% of each run, Pallas kernels for 6% -> 6%
where the time goes in v8:
time: 37.7 us; the launch traced here: 37.5 us
  starting transfers between devices  17.7 us (47%)
  waiting for transfers between devices  9.02 us (24%)
  Pallas kernels  8.11 us (22%)
  other arithmetic  1.1 us (3%)
  between operations  0.75 us (2%)
  local copies, waits for them, and re-layouts  0.65 us (2%)
    ppermute x4, starting transfers between devices, across(): return lax.ppermute(x, 'mode', [(i, i ^ bit) for i in range(groups)])  10.5 us
    ppermute x4, waiting for transfers between devices, across(): return lax.ppermute(x, 'mode', [(i, i ^ bit) for i in range(groups)])  6.28 us
    pallas_call x1, Pallas kernels, body(): steps_call(functools.partial(steps_kernel, modes, tiles))  6.01 us
    ppermute x2, starting transfers between devices, to_pair(): return lax.ppermute(x, 'mode', pairs)  3.94 us
    ppermute x4, starting transfers between devices, to_tile(): return lax.ppermute(x, 'tile', pairs)  3.28 us
    ppermute x4, waiting for transfers between devices, to_tile(): return lax.ppermute(x, 'tile', pairs)  2.73 us
    pallas_call x1, Pallas kernels, body(): small_kernel(pack_kernel, 'pack_edges', shape(9, 8, 128), [VMEM] * 2, LONG)  1.2 us
    select_n x3, other arithmetic, choose(): return jnp.where(jnp.bitwise_and(away, bit) == 0, x, y)  0.96 us
  transfers between devices with their start and end apart: 10, of which 2 were waited for; matrix products, arithmetic and copies ran while one was open for 3% of the time, Pallas kernels for 6%

profile of v8, /device:TPU:0, one launch (start us, length us, event | category | flops | bytes accessed | tf_op | source)
XLA Modules:
  0.0 37.5 jit_solution(5271200690478349367)
XLA Ops:
  0.0 3.0 %collective-permute-start.6 = (f32[1,9,32,128]{3,2,1,0:T(8,128)}, f32[1,9,32,128]{3,2,1,0:T(8,128)S(1)}, u32[]{:S(2)}, u32[]{:S(2)}) collective-permute-start(f32[1,9,32,128]{3,2,1,0:T(8,128)} %param.9), channel_id=1, source_target_pairs={{0,8},{4,12},{8,0},{12,4},{16,24},{20,28},{24,16},{28,20},{1,9},{5... | collective-permute-start | bytes 442376 | tf_op jit(solution)/shard_map/ppermute | solution.py:379
  3.0 1.5 %collective-permute-start.8 = (f32[4,6,32,128]{3,2,1,0:T(8,128)}, f32[4,6,32,128]{3,2,1,0:T(8,128)S(1)}, u32[]{:S(2)}, u32[]{:S(2)}) collective-permute-start(f32[4,6,32,128]{3,2,1,0:T(8,128)} %own_hbm.1), channel_id=1, source_target_pairs={{0,4},{4,0},{8,12},{12,8},{16,20},{20,16},{24,28},{28,24},{1,5},{5... | collective-permute-start | bytes 1179656 | tf_op jit(solution)/shard_map/ppermute | solution.py:376
  4.5 2.4 %collective-permute-start.9 = (f32[4,6,32,128]{3,2,1,0:T(8,128)}, f32[4,6,32,128]{3,2,1,0:T(8,128)S(1)}, u32[]{:S(2)}, u32[]{:S(2)}) collective-permute-start(f32[4,6,32,128]{3,2,1,0:T(8,128)} %own_hbm.1), channel_id=1, source_target_pairs={{4,8},{8,4},{12,16},{16,12},{20,24},{24,20},{28,0},{0,28},{5,9},{9... | collective-permute-start | bytes 1179656 | tf_op jit(solution)/shard_map/ppermute | solution.py:376
  7.6 0.0 copy-start.1
  7.6 0.6 %copy-done.1 = s32[4]{0:T(128)S(1)} copy-done((s32[4]{0:T(128)S(1)}, s32[4]{0:T(128)}, u32[]{:S(2)}) %copy-start.1) | copy-done | bytes 40
  8.3 0.1 pad_add_fusion.info_ref
  8.4 0.0 collective-permute-done.6
  8.4 0.9 %broadcast_select_fusion.2.flow_ref = f32[1,9,32,128]{3,2,1,0:T(8,128)S(1)} fusion(f32[1,9,32,128]{3,2,1,0:T(8,128)} %param.9, f32[1,9,32,128]{3,2,1,0:T(8,128)S(1)} %collective-permute-done.6, pred[]{:T(512)S(6)} %eq.20), kind=kLoop, calls=%fused_computation.15 | loop fusion | flops 36864 | bytes 442369 | tf_op jit(solution)/shard_map/jit(_where)/select_n | solution.py:392
  9.3 1.2 %pack_edges.1 = f32[9,8,128]{2,1,0:T(8,128)S(1)} custom-call(f32[4,6,32,128]{3,2,1,0:T(8,128)} %own_hbm.1, f32[1,9,32,128]{3,2,1,0:T(8,128)S(1)} %broadcast_select_fusion.2.flow_ref), custom_call_target="tpu_custom_call" | custom-call | flops 1000000000 | bytes 100000000 | tf_op jit(solution)/shard_map/pack_edges/pallas_call | solution.py:406
  10.6 12.3 %conditional.2 = (f32[39,8,128]{2,1,0:T(8,128)S(1)}, f32[2,6,8,128]{3,2,1,0:T(8,128)S(1)}) conditional(s32[]{:T(128)} %convert_element_type.6, () %tuple.24, (s32[]{:T(128)}, f32[1,9,32,128]{3,2,1,0:T(8,128)S(1)}, s32[]{:T(128)}, f32[9,8,128]{2,1,0:T(8,128)S(1)}) %tuple.25), branch_computations={%region_0.1_spmd, %region_1.2_spmd} | conditional | flops 163600 | bytes 2159186 | solution.py:444
  10.6 0.2 collective-permute-start.4
  10.7 1.5 %collective-permute-start.3 = (f32[9,8,128]{2,1,0:T(8,128)S(1)}, f32[9,8,128]{2,1,0:T(8,128)S(1)}, u32[]{:S(2)}, u32[]{:S(2)}) collective-permute-start(f32[9,8,128]{2,1,0:T(8,128)S(1)} %get-tuple-element.20), channel_id=1, source_target_pairs={{0,1},{1,0},{2,3},{3,2},{4,5},{5,4},{6,7},{7,6},{8,9},{9,8},{10,11... | collective-permute-start | bytes 110600 | tf_op jit(solution)/shard_map/cond/branch_1_fun/ppermute | solution.py:385
  12.2 2.1 %collective-permute-start.2 = (f32[1,9,32,128]{3,2,1,0:T(8,128)S(1)}, f32[1,9,32,128]{3,2,1,0:T(8,128)S(1)}, u32[]{:S(2)}, u32[]{:S(2)}) collective-permute-start(f32[1,9,32,128]{3,2,1,0:T(8,128)S(1)} %get-tuple-element.21), channel_id=1, source_target_pairs={{0,16},{4,20},{8,24},{12,28},{16,0},{20,4},{24,8},{28,12},{1,17},{... | collective-permute-start | bytes 442376 | tf_op jit(solution)/shard_map/cond/branch_1_fun/ppermute | solution.py:379
  14.3 0.0 collective-permute-done.4
  14.4 0.0 collective-permute-done.3
  14.4 2.1 %collective-permute-start.5 = (f32[3,8,128]{2,1,0:T(8,128)S(1)}, f32[3,8,128]{2,1,0:T(8,128)S(1)}, u32[]{:S(2)}, u32[]{:S(2)}) collective-permute-start(f32[3,8,128]{2,1,0:T(8,128)S(1)} %slice_select_fusion.2), channel_id=1, source_target_pairs={{0,16},{4,20},{8,24},{12,28},{16,0},{20,4},{24,8},{28,12},{1,17},{... | collective-permute-start | bytes 36872 | tf_op jit(solution)/shard_map/cond/branch_1_fun/ppermute | solution.py:379
  16.5 6.3 %collective-permute-done.5 = f32[3,8,128]{2,1,0:T(8,128)S(1)} collective-permute-done((f32[3,8,128]{2,1,0:T(8,128)S(1)}, f32[3,8,128]{2,1,0:T(8,128)S(1)}, u32[]{:S(2)}, u32[]{:S(2)}) %collective-permute-start.5) | collective-permute-done | bytes 12320 | tf_op jit(solution)/shard_map/cond/branch_1_fun/ppermute | solution.py:379
  22.8 0.0 collective-permute-done.2
  22.9 3.3 %collective-permute-start.7 = (f32[39,8,128]{2,1,0:T(8,128)S(1)}, f32[39,8,128]{2,1,0:T(8,128)S(1)}, u32[]{:S(2)}, u32[]{:S(2)}) collective-permute-start(f32[39,8,128]{2,1,0:T(8,128)S(1)} %get-tuple-element.36.flow_ref), channel_id=1, source_target_pairs={{0,4},{4,0},{8,12},{12,8},{16,20},{20,16},{24,28},{28,24},{1,5},{5... | collective-permute-start | bytes 479240 | tf_op jit(solution)/shard_map/ppermute | solution.py:379
  26.2 0.0 collective-permute-done.8.pair_hbm
  26.2 0.0 collective-permute-done.9.other_hbm
  26.2 0.0 copy-start
  26.2 5.2 %conditional.3 = (f32[2,6,8,128]{3,2,1,0:T(8,128)}, f32[2,6,8,128]{3,2,1,0:T(8,128)}, f32[2,6,8,128]{3,2,1,0:T(8,128)}) conditional(s32[]{:T(128)} %convert_element_type.7, () %tuple.26, (f32[4,6,32,128]{3,2,1,0:T(8,128)S(1)}, f32[4,6,32,128]{3,2,1,0:T(8,128)S(1)}) %tuple.27), branch_computations={%region_2.3_spmd, %region_3.4_spmd} | conditional | flops 8 | bytes 393328 | solution.py:446
  26.2 0.9 %pack_field_edges.1 = f32[2,6,8,128]{3,2,1,0:T(8,128)} custom-call(f32[4,6,32,128]{3,2,1,0:T(8,128)S(1)} %get-tuple-element.25.pair_ref, f32[4,6,32,128]{3,2,1,0:T(8,128)S(1)} %get-tuple-element.26.other_ref), custom_call_target="tpu_custom_call" | custom-call | flops 8 | bytes 8 | tf_op jit(solution)/shard_map/cond/branch_1_fun/pack_field_edges/pallas_call | solution.py:436
  27.1 0.9 %collective-permute-start.1 = (f32[2,6,8,128]{3,2,1,0:T(8,128)}, f32[2,6,8,128]{3,2,1,0:T(8,128)}, u32[]{:S(2)}, u32[]{:S(2)}) collective-permute-start(f32[2,6,8,128]{3,2,1,0:T(8,128)} %pack_field_edges.1), channel_id=1, source_target_pairs={{1,2},{2,1},{3,0},{0,3},{5,6},{6,5},{7,4},{4,7},{9,10},{10,9},{11,... | collective-permute-start | bytes 147464 | tf_op jit(solution)/shard_map/cond/branch_1_fun/ppermute | solution.py:385
  28.0 0.7 %collective-permute-start = (f32[2,6,8,128]{3,2,1,0:T(8,128)}, f32[2,6,8,128]{3,2,1,0:T(8,128)}, u32[]{:S(2)}, u32[]{:S(2)}) collective-permute-start(f32[2,6,8,128]{3,2,1,0:T(8,128)} %pack_field_edges.1), channel_id=1, source_target_pairs={{0,1},{1,0},{2,3},{3,2},{4,5},{5,4},{6,7},{7,6},{8,9},{9,8},{10,11... | collective-permute-start | bytes 147464 | tf_op jit(solution)/shard_map/cond/branch_1_fun/ppermute | solution.py:385
  28.7 2.7 %collective-permute-done.1 = f32[2,6,8,128]{3,2,1,0:T(8,128)} collective-permute-done((f32[2,6,8,128]{3,2,1,0:T(8,128)}, f32[2,6,8,128]{3,2,1,0:T(8,128)}, u32[]{:S(2)}, u32[]{:S(2)}) %collective-permute-start.1) | collective-permute-done | bytes 49184 | tf_op jit(solution)/shard_map/cond/branch_1_fun/ppermute | solution.py:385
  31.4 0.0 collective-permute-done
  31.4 0.0 collective-permute-done.7.flow2_ref
  31.4 0.0 copy-done
  31.4 6.0 %heun_steps.1 = f32[4,6,32,128]{3,2,1,0:T(8,128)} custom-call(s32[4]{0:T(128)S(1)} %pad_add_fusion.info_ref, f32[39,8,128]{2,1,0:T(8,128)S(1)} %get-tuple-element.36.flow_ref, f32[39,8,128]{2,1,0:T(8,128)S(1)} %collective-permute-done.7.flow2_ref, f32[2,6,8,128]{3,2,1,0:T(8,128)S(1)} %get-tuple-element.37.strips_ref, ...), custom_call_target="tpu_custom_call" | custom-call | tf_op jit(solution)/shard_map/heun_steps/pallas_call | solution.py:447
  (10 shorter events, 0.1 us)
Async XLA Ops:
  0.0 8.4 %collective-permute-start.6 = (f32[1,9,32,128]{3,2,1,0:T(8,128)}, f32[1,9,32,128]{3,2,1,0:T(8,128)S(1)}, u32[]{:S(2)}, u32[]{:S(2)}) collective-permute-start(f32[1,9,32,128]{3,2,1,0:T(8,128)} %param.9), channel_id=1, source_target_pairs={{0,8},{4,12},{8,0},{12,4},{16,24},{20,28},{24,16},{28,20},{1,9},{5... | collective-permute-start | bytes 442376 | tf_op jit(solution)/shard_map/ppermute | solution.py:379
  3.0 23.2 %collective-permute-start.8 = (f32[4,6,32,128]{3,2,1,0:T(8,128)}, f32[4,6,32,128]{3,2,1,0:T(8,128)S(1)}, u32[]{:S(2)}, u32[]{:S(2)}) collective-permute-start(f32[4,6,32,128]{3,2,1,0:T(8,128)} %own_hbm.1), channel_id=1, source_target_pairs={{0,4},{4,0},{8,12},{12,8},{16,20},{20,16},{24,28},{28,24},{1,5},{5... | collective-permute-start | bytes 1179656 | tf_op jit(solution)/shard_map/ppermute | solution.py:376
  4.5 21.7 %collective-permute-start.9 = (f32[4,6,32,128]{3,2,1,0:T(8,128)}, f32[4,6,32,128]{3,2,1,0:T(8,128)S(1)}, u32[]{:S(2)}, u32[]{:S(2)}) collective-permute-start(f32[4,6,32,128]{3,2,1,0:T(8,128)} %own_hbm.1), channel_id=1, source_target_pairs={{4,8},{8,4},{12,16},{16,12},{20,24},{24,20},{28,0},{0,28},{5,9},{9... | collective-permute-start | bytes 1179656 | tf_op jit(solution)/shard_map/ppermute | solution.py:376
  7.6 0.7 %copy-start.1 = (s32[4]{0:T(128)S(1)}, s32[4]{0:T(128)}, u32[]{:S(2)}) copy-start(s32[4]{0:T(128)} %param.10) | copy-start | bytes 52
  10.6 3.8 %collective-permute-start.4 = (f32[9,8,128]{2,1,0:T(8,128)S(1)}, f32[9,8,128]{2,1,0:T(8,128)S(1)}, u32[]{:S(2)}, u32[]{:S(2)}) collective-permute-start(f32[9,8,128]{2,1,0:T(8,128)S(1)} %get-tuple-element.20), channel_id=1, source_target_pairs={{1,2},{2,1},{3,0},{0,3},{5,6},{6,5},{7,4},{4,7},{9,10},{10,9},{11,... | collective-permute-start | bytes 110600 | tf_op jit(solution)/shard_map/cond/branch_1_fun/ppermute | solution.py:385
  10.7 3.6 %collective-permute-start.3 = (f32[9,8,128]{2,1,0:T(8,128)S(1)}, f32[9,8,128]{2,1,0:T(8,128)S(1)}, u32[]{:S(2)}, u32[]{:S(2)}) collective-permute-start(f32[9,8,128]{2,1,0:T(8,128)S(1)} %get-tuple-element.20), channel_id=1, source_target_pairs={{0,1},{1,0},{2,3},{3,2},{4,5},{5,4},{6,7},{7,6},{8,9},{9,8},{10,11... | collective-permute-start | bytes 110600 | tf_op jit(solution)/shard_map/cond/branch_1_fun/ppermute | solution.py:385
  12.2 10.6 %collective-permute-start.2 = (f32[1,9,32,128]{3,2,1,0:T(8,128)S(1)}, f32[1,9,32,128]{3,2,1,0:T(8,128)S(1)}, u32[]{:S(2)}, u32[]{:S(2)}) collective-permute-start(f32[1,9,32,128]{3,2,1,0:T(8,128)S(1)} %get-tuple-element.21), channel_id=1, source_target_pairs={{0,16},{4,20},{8,24},{12,28},{16,0},{20,4},{24,8},{28,12},{1,17},{... | collective-permute-start | bytes 442376 | tf_op jit(solution)/shard_map/cond/branch_1_fun/ppermute | solution.py:379
  14.4 8.4 %collective-permute-start.5 = (f32[3,8,128]{2,1,0:T(8,128)S(1)}, f32[3,8,128]{2,1,0:T(8,128)S(1)}, u32[]{:S(2)}, u32[]{:S(2)}) collective-permute-start(f32[3,8,128]{2,1,0:T(8,128)S(1)} %slice_select_fusion.2), channel_id=1, source_target_pairs={{0,16},{4,20},{8,24},{12,28},{16,0},{20,4},{24,8},{28,12},{1,17},{... | collective-permute-start | bytes 36872 | tf_op jit(solution)/shard_map/cond/branch_1_fun/ppermute | solution.py:379
  22.9 8.6 %collective-permute-start.7 = (f32[39,8,128]{2,1,0:T(8,128)S(1)}, f32[39,8,128]{2,1,0:T(8,128)S(1)}, u32[]{:S(2)}, u32[]{:S(2)}) collective-permute-start(f32[39,8,128]{2,1,0:T(8,128)S(1)} %get-tuple-element.36.flow_ref), channel_id=1, source_target_pairs={{0,4},{4,0},{8,12},{12,8},{16,20},{20,16},{24,28},{28,24},{1,5},{5... | collective-permute-start | bytes 479240 | tf_op jit(solution)/shard_map/ppermute | solution.py:379
  26.2 5.2 %copy-start = (f32[4,6,32,128]{3,2,1,0:T(8,128)S(1)}, f32[4,6,32,128]{3,2,1,0:T(8,128)}, u32[]{:S(2)}) copy-start(f32[4,6,32,128]{3,2,1,0:T(8,128)} %own_hbm.1) | copy-start | bytes 1179652
  27.1 4.3 %collective-permute-start.1 = (f32[2,6,8,128]{3,2,1,0:T(8,128)}, f32[2,6,8,128]{3,2,1,0:T(8,128)}, u32[]{:S(2)}, u32[]{:S(2)}) collective-permute-start(f32[2,6,8,128]{3,2,1,0:T(8,128)} %pack_field_edges.1), channel_id=1, source_target_pairs={{1,2},{2,1},{3,0},{0,3},{5,6},{6,5},{7,4},{4,7},{9,10},{10,9},{11,... | collective-permute-start | bytes 147464 | tf_op jit(solution)/shard_map/cond/branch_1_fun/ppermute | solution.py:385
  28.0 3.5 %collective-permute-start = (f32[2,6,8,128]{3,2,1,0:T(8,128)}, f32[2,6,8,128]{3,2,1,0:T(8,128)}, u32[]{:S(2)}, u32[]{:S(2)}) collective-permute-start(f32[2,6,8,128]{3,2,1,0:T(8,128)} %pack_field_edges.1), channel_id=1, source_target_pairs={{0,1},{1,0},{2,3},{3,2},{4,5},{5,4},{6,7},{7,6},{8,9},{9,8},{10,11... | collective-permute-start | bytes 147464 | tf_op jit(solution)/shard_map/cond/branch_1_fun/ppermute | solution.py:385
